TPU v7x, 512 devices: a whole 4x8x8 slice. The times are simulated.
512 devices in a mesh: dp: 512 (over y, x, z, core).
Axes of the slice: x: 4, y: 8, z: 8, core: 2. Of those that a mesh axis runs over, the one named last changes fastest.
Arguments:
- image_feats: bfloat16 [131072, 1152], P('dp'), may hold values from -180 to 180
- text_embeds: bfloat16 [131072, 640], P('dp'), may hold values from -180 to 180
- head_weight: bfloat16 [1152, 640], replicated, may hold values from -0.1875 to 0.1875
- logit_scale: float32 [1], replicated, may hold values from 5 to 15
- logit_bias: float32 [1], replicated, may hold values from -6 to -2
Outputs:
- loss: float32 [], replicated
- image_grad: bfloat16 [131072, 1152], P('dp')
- text_grad: bfloat16 [131072, 640], P('dp')
- head_grad: bfloat16 [1152, 640], replicated
All inputs are finite; a program needn't handle non-finite values.
Results may differ from a plain program's by a relative error of at most 0.0064.
Values may be sent and summed in bfloat16 or wider, within the bound.
No kernel may reach another device: no remote copies, remote signals or barrier semaphores. Data moves between devices by JAX's collectives and lax.ppermute only.
A program may use at most 64 MiB of HBM per device.

v0:
```python
import jax
import jax.numpy as jnp
from jax import lax
from jax.sharding import PartitionSpec as P

TOK_DEV = 256
HOPS = 4


EPS = 1e-06


def passed_along(block, axis, distance):
    devices = range(lax.axis_size(axis))
    route = [((i - distance) % len(devices), i) for i in devices]
    return lax.ppermute(block, axis, route)


def pair_labels(logits, with_pairs):
    rows, cols = logits.shape
    if with_pairs:
        return jnp.where(jnp.eye(rows, cols, dtype=bool), 1.0, -1.0).astype(jnp.float32)
    return -jnp.ones(logits.shape, jnp.float32)


def score_block(image_b, text_b, scale, bias, with_pairs):
    prods = jnp.dot(image_b, text_b.T, preferred_element_type=jnp.float32)
    logits = scale * prods + bias
    label = pair_labels(logits, with_pairs)
    loss_part = jnp.sum(jax.nn.softplus(-label * logits))
    coef = (-label * jax.nn.sigmoid(-label * logits)).astype(jnp.bfloat16)
    image_part = scale * jnp.dot(coef, text_b, preferred_element_type=jnp.float32)
    text_part = scale * jnp.dot(coef.T, image_b, preferred_element_type=jnp.float32)
    return (loss_part, image_part, text_part)


def per_device(image_feats, text_embeds, head_weight, logit_scale, logit_bias):
    scale = logit_scale[0]
    bias = logit_bias[0]
    rows = image_feats.shape[0]
    u_local = jnp.dot(image_feats, head_weight, preferred_element_type=jnp.float32)
    inv_u = lax.rsqrt(jnp.sum(u_local * u_local, axis=1, keepdims=True) + EPS)
    zi = u_local * inv_u
    zi_b = zi.astype(jnp.bfloat16)
    text_f = text_embeds.astype(jnp.float32)
    inv_y = lax.rsqrt(jnp.sum(text_f * text_f, axis=1, keepdims=True) + EPS)
    zt = text_f * inv_y
    zt_b = zt.astype(jnp.bfloat16)
    current = passed_along(zt_b, "dp", -HOPS)
    loss_local, dzi, carried = score_block(zi_b, current, scale, bias, HOPS == 0)
    for step in range(2 * HOPS):
        current = passed_along(current, "dp", 1)
        carried = passed_along(carried, "dp", 1)
        loss_part, image_part, text_part = score_block(zi_b, current, scale, bias, step + 1 == HOPS)
        loss_local = loss_local + loss_part
        dzi = dzi + image_part
        carried = carried + text_part
    dzt = passed_along(carried, "dp", -HOPS)
    du = ((dzi - zi * jnp.sum(zi * dzi, axis=1, keepdims=True)) * inv_u).astype(jnp.bfloat16)
    image_grad = jnp.dot(du, head_weight.T, preferred_element_type=jnp.float32).astype(jnp.bfloat16)
    head_local = jnp.dot(image_feats.T, du, preferred_element_type=jnp.float32)
    head_total, loss_total = lax.psum((head_local, loss_local), "dp")
    head_grad = (head_total / TOK_DEV).astype(jnp.bfloat16)
    text_grad = ((dzt - zt * jnp.sum(zt * dzt, axis=1, keepdims=True)) * inv_y).astype(jnp.bfloat16)
    loss = loss_total / (rows * lax.axis_size("dp"))
    return (loss, image_grad, text_grad, head_grad)


def solution(mesh):
    placed = (P("dp", None), P("dp", None), P(), P(), P())
    return jax.shard_map(
        per_device,
        mesh=mesh,
        in_specs=placed,
        out_specs=(P(), P("dp", None), P("dp", None), P()),
        check_vma=False,
    )
```

profile of v0, /device:TPU:1, one launch (start us, length us, event | category | flops | bytes accessed | tf_op | source)
XLA Modules:
  0.0 485.4 jit_solution(18431520703374116565)
XLA Ops:
  7.2 1.2 fusion.19
  8.5 1.1 fusion.14
  9.6 16.6 %collective-permute-start = (bf16[256,640]{1,0:T(8,128)(2,1)S(1)}, bf16[256,640]{1,0:T(8,128)(2,1)S(1)}, u32[]{:S(2)}, u32[]{:S(2)}) collective-permute-start(bf16[256,640]{1,0:T(8,128)(2,1)S(1)} %fusion.14), channel_id=1, source_target_pairs={{4,0},{5,1},{6,2},{7,3},{8,4},{9,5},{10,6},{11,7},{12,8},{13,9},{1... | collective-permute-start | bytes 983048 | tf_op jit(solution)/shard_map/ppermute | solution.py:16
  26.2 1.8 multiply_reduce_fusion.1
  29.4 5.5 %collective-permute-done = bf16[256,640]{1,0:T(8,128)(2,1)S(1)} collective-permute-done((bf16[256,640]{1,0:T(8,128)(2,1)S(1)}, bf16[256,640]{1,0:T(8,128)(2,1)S(1)}, u32[]{:S(2)}, u32[]{:S(2)}) %collective-permute-start) | collective-permute-done | bytes 327712 | tf_op jit(solution)/shard_map/ppermute | solution.py:16
  34.9 6.4 %collective-permute-start.1 = (bf16[256,640]{1,0:T(8,128)(2,1)S(1)}, bf16[256,640]{1,0:T(8,128)(2,1)S(1)}, u32[]{:S(2)}, u32[]{:S(2)}) collective-permute-start(bf16[256,640]{1,0:T(8,128)(2,1)S(1)} %collective-permute-done), channel_id=1, source_target_pairs={{511,0},{0,1},{1,2},{2,3},{3,4},{4,5},{5,6},{6,7},{7,8},{8,9},{9,1... | collective-permute-start | bytes 983048 | tf_op jit(solution)/shard_map/ppermute | solution.py:16
  41.3 1.1 fusion.20
  42.4 0.3 convolution_multiply_fusion.8
  42.7 1.9 collective-permute-start.9
  45.0 0.3 collective-permute-done.1
  45.3 4.4 collective-permute-start.2
  49.7 1.0 fusion.21
  51.0 1.3 collective-permute-done.9
  52.3 0.3 fusion
  52.7 4.4 collective-permute-start.10
  57.1 3.1 collective-permute-start.3
  60.2 1.0 fusion.22
  61.2 0.3 convolution_multiply_fusion.6
  61.9 8.9 %collective-permute-done.3 = bf16[256,640]{1,0:T(8,128)(2,1)S(1)} collective-permute-done((bf16[256,640]{1,0:T(8,128)(2,1)S(1)}, bf16[256,640]{1,0:T(8,128)(2,1)S(1)}, u32[]{:S(2)}, u32[]{:S(2)}) %collective-permute-start.3) | collective-permute-done | bytes 327712 | tf_op jit(solution)/shard_map/ppermute | solution.py:16
  70.7 1.9 collective-permute-start.4
  72.7 1.0 fusion.23
  73.7 0.3 convolution_multiply_fusion.5
  74.4 1.9 collective-permute-start.11
  76.3 8.8 %collective-permute-done.4 = bf16[256,640]{1,0:T(8,128)(2,1)S(1)} collective-permute-done((bf16[256,640]{1,0:T(8,128)(2,1)S(1)}, bf16[256,640]{1,0:T(8,128)(2,1)S(1)}, u32[]{:S(2)}, u32[]{:S(2)}) %collective-permute-start.4) | collective-permute-done | bytes 327712 | tf_op jit(solution)/shard_map/ppermute | solution.py:16
  85.1 1.9 collective-permute-start.5
  87.1 1.1 fusion.24
  88.5 0.3 convolution_multiply_fusion.4
  88.8 10.1 %collective-permute-done.5 = bf16[256,640]{1,0:T(8,128)(2,1)S(1)} collective-permute-done((bf16[256,640]{1,0:T(8,128)(2,1)S(1)}, bf16[256,640]{1,0:T(8,128)(2,1)S(1)}, u32[]{:S(2)}, u32[]{:S(2)}) %collective-permute-start.5) | collective-permute-done | bytes 327712 | tf_op jit(solution)/shard_map/ppermute | solution.py:16
  98.9 1.9 collective-permute-start.6
  100.9 1.0 fusion.25
  102.3 1.9 collective-permute-start.12
  104.2 0.3 convolution_multiply_fusion.3
  104.5 8.2 %collective-permute-done.6 = bf16[256,640]{1,0:T(8,128)(2,1)S(1)} collective-permute-done((bf16[256,640]{1,0:T(8,128)(2,1)S(1)}, bf16[256,640]{1,0:T(8,128)(2,1)S(1)}, u32[]{:S(2)}, u32[]{:S(2)}) %collective-permute-start.6) | collective-permute-done | bytes 327712 | tf_op jit(solution)/shard_map/ppermute | solution.py:16
  112.8 1.9 collective-permute-start.7
  114.7 1.0 fusion.26
  116.0 0.6 collective-permute-done.12
  116.6 1.9 collective-permute-start.13
  118.6 0.3 convolution_multiply_fusion.2
  118.9 7.7 %collective-permute-done.7 = bf16[256,640]{1,0:T(8,128)(2,1)S(1)} collective-permute-done((bf16[256,640]{1,0:T(8,128)(2,1)S(1)}, bf16[256,640]{1,0:T(8,128)(2,1)S(1)}, u32[]{:S(2)}, u32[]{:S(2)}) %collective-permute-start.7) | collective-permute-done | bytes 327712 | tf_op jit(solution)/shard_map/ppermute | solution.py:16
  126.6 1.9 collective-permute-start.8
  128.5 1.0 fusion.27
  129.8 0.4 copy-done.4
  130.2 3.9 collective-permute-done.13
  134.2 1.9 collective-permute-start.14
  136.1 4.2 collective-permute-done.8
  140.4 1.0 fusion.28
  141.4 0.4 multiply_reduce_fusion
  142.3 9.3 %collective-permute-done.14 = f32[256,640]{1,0:T(8,128)S(1)} collective-permute-done((f32[256,640]{1,0:T(8,128)S(1)}, f32[256,640]{1,0:T(8,128)S(1)}, u32[]{:S(2)}, u32[]{:S(2)}) %collective-permute-start.14) | collective-permute-done | bytes 655392 | tf_op jit(solution)/shard_map/ppermute | solution.py:16
  151.6 1.9 collective-permute-start.15
  153.6 2.3 convolution_bitcast_fusion
  155.9 1.3 convolution_multiply_fusion.1
  157.1 11.8 %collective-permute-done.15 = f32[256,640]{1,0:T(8,128)S(1)} collective-permute-done((f32[256,640]{1,0:T(8,128)S(1)}, f32[256,640]{1,0:T(8,128)S(1)}, u32[]{:S(2)}, u32[]{:S(2)}) %collective-permute-start.15) | collective-permute-done | bytes 655392 | tf_op jit(solution)/shard_map/ppermute | solution.py:16
  169.0 2.1 collective-permute-start.16
  176.7 1.3 convolution_multiply_fusion
  178.0 8.5 %collective-permute-done.16 = f32[256,640]{1,0:T(8,128)S(1)} collective-permute-done((f32[256,640]{1,0:T(8,128)S(1)}, f32[256,640]{1,0:T(8,128)S(1)}, u32[]{:S(2)}, u32[]{:S(2)}) %collective-permute-start.16) | collective-permute-done | bytes 655392 | tf_op jit(solution)/shard_map/ppermute | solution.py:16
  186.5 0.9 add.238
  187.4 1.9 collective-permute-start.17
  189.3 1.5 convolution_convert_fusion
  190.8 119.3 %psum.14 = f32[]{:T(128)} all-reduce(f32[]{:T(128)S(6)} %add.213), channel_id=1, replica_groups=mesh['dp'=512] {'dp'}, use_global_device_ids=true, to_apply=%region_11.12 | all-reduce | flops 1 | bytes 8 | tf_op jit(solution)/shard_map/psum | solution.py:62
  310.7 159.2 %all-reduce.2.cloned.1.call-done = f32[1152,640]{0,1:T(8,128)} async-done(((f32[1152,640]{0,1:T(8,128)}), f32[1152,640]{0,1:T(8,128)}) %all-reduce.2.cloned.1.call-update) | async-done | bytes 2949136 | tf_op jit(solution)/shard_map/psum | solution.py:62
  469.9 2.0 multiply_convert_fusion
  472.0 2.1 copy.9
  474.1 1.3 fusion.15
  475.4 2.0 fusion.18
  (33 shorter events, 3.4 us)
Async XLA Ops:
  7.2 19.0 %copy-start = (bf16[1152,640]{1,0:T(8,128)(2,1)S(1)}, bf16[1152,640]{1,0:T(8,128)(2,1)}, u32[]{:S(2)}) copy-start(bf16[1152,640]{1,0:T(8,128)(2,1)} %param.7) | copy-start | bytes 4423684
  7.2 462.7 %all-reduce.2.cloned.1.call-start = ((), (), s32[]{:S(2)}) async-start(), calls=%async_computation | async-start | bytes 5898240 | tf_op jit(solution)/shard_map/psum | solution.py:62
  9.6 25.3 %collective-permute-start = (bf16[256,640]{1,0:T(8,128)(2,1)S(1)}, bf16[256,640]{1,0:T(8,128)(2,1)S(1)}, u32[]{:S(2)}, u32[]{:S(2)}) collective-permute-start(bf16[256,640]{1,0:T(8,128)(2,1)S(1)} %fusion.14), channel_id=1, source_target_pairs={{4,0},{5,1},{6,2},{7,3},{8,4},{9,5},{10,6},{11,7},{12,8},{13,9},{1... | collective-permute-start | bytes 983048 | tf_op jit(solution)/shard_map/ppermute | solution.py:16
  34.9 10.4 %collective-permute-start.1 = (bf16[256,640]{1,0:T(8,128)(2,1)S(1)}, bf16[256,640]{1,0:T(8,128)(2,1)S(1)}, u32[]{:S(2)}, u32[]{:S(2)}) collective-permute-start(bf16[256,640]{1,0:T(8,128)(2,1)S(1)} %collective-permute-done), channel_id=1, source_target_pairs={{511,0},{0,1},{1,2},{2,3},{3,4},{4,5},{5,6},{6,7},{7,8},{8,9},{9,1... | collective-permute-start | bytes 983048 | tf_op jit(solution)/shard_map/ppermute | solution.py:16
  42.7 9.6 %collective-permute-start.9 = (f32[256,640]{1,0:T(8,128)S(1)}, f32[256,640]{1,0:T(8,128)S(1)}, u32[]{:S(2)}, u32[]{:S(2)}) collective-permute-start(f32[256,640]{1,0:T(8,128)S(1)} %convolution_multiply_fusion.8), channel_id=1, source_target_pairs={{511,0},{0,1},{1,2},{2,3},{3,4},{4,5},{5,6},{6,7},{7,8},{8,9},{9,1... | collective-permute-start | bytes 1966088 | tf_op jit(solution)/shard_map/ppermute | solution.py:16
  45.3 11.8 %collective-permute-start.2 = (bf16[256,640]{1,0:T(8,128)(2,1)S(1)}, bf16[256,640]{1,0:T(8,128)(2,1)S(1)}, u32[]{:S(2)}, u32[]{:S(2)}) collective-permute-start(bf16[256,640]{1,0:T(8,128)(2,1)S(1)} %collective-permute-done.1), channel_id=1, source_target_pairs={{511,0},{0,1},{1,2},{2,3},{3,4},{4,5},{5,6},{6,7},{7,8},{8,9},{9,1... | collective-permute-start | bytes 983048 | tf_op jit(solution)/shard_map/ppermute | solution.py:16
  52.7 21.7 %collective-permute-start.10 = (f32[256,640]{1,0:T(8,128)S(1)}, f32[256,640]{1,0:T(8,128)S(1)}, u32[]{:S(2)}, u32[]{:S(2)}) collective-permute-start(f32[256,640]{1,0:T(8,128)S(1)} %fusion), channel_id=1, source_target_pairs={{511,0},{0,1},{1,2},{2,3},{3,4},{4,5},{5,6},{6,7},{7,8},{8,9},{9,1... | collective-permute-start | bytes 1966088 | tf_op jit(solution)/shard_map/ppermute | solution.py:16
  57.1 13.7 %collective-permute-start.3 = (bf16[256,640]{1,0:T(8,128)(2,1)S(1)}, bf16[256,640]{1,0:T(8,128)(2,1)S(1)}, u32[]{:S(2)}, u32[]{:S(2)}) collective-permute-start(bf16[256,640]{1,0:T(8,128)(2,1)S(1)} %collective-permute-done.2), channel_id=1, source_target_pairs={{511,0},{0,1},{1,2},{2,3},{3,4},{4,5},{5,6},{6,7},{7,8},{8,9},{9,1... | collective-permute-start | bytes 983048 | tf_op jit(solution)/shard_map/ppermute | solution.py:16
  70.7 14.4 %collective-permute-start.4 = (bf16[256,640]{1,0:T(8,128)(2,1)S(1)}, bf16[256,640]{1,0:T(8,128)(2,1)S(1)}, u32[]{:S(2)}, u32[]{:S(2)}) collective-permute-start(bf16[256,640]{1,0:T(8,128)(2,1)S(1)} %collective-permute-done.3), channel_id=1, source_target_pairs={{511,0},{0,1},{1,2},{2,3},{3,4},{4,5},{5,6},{6,7},{7,8},{8,9},{9,1... | collective-permute-start | bytes 983048 | tf_op jit(solution)/shard_map/ppermute | solution.py:16
  74.4 27.8 %collective-permute-start.11 = (f32[256,640]{1,0:T(8,128)S(1)}, f32[256,640]{1,0:T(8,128)S(1)}, u32[]{:S(2)}, u32[]{:S(2)}) collective-permute-start(f32[256,640]{1,0:T(8,128)S(1)} %add.232), channel_id=1, source_target_pairs={{511,0},{0,1},{1,2},{2,3},{3,4},{4,5},{5,6},{6,7},{7,8},{8,9},{9,1... | collective-permute-start | bytes 1966088 | tf_op jit(solution)/shard_map/ppermute | solution.py:16
  85.1 13.8 %collective-permute-start.5 = (bf16[256,640]{1,0:T(8,128)(2,1)S(1)}, bf16[256,640]{1,0:T(8,128)(2,1)S(1)}, u32[]{:S(2)}, u32[]{:S(2)}) collective-permute-start(bf16[256,640]{1,0:T(8,128)(2,1)S(1)} %collective-permute-done.4), channel_id=1, source_target_pairs={{511,0},{0,1},{1,2},{2,3},{3,4},{4,5},{5,6},{6,7},{7,8},{8,9},{9,1... | collective-permute-start | bytes 983048 | tf_op jit(solution)/shard_map/ppermute | solution.py:16
  98.9 13.8 %collective-permute-start.6 = (bf16[256,640]{1,0:T(8,128)(2,1)S(1)}, bf16[256,640]{1,0:T(8,128)(2,1)S(1)}, u32[]{:S(2)}, u32[]{:S(2)}) collective-permute-start(bf16[256,640]{1,0:T(8,128)(2,1)S(1)} %collective-permute-done.5), channel_id=1, source_target_pairs={{511,0},{0,1},{1,2},{2,3},{3,4},{4,5},{5,6},{6,7},{7,8},{8,9},{9,1... | collective-permute-start | bytes 983048 | tf_op jit(solution)/shard_map/ppermute | solution.py:16
  102.3 14.3 %collective-permute-start.12 = (f32[256,640]{1,0:T(8,128)S(1)}, f32[256,640]{1,0:T(8,128)S(1)}, u32[]{:S(2)}, u32[]{:S(2)}) collective-permute-start(f32[256,640]{1,0:T(8,128)S(1)} %add.233), channel_id=1, source_target_pairs={{511,0},{0,1},{1,2},{2,3},{3,4},{4,5},{5,6},{6,7},{7,8},{8,9},{9,1... | collective-permute-start | bytes 1966088 | tf_op jit(solution)/shard_map/ppermute | solution.py:16
  112.8 13.8 %collective-permute-start.7 = (bf16[256,640]{1,0:T(8,128)(2,1)S(1)}, bf16[256,640]{1,0:T(8,128)(2,1)S(1)}, u32[]{:S(2)}, u32[]{:S(2)}) collective-permute-start(bf16[256,640]{1,0:T(8,128)(2,1)S(1)} %collective-permute-done.6), channel_id=1, source_target_pairs={{511,0},{0,1},{1,2},{2,3},{3,4},{4,5},{5,6},{6,7},{7,8},{8,9},{9,1... | collective-permute-start | bytes 983048 | tf_op jit(solution)/shard_map/ppermute | solution.py:16
  116.6 17.5 %collective-permute-start.13 = (f32[256,640]{1,0:T(8,128)S(1)}, f32[256,640]{1,0:T(8,128)S(1)}, u32[]{:S(2)}, u32[]{:S(2)}) collective-permute-start(f32[256,640]{1,0:T(8,128)S(1)} %add.234), channel_id=1, source_target_pairs={{511,0},{0,1},{1,2},{2,3},{3,4},{4,5},{5,6},{6,7},{7,8},{8,9},{9,1... | collective-permute-start | bytes 1966088 | tf_op jit(solution)/shard_map/ppermute | solution.py:16
  126.6 13.8 %collective-permute-start.8 = (bf16[256,640]{1,0:T(8,128)(2,1)S(1)}, bf16[256,640]{1,0:T(8,128)(2,1)S(1)}, u32[]{:S(2)}, u32[]{:S(2)}) collective-permute-start(bf16[256,640]{1,0:T(8,128)(2,1)S(1)} %collective-permute-done.7), channel_id=1, source_target_pairs={{511,0},{0,1},{1,2},{2,3},{3,4},{4,5},{5,6},{6,7},{7,8},{8,9},{9,1... | collective-permute-start | bytes 983048 | tf_op jit(solution)/shard_map/ppermute | solution.py:16
  129.5 0.7 copy-start.4
  134.2 17.3 %collective-permute-start.14 = (f32[256,640]{1,0:T(8,128)S(1)}, f32[256,640]{1,0:T(8,128)S(1)}, u32[]{:S(2)}, u32[]{:S(2)}) collective-permute-start(f32[256,640]{1,0:T(8,128)S(1)} %add.235), channel_id=1, source_target_pairs={{511,0},{0,1},{1,2},{2,3},{3,4},{4,5},{5,6},{6,7},{7,8},{8,9},{9,1... | collective-permute-start | bytes 1966088 | tf_op jit(solution)/shard_map/ppermute | solution.py:16
  141.4 0.7 copy-start.3
  142.1 11.4 %copy-start.2 = (bf16[256,1152]{1,0:T(8,128)(2,1)S(1)}, bf16[256,1152]{1,0:T(8,128)(2,1)}, u32[]{:S(2)}) copy-start(bf16[256,1152]{1,0:T(8,128)(2,1)} %param.5) | copy-start | bytes 1769476
  151.6 17.3 %collective-permute-start.15 = (f32[256,640]{1,0:T(8,128)S(1)}, f32[256,640]{1,0:T(8,128)S(1)}, u32[]{:S(2)}, u32[]{:S(2)}) collective-permute-start(f32[256,640]{1,0:T(8,128)S(1)} %add.236), channel_id=1, source_target_pairs={{511,0},{0,1},{1,2},{2,3},{3,4},{4,5},{5,6},{6,7},{7,8},{8,9},{9,1... | collective-permute-start | bytes 1966088 | tf_op jit(solution)/shard_map/ppermute | solution.py:16
  169.0 17.5 %collective-permute-start.16 = (f32[256,640]{1,0:T(8,128)S(1)}, f32[256,640]{1,0:T(8,128)S(1)}, u32[]{:S(2)}, u32[]{:S(2)}) collective-permute-start(f32[256,640]{1,0:T(8,128)S(1)} %add.237), channel_id=1, source_target_pairs={{511,0},{0,1},{1,2},{2,3},{3,4},{4,5},{5,6},{6,7},{7,8},{8,9},{9,1... | collective-permute-start | bytes 1966088 | tf_op jit(solution)/shard_map/ppermute | solution.py:16
  187.4 286.7 %collective-permute-start.17 = (f32[256,640]{1,0:T(8,128)}, f32[256,640]{1,0:T(8,128)}, u32[]{:S(2)}, u32[]{:S(2)}) collective-permute-start(f32[256,640]{1,0:T(8,128)} %add.238), channel_id=1, source_target_pairs={{4,0},{5,1},{6,2},{7,3},{8,4},{9,5},{10,6},{11,7},{12,8},{13,9},{1... | collective-permute-start | bytes 1966088 | tf_op jit(solution)/shard_map/ppermute | solution.py:16
  472.0 2.1 copy-start.1
Sparse Core Ops, SparseCore 0:
  156.0 313.9 all-reduce.1
where the time goes:
time: 487 us; the launch traced here: 485 us
  waiting for transfers between devices  248 us (51%)
  blocking collectives  119 us (24%)
  starting transfers between devices  60 us (12%)
  between operations  23.1 us (5%)
  matrix products  22.6 us (5%)
  other arithmetic  9.27 us (2%)
    psum x1, waiting for transfers between devices, per_device(): head_total, loss_total = lax.psum((head_local, loss_local), 'dp')  159 us
    psum x1, blocking collectives, per_device(): head_total, loss_total = lax.psum((head_local, loss_local), 'dp')  119 us
    ppermute x18, waiting for transfers between devices, passed_along(): return lax.ppermute(block, axis, route)  89.1 us
    ppermute x18, starting transfers between devices, passed_along(): return lax.ppermute(block, axis, route)  60 us
  transfers between devices with their start and end apart: 19, of which 15 were waited for; matrix products, arithmetic and copies ran while one was open for 6% of the time, Pallas kernels for 0%

commit v1 on v0

v1 whole, which is shorter than its diff:
```python
import functools

import jax
import jax.numpy as jnp
from jax import lax
from jax.experimental import pallas as pl
from jax.experimental.pallas import tpu as pltpu
from jax.sharding import Mesh, PartitionSpec as P

D = 1152
E = 640
ROWS = 256
HALF = D // 2
LANES = 128
EPS = 1e-06
CHUNK = 64

BF = jnp.bfloat16
F32 = jnp.float32
VMEM = pl.BlockSpec(memory_space=pltpu.VMEM)
SMEM = pl.BlockSpec(memory_space=pltpu.SMEM)
PARAMS = pltpu.CompilerParams(vmem_limit_bytes=32 * 1024 * 1024)


def call(body, out_shape, n_smem, n_vmem, out_specs, scratch=(), flops=0, bytes_accessed=0):
    return pl.pallas_call(
        body,
        out_shape=out_shape,
        in_specs=[SMEM] * n_smem + [VMEM] * n_vmem,
        out_specs=out_specs,
        scratch_shapes=list(scratch),
        compiler_params=PARAMS,
        cost_estimate=pl.CostEstimate(flops=flops, bytes_accessed=bytes_accessed, transcendentals=0),
    )


def project_kernel(core_ref, own_ref, other_ref, weight_ref, zi_ref, zib_ref, inv_ref, xt_ref, all_ref):
    for part, ref in enumerate((own_ref, other_ref)):
        rows = pl.ds(part * ROWS, ROWS)
        all_ref[:, part * ROWS : (part + 1) * ROWS] = ref[...].T
        u = jnp.dot(ref[...], weight_ref[...], preferred_element_type=F32)
        inv = lax.rsqrt(jnp.sum(u * u, axis=1, keepdims=True) + EPS)
        zi = u * inv
        zi_ref[rows, :] = zi
        zib_ref[rows, :] = zi.astype(BF)
        inv_ref[rows, :] = jnp.broadcast_to(inv, (ROWS, LANES))
    xt_ref[...] = all_ref[pl.ds(pl.multiple_of(core_ref[0] * HALF, HALF), HALF), :]


def score_kernel(parts, has_dzi, scal_ref, zib_ref, text_ref, *refs):
    dzi_in = None
    if has_dzi:
        dzi_in, *refs = refs
    dzi_ref, dzt_ref, loss_ref, s_ref, c_ref = refs
    scale = scal_ref[0]
    bias = scal_ref[1]
    loss = jnp.zeros((8, ROWS), F32)
    for order, (q, n, diag) in enumerate(parts):
        cols = pl.ds(q * ROWS, ROWS)
        text = text_ref[cols, :].astype(F32)
        inv = lax.rsqrt(jnp.sum(text * text, axis=1, keepdims=True) + EPS)
        ztb = (text * inv).astype(BF)
        zib = zib_ref[0:n, :]
        s_ref[0:n, :] = lax.dot_general(zib, ztb, (((1,), (1,)), ((), ())), preferred_element_type=F32)
        for start in range(0, n, CHUNK):
            v = scale * s_ref[start : start + CHUNK, :] + bias
            paired = diag and start < ROWS
            if paired:
                row = lax.broadcasted_iota(jnp.int32, (CHUNK, ROWS), 0) + start
                col = lax.broadcasted_iota(jnp.int32, (CHUNK, ROWS), 1)
                own = row == col
                v = jnp.where(own, -v, v)
            e = jnp.exp(v)
            w = 1.0 + e
            r = 1.0 / w
            c = e * r
            if paired:
                c = jnp.where(own, -c, c)
            c_ref[start : start + CHUNK, :] = c.astype(BF)
            lost = (e - (w - 1.0)) * r
            loss = loss + jnp.sum(lost.reshape(CHUNK // 8, 8, ROWS), axis=0)
            k = CHUNK // 4
            prod = (w[0:k] * w[k : 2 * k]) * (w[2 * k : 3 * k] * w[3 * k :])
            loss = loss + jnp.sum(jnp.log(prod).reshape(k // 8, 8, ROWS), axis=0)
        coef = c_ref[0:n, :]
        dzi = scale * jnp.dot(coef, ztb, preferred_element_type=F32)
        if order:
            dzi_ref[0:n, :] += dzi
        elif has_dzi:
            dzi_ref[...] = dzi_in[...] + dzi
        else:
            dzi_ref[...] = dzi
        dzt = scale * lax.dot_general(coef, zib, (((0,), (0,)), ((), ())), preferred_element_type=F32)
        dzt_ref[cols, :] = dzt.astype(dzt_ref.dtype)
    loss_ref[...] = loss


def score(parts, scal, zib, text, dzi, dzt_dtype):
    n = len(parts) * ROWS
    args = (scal, zib, text) + (() if dzi is None else (dzi,))
    return call(
        functools.partial(score_kernel, parts, dzi is not None),
        (
            jax.ShapeDtypeStruct((2 * ROWS, E), F32),
            jax.ShapeDtypeStruct((n, E), dzt_dtype),
            jax.ShapeDtypeStruct((8, ROWS), F32),
        ),
        1,
        len(args) - 1,
        (VMEM, VMEM, VMEM),
        scratch=(pltpu.VMEM((2 * ROWS, ROWS), F32), pltpu.VMEM((2 * ROWS, ROWS), BF)),
        flops=sum(6 * n * ROWS * E for _, n, _ in parts),
        bytes_accessed=4 << 20,
    )(*args)


def head_kernel(dzi_ref, sent_ref, zi_ref, inv_ref, xt_ref, la_ref, lb_ref, lc_ref, du_ref, flat_ref, all_ref):
    for part in range(2):
        rows = pl.ds(part * ROWS, ROWS)
        swapped = pl.ds((1 - part) * ROWS, ROWS)
        dzi = dzi_ref[rows, :] + sent_ref[swapped, :]
        zi = zi_ref[rows, :]
        along = jnp.sum(zi * dzi, axis=1, keepdims=True)
        du = ((dzi - zi * along) * inv_ref[rows, 0:1]).astype(BF)
        all_ref[rows, :] = du
        if part == 0:
            du_ref[...] = du
    for slab in range(E // LANES):
        part = jnp.dot(xt_ref[...], all_ref[:, slab * LANES : (slab + 1) * LANES], preferred_element_type=F32)
        flat_ref[slab * HALF : (slab + 1) * HALF, :] = part.astype(BF)
    loss = jnp.sum(la_ref[...] + lb_ref[...] + lc_ref[...])
    total = jnp.full((16, LANES), loss, F32)
    high = total.astype(BF).astype(F32)
    low = (total - high).astype(BF).astype(F32)
    row = lax.broadcasted_iota(jnp.int32, (16, LANES), 0)
    lane = lax.broadcasted_iota(jnp.int32, (16, LANES), 1)
    both = jnp.where(lane == 0, high, jnp.where(lane == 1, low, 0.0))
    base = (E // LANES) * HALF
    flat_ref[base : base + 16, :] = jnp.where(row == 0, both, 0.0).astype(BF)
    flat_ref[base + 16 :, :] = jnp.zeros((flat_ref.shape[0] - base - 16, LANES), BF)


def reduce_kernel(share, chip_ref, pieces_ref, out_ref, sum_ref):
    group = 4 * share
    groups = pieces_ref.shape[0] // group
    total = jnp.zeros((group, LANES), F32)
    for g in range(groups):
        total = total + pieces_ref[g * group : (g + 1) * group, :].astype(F32)
    sum_ref[...] = total
    total = sum_ref[0:share, :] + sum_ref[share : 2 * share, :]
    total = total + (sum_ref[2 * share : 3 * share, :] + sum_ref[3 * share :, :])
    total = total * (1.0 / ROWS)
    loss_row = (E // LANES) * HALF
    row = lax.broadcasted_iota(jnp.int32, (share, LANES), 0)
    lane = lax.broadcasted_iota(jnp.int32, (share, LANES), 1)
    is_loss = (row == loss_row % share) & (chip_ref[0] == loss_row // share)
    loss = jnp.sum(jnp.where(row == loss_row % share, total, 0.0), axis=(0, 1), keepdims=True)
    loss = jnp.broadcast_to(loss, (share, LANES))
    high = loss.astype(BF).astype(F32)
    terms = jnp.where(lane == 0, high, jnp.where(lane == 1, loss - high, 0.0))
    total = jnp.where(is_loss, terms, total)
    for k in range(4):
        sum_ref[k * share : (k + 1) * share, :] = total
    tile = sum_ref[...].astype(BF)
    for g in range(groups):
        out_ref[g * group : (g + 1) * group, :] = tile


def assemble_kernel(core_ref, own_ref, other_ref, head_ref, loss_ref):
    core = core_ref[0]
    for slab in range(E // LANES):
        for ref, half in ((own_ref, core), (other_ref, 1 - core)):
            rows = pl.ds(pl.multiple_of(half * HALF, HALF), HALF)
            head_ref[rows, slab * LANES : (slab + 1) * LANES] = ref[slab * HALF : (slab + 1) * HALF, :]
    base = (E // LANES) * HALF
    terms = own_ref[base : base + 16, :].astype(F32) + other_ref[base : base + 16, :].astype(F32)
    loss_ref[0, 0] = jnp.sum(terms)


def text_kernel(own_ref, far_ref, near_ref, text_ref, out_ref):
    dzt = own_ref[...] + far_ref[0:ROWS, :].astype(F32) + near_ref[...].astype(F32)
    text = text_ref[...].astype(F32)
    inv = lax.rsqrt(jnp.sum(text * text, axis=1, keepdims=True) + EPS)
    zt = text * inv
    along = jnp.sum(zt * dzt, axis=1, keepdims=True)
    out_ref[...] = ((dzt - zt * along) * inv).astype(BF)


def per_device(chips, image_feats, text_embeds, head_weight, logit_scale, logit_bias):
    axes = ("chip", "core")
    core = lax.axis_index("core")
    core_id = core.astype(jnp.int32).reshape(1)
    chip_id = lax.axis_index("chip").astype(jnp.int32).reshape(1)
    across = [(i, i ^ 1) for i in range(2 * chips)]
    onward = [(2 * k + b, 2 * ((k + 1 - 2 * b) % chips) + b) for k in range(chips) for b in range(2)]
    back = [(d, s) for s, d in onward]
    scal = jnp.concatenate([logit_scale, logit_bias])

    text_other = lax.ppermute(text_embeds, axes, across)
    x_other = lax.ppermute(image_feats, axes, across)
    texts0 = jnp.concatenate([text_embeds, text_other])
    texts1 = lax.ppermute(texts0, axes, onward)
    texts2 = lax.ppermute(texts1, axes, onward)

    zi, zib, inv_u, x_half = call(
        project_kernel,
        (
            jax.ShapeDtypeStruct((2 * ROWS, E), F32),
            jax.ShapeDtypeStruct((2 * ROWS, E), BF),
            jax.ShapeDtypeStruct((2 * ROWS, LANES), F32),
            jax.ShapeDtypeStruct((HALF, 2 * ROWS), BF),
        ),
        1,
        3,
        (VMEM, VMEM, VMEM, VMEM),
        scratch=(pltpu.VMEM((D, 2 * ROWS), BF),),
        flops=2 * 2 * ROWS * D * E,
        bytes_accessed=5 << 20,
    )(core_id, image_feats, x_other, head_weight)

    both = 2 * ROWS
    dzi, dzt0, loss0 = score([(0, both, True)], scal, zib, text_embeds, None, F32)
    dzi, dzt1, loss1 = score([(0, both, False), (1, both, False)], scal, zib, texts1, dzi, F32)
    dzi, dzt2, loss2 = score([(1, both, False), (0, ROWS, False)], scal, zib, texts2, dzi, BF)
    dzi_sent = lax.ppermute(dzi, axes, across)
    far = lax.ppermute(dzt2, axes, back)

    flat_rows = 3072
    du, flat = call(
        head_kernel,
        (
            jax.ShapeDtypeStruct((ROWS, E), BF),
            jax.ShapeDtypeStruct((flat_rows, LANES), BF),
        ),
        0,
        8,
        (VMEM, VMEM),
        scratch=(pltpu.VMEM((2 * ROWS, E), BF),),
        flops=2 * 2 * ROWS * HALF * E,
        bytes_accessed=7 << 20,
    )(dzi, dzi_sent, zi, inv_u, x_half, loss0, loss1, loss2)

    dzt1, _ = lax.optimization_barrier((dzt1, flat))
    near = (far.astype(F32) + dzt1).astype(BF)
    near = lax.ppermute(near, axes, back)

    share = flat_rows // chips
    pieces = lax.all_to_all(flat.reshape(chips, share // 2, 2, LANES), "chip", 0, 0)
    spread = call(
        functools.partial(reduce_kernel, share),
        jax.ShapeDtypeStruct((flat_rows, LANES), BF),
        1,
        1,
        VMEM,
        scratch=(pltpu.VMEM((4 * share, LANES), F32),),
        flops=flat_rows * LANES,
        bytes_accessed=2 << 20,
    )(chip_id, pieces.reshape(flat_rows, LANES)).reshape(chips, share // 2, 2, LANES)
    half = lax.all_to_all(spread, "chip", 0, 0).reshape(flat_rows, LANES)
    half_other = lax.ppermute(half, axes, across)

    near_other = lax.ppermute(near[ROWS:], axes, across)
    image_grad = lax.dot_general(du, head_weight, (((1,), (1,)), ((), ())), preferred_element_type=F32).astype(BF)
    text_grad = call(
        text_kernel, jax.ShapeDtypeStruct((ROWS, E), BF), 0, 4, VMEM, flops=10 * ROWS * E, bytes_accessed=3 << 20
    )(dzt0, near, near_other, text_embeds)

    head_grad, loss = call(
        assemble_kernel,
        (jax.ShapeDtypeStruct((D, E), BF), jax.ShapeDtypeStruct((1, 1), F32)),
        1,
        2,
        (VMEM, SMEM),
        flops=1,
        bytes_accessed=3 << 20,
    )(core_id, half, half_other)
    loss = loss[0, 0] / (2 * chips)
    return (loss, image_grad, text_grad, head_grad)


def solution(mesh):
    chips = mesh.devices.size // 2
    by_chip = Mesh(mesh.devices.reshape(chips, 2), ("chip", "core"))
    rows = P(("chip", "core"), None)
    return jax.shard_map(
        functools.partial(per_device, chips),
        mesh=by_chip,
        in_specs=(rows, rows, P(), P(), P()),
        out_specs=(P(), rows, rows, P()),
        check_vma=False,
    )
```

time: 487 us -> 165 us (0.34)
  waiting for transfers between devices: 248 us -> 74.4 us
  blocking collectives: 119 us -> 0 us
  matrix products: 22.6 us -> 2.46 us
  between operations: 23.1 us -> 3.83 us
  Pallas kernels: 0 us -> 14.8 us
  other arithmetic: 9.27 us -> 3.41 us
    psum x1 -> x0, waiting for transfers between devices: 159 us -> none  [per_device(): head_total, loss_total = lax.psum((head_local, loss_local), 'dp')]
    psum x1 -> x0, blocking collectives: 119 us -> none  [per_device(): head_total, loss_total = lax.psum((head_local, loss_local), 'dp')]
    ppermute x18 -> x9, waiting for transfers between devices: 89.1 us -> 49.4 us  [the longest x1 28.1 us: per_device(): far = lax.ppermute(dzt2, axes, back)]
    all_to_all x0 -> x2, waiting for transfers between devices: none -> 24.9 us  [the longest x1 24.9 us: per_device(): lax.all_to_all(flat.reshape(chips, share // 2, 2, LANES), 'chip', 0, 0)]
    dot_general x30 -> x1, matrix products: 22.6 us -> 2.46 us  [per_device(): lax.dot_general(du, head_weight, (((1,), (1,)), ((), ())), preferred_elem...]
    all_to_all x0 -> x2, starting transfers between devices: none -> 19.1 us  [the longest x1 9.93 us: per_device(): lax.all_to_all(flat.reshape(chips, share // 2, 2, LANES), 'chip', 0, 0)]
    ppermute x18 -> x9, starting transfers between devices: 60 us -> 42 us  [the longest x1 10.4 us: per_device(): texts1 = lax.ppermute(texts0, axes, onward)]
    pallas_call x0 -> x8, Pallas kernels: none -> 14.8 us  [the longest x3 7.61 us: score(): call(functools.partial(score_kernel, parts, dzi is not None), (jax.ShapeD...]
  transfers between devices with their start and end apart: 19 -> 11, of which waited for: 15 -> 6; matrix products, arithmetic and copies ran while one was open for 6% -> 3% of each run, Pallas kernels for 0% -> 5%
where the time goes in v1:
time: 165 us; the launch traced here: 164 us
  waiting for transfers between devices  74.4 us (45%)
  starting transfers between devices  61.2 us (37%)
  Pallas kernels  14.8 us (9%)
  local copies, waits for them, and re-layouts  4.06 us (2%)
  between operations  3.83 us (2%)
  other arithmetic  3.41 us (2%)
  matrix products  2.46 us (1%)
    ppermute x1, waiting for transfers between devices, per_device(): far = lax.ppermute(dzt2, axes, back)  28.1 us
    all_to_all x1, waiting for transfers between devices, per_device(): lax.all_to_all(flat.reshape(chips, share // 2, 2, LANES), 'chip', 0, 0)  24.9 us
    ppermute x1, waiting for transfers between devices, per_device(): near = lax.ppermute(near, axes, back)  11.3 us
    ppermute x1, starting transfers between devices, per_device(): texts1 = lax.ppermute(texts0, axes, onward)  10.4 us
    all_to_all x1, starting transfers between devices, per_device(): lax.all_to_all(flat.reshape(chips, share // 2, 2, LANES), 'chip', 0, 0)  9.93 us
    ppermute x1, starting transfers between devices, per_device(): texts2 = lax.ppermute(texts1, axes, onward)  9.23 us
    all_to_all x1, starting transfers between devices, per_device(): half = lax.all_to_all(spread, 'chip', 0, 0).reshape(flat_rows, LANES)  9.21 us
    ppermute x1, starting transfers between devices, per_device(): text_other = lax.ppermute(text_embeds, axes, across)  8.92 us
  transfers between devices with their start and end apart: 11, of which 6 were waited for; matrix products, arithmetic and copies ran while one was open for 3% of the time, Pallas kernels for 5%

profile of v1, /device:TPU:1, one launch (start us, length us, event | category | flops | bytes accessed | tf_op | source)
XLA Modules:
  0.0 164.1 jit_solution(13166441589326120298)
XLA Ops:
  0.6 0.0 copy-start.7
  0.6 8.9 %collective-permute-start.1 = (bf16[256,640]{1,0:T(8,128)(2,1)}, bf16[256,640]{1,0:T(8,128)(2,1)S(1)}, u32[]{:S(2)}, u32[]{:S(2)}) collective-permute-start(bf16[256,640]{1,0:T(8,128)(2,1)} %text_ref.3), channel_id=1, source_target_pairs={{0,1},{1,0},{2,3},{3,2},{4,5},{5,4},{6,7},{7,6},{8,9},{9,8},{10,11... | collective-permute-start | bytes 983048 | tf_op jit(solution)/shard_map/ppermute | solution.py:199
  9.6 1.4 collective-permute-done.1
  11.0 1.0 pad_maximum_fusion
  12.0 10.4 %collective-permute-start.2 = (bf16[512,640]{1,0:T(8,128)(2,1)S(1)}, bf16[512,640]{1,0:T(8,128)(2,1)S(1)}, u32[]{:S(2)}, u32[]{:S(2)}) collective-permute-start(bf16[512,640]{1,0:T(8,128)(2,1)S(1)} %pad_maximum_fusion), channel_id=1, source_target_pairs={{0,2},{1,511},{2,4},{3,1},{4,6},{5,3},{6,8},{7,5},{8,10},{9,7},{10... | collective-permute-start | bytes 1966088 | tf_op jit(solution)/shard_map/ppermute | solution.py:202
  22.4 0.0 copy-done.7
  22.5 1.9 %collective-permute-start = (bf16[256,1152]{1,0:T(8,128)(2,1)S(1)}, bf16[256,1152]{1,0:T(8,128)(2,1)S(1)}, u32[]{:S(2)}, u32[]{:S(2)}) collective-permute-start(bf16[256,1152]{1,0:T(8,128)(2,1)S(1)} %copy-done.7), channel_id=1, source_target_pairs={{0,1},{1,0},{2,3},{3,2},{4,5},{5,4},{6,7},{7,6},{8,9},{9,8},{10,11... | collective-permute-start | bytes 1769480 | tf_op jit(solution)/shard_map/ppermute | solution.py:200
  24.4 5.6 %collective-permute-done.2.text_ref = bf16[512,640]{1,0:T(8,128)(2,1)S(1)} collective-permute-done((bf16[512,640]{1,0:T(8,128)(2,1)S(1)}, bf16[512,640]{1,0:T(8,128)(2,1)S(1)}, u32[]{:S(2)}, u32[]{:S(2)}) %collective-permute-start.2) | collective-permute-done | bytes 655392 | tf_op jit(solution)/shard_map/ppermute | solution.py:202
  30.0 9.2 %collective-permute-start.3 = (bf16[512,640]{1,0:T(8,128)(2,1)S(1)}, bf16[512,640]{1,0:T(8,128)(2,1)S(1)}, u32[]{:S(2)}, u32[]{:S(2)}) collective-permute-start(bf16[512,640]{1,0:T(8,128)(2,1)S(1)} %collective-permute-done.2.text_ref), channel_id=1, source_target_pairs={{0,2},{1,511},{2,4},{3,1},{4,6},{5,3},{6,8},{7,5},{8,10},{9,7},{10... | collective-permute-start | bytes 1966088 | tf_op jit(solution)/shard_map/ppermute | solution.py:203
  40.5 0.1 pad_maximum_fusion.1.scal_ref
  40.6 0.0 collective-permute-done.other_ref
  40.6 0.0 copy-start
  40.6 1.4 copy-done
  41.9 0.0 copy-start.2
  41.9 1.3 shard_map.84
  43.3 0.0 copy-done.2
  43.3 2.0 %shard_map.85 = (f32[512,640]{1,0:T(8,128)S(1)}, f32[256,640]{1,0:T(8,128)S(1)}, f32[8,256]{1,0:T(8,128)S(1)}) custom-call(f32[2]{0:T(128)S(1)} %pad_maximum_fusion.1.scal_ref, bf16[512,640]{1,0:T(8,128)(2,1)S(1)} %get-tuple-element.22.zib_ref, bf16[256,640]{1,0:T(8,128)(2,1)S(1)} %copy-done.2), custom_call_target="tpu_custom_call" | custom-call | flops 503316480 | bytes 4194304 | tf_op jit(solution)/shard_map/pallas_call | solution.py:101
  45.3 0.0 copy-start.4
  45.3 0.9 copy-done.4
  46.2 3.1 %shard_map.86 = (f32[512,640]{1,0:T(8,128)S(1)}, f32[512,640]{1,0:T(8,128)S(1)}, f32[8,256]{1,0:T(8,128)S(1)}) custom-call(f32[2]{0:T(128)S(1)} %pad_maximum_fusion.1.scal_ref, bf16[512,640]{1,0:T(8,128)(2,1)S(1)} %get-tuple-element.22.zib_ref, bf16[512,640]{1,0:T(8,128)(2,1)S(1)} %collective-permute-done.2.text_ref, f32[512,640]{1,0:T(8,128)S(1)} %get-tuple-element.23.refs_0_), custom_call_target="tpu_custom_call" | custom-call | flops 1006632960 | bytes 4194304 | tf_op jit(solution)/shard_map/pallas_call | solution.py:101
  49.2 0.0 copy-start.3
  49.3 1.0 copy-done.3
  50.3 0.0 collective-permute-done.3.text_ref
  50.3 2.6 %shard_map.87 = (f32[512,640]{1,0:T(8,128)S(1)}, bf16[512,640]{1,0:T(8,128)(2,1)S(1)}, f32[8,256]{1,0:T(8,128)S(1)}) custom-call(f32[2]{0:T(128)S(1)} %pad_maximum_fusion.1.scal_ref, bf16[512,640]{1,0:T(8,128)(2,1)S(1)} %get-tuple-element.22.zib_ref, bf16[512,640]{1,0:T(8,128)(2,1)S(1)} %collective-permute-done.3.text_ref, ...), custom_call_target="tpu_custom_call" | custom-call | flops 754974720 | bytes 4194304 | tf_op jit(solution)/shard_map/pallas_call | solution.py:101
  52.9 1.9 %collective-permute-start.4 = (f32[512,640]{1,0:T(8,128)S(1)}, f32[512,640]{1,0:T(8,128)S(1)}, u32[]{:S(2)}, u32[]{:S(2)}) collective-permute-start(f32[512,640]{1,0:T(8,128)S(1)} %get-tuple-element.25.dzi_ref), channel_id=1, source_target_pairs={{0,1},{1,0},{2,3},{3,2},{4,5},{5,4},{6,7},{7,6},{8,9},{9,8},{10,11... | collective-permute-start | bytes 3932168 | tf_op jit(solution)/shard_map/ppermute | solution.py:225
  54.8 3.0 %collective-permute-done.4.sent_ref = f32[512,640]{1,0:T(8,128)S(1)} collective-permute-done((f32[512,640]{1,0:T(8,128)S(1)}, f32[512,640]{1,0:T(8,128)S(1)}, u32[]{:S(2)}, u32[]{:S(2)}) %collective-permute-start.4) | collective-permute-done | bytes 1310752 | tf_op jit(solution)/shard_map/ppermute | solution.py:225
  57.8 2.3 %shard_map.88 = (bf16[256,640]{1,0:T(8,128)(2,1)S(1)}, bf16[3072,128]{1,0:T(8,128)(2,1)}) custom-call(f32[512,640]{1,0:T(8,128)S(1)} %get-tuple-element.25.dzi_ref, f32[512,640]{1,0:T(8,128)S(1)} %collective-permute-done.4.sent_ref, f32[512,640]{1,0:T(8,128)S(1)} %get-tuple-element.26.zi_ref, f32[512,128]{1,0:T(8,128)S(1)} %get-tuple-element.27.inv_ref, ...), custom_call_target="tpu_custom_call" | custom-call | flops 377487360 | bytes 7340032 | tf_op jit(solution)/shard_map/pallas_call | solution.py:229
  60.1 0.0 copy-start.6
  60.1 0.7 copy-done.6
  60.8 9.9 %all-to-all-start = ((bf16[256,6,2,128]{3,2,1,0:T(2,128)(2,1)}), bf16[256,6,2,128]{3,2,1,0:T(2,128)(2,1)S(1)}, u32[]{:S(2)}, u32[]{:S(2)}) async-start(bf16[256,6,2,128]{3,2,1,0:T(2,128)(2,1)} %bitcast.2), calls=%async_computation | async-start | bytes 1572864 | tf_op jit(solution)/shard_map/all_to_all | solution.py:248
  70.8 24.9 %all-to-all-done = bf16[256,6,2,128]{3,2,1,0:T(2,128)(2,1)S(1)} async-done(((bf16[256,6,2,128]{3,2,1,0:T(2,128)(2,1)}), bf16[256,6,2,128]{3,2,1,0:T(2,128)(2,1)S(1)}, u32[]{:S(2)}, u32[]{:S(2)}) %all-to-all-start) | async-done | bytes 786464 | tf_op jit(solution)/shard_map/all_to_all | solution.py:248
  95.7 1.2 shard_map.89
  96.9 9.2 %all-to-all-start.1 = ((bf16[256,6,2,128]{3,2,1,0:T(2,128)(2,1)}), bf16[256,6,2,128]{3,2,1,0:T(2,128)(2,1)S(1)}, u32[]{:S(2)}, u32[]{:S(2)}) async-start(bf16[256,6,2,128]{3,2,1,0:T(2,128)(2,1)} %bitcast.4), calls=%async_computation.1 | async-start | bytes 1572864 | tf_op jit(solution)/shard_map/all_to_all | solution.py:259
  106.1 1.9 %collective-permute-start.6 = (bf16[512,640]{1,0:T(8,128)(2,1)S(1)}, bf16[512,640]{1,0:T(8,128)(2,1)S(1)}, u32[]{:S(2)}, u32[]{:S(2)}) collective-permute-start(bf16[512,640]{1,0:T(8,128)(2,1)S(1)} %get-tuple-element.36), channel_id=1, source_target_pairs={{2,0},{511,1},{4,2},{1,3},{6,4},{3,5},{8,6},{5,7},{10,8},{7,9},{12... | collective-permute-start | bytes 1966088 | tf_op jit(solution)/shard_map/ppermute | solution.py:226
  108.0 0.0 copy-start.1
  108.0 28.1 %collective-permute-done.6 = bf16[512,640]{1,0:T(8,128)(2,1)S(1)} collective-permute-done((bf16[512,640]{1,0:T(8,128)(2,1)S(1)}, bf16[512,640]{1,0:T(8,128)(2,1)S(1)}, u32[]{:S(2)}, u32[]{:S(2)}) %collective-permute-start.6) | collective-permute-done | bytes 655392 | tf_op jit(solution)/shard_map/ppermute | solution.py:226
  136.1 2.3 %add_convert_fusion = bf16[512,640]{1,0:T(8,128)(2,1)} fusion(f32[512,640]{1,0:T(8,128)} %copy-done.3, bf16[512,640]{1,0:T(8,128)(2,1)S(1)} %collective-permute-done.6), kind=kLoop, calls=%fused_computation.1 | loop fusion | flops 983040 | bytes 2621440 | tf_op jit(solution)/shard_map/convert_element_type | solution.py:244
  138.4 1.9 %collective-permute-start.7 = (bf16[512,640]{1,0:T(8,128)(2,1)}, bf16[512,640]{1,0:T(8,128)(2,1)S(1)}, u32[]{:S(2)}, u32[]{:S(2)}) collective-permute-start(bf16[512,640]{1,0:T(8,128)(2,1)} %add_convert_fusion), channel_id=1, source_target_pairs={{2,0},{511,1},{4,2},{1,3},{6,4},{3,5},{8,6},{5,7},{10,8},{7,9},{12... | collective-permute-start | bytes 1966088 | tf_op jit(solution)/shard_map/ppermute | solution.py:245
  140.4 0.0 all-to-all-done.1
  140.4 3.7 %collective-permute-start.5 = (bf16[3072,128]{1,0:T(8,128)(2,1)S(1)}, bf16[3072,128]{1,0:T(8,128)(2,1)S(1)}, u32[]{:S(2)}, u32[]{:S(2)}) collective-permute-start(bf16[3072,128]{1,0:T(8,128)(2,1)S(1)} %bitcast.9), channel_id=1, source_target_pairs={{0,1},{1,0},{2,3},{3,2},{4,5},{5,4},{6,7},{7,6},{8,9},{9,8},{10,11... | collective-permute-start | bytes 2359304 | tf_op jit(solution)/shard_map/ppermute | solution.py:260
  144.1 11.3 %collective-permute-done.7.far_ref = bf16[512,640]{1,0:T(8,128)(2,1)S(1)} collective-permute-done((bf16[512,640]{1,0:T(8,128)(2,1)}, bf16[512,640]{1,0:T(8,128)(2,1)S(1)}, u32[]{:S(2)}, u32[]{:S(2)}) %collective-permute-start.7) | collective-permute-done | bytes 655392 | tf_op jit(solution)/shard_map/ppermute | solution.py:245
  155.4 0.0 copy-start.5
  155.4 2.1 %collective-permute-start.8 = (bf16[256,640]{1,0:T(8,128)(2,1)S(1)}, bf16[256,640]{1,0:T(8,128)(2,1)S(1)}, u32[]{:S(2)}, u32[]{:S(2)}) collective-permute-start(bf16[256,640]{1,0:T(8,128)(2,1)S(1)} %slice.4), channel_id=1, source_target_pairs={{0,1},{1,0},{2,3},{3,2},{4,5},{5,4},{6,7},{7,6},{8,9},{9,8},{10,11... | collective-permute-start | bytes 983048 | tf_op jit(solution)/shard_map/ppermute | solution.py:262
  157.5 0.0 copy-done.1
  157.5 2.5 %convolution_convert_fusion = bf16[256,1152]{1,0:T(8,128)(2,1)} fusion(bf16[256,640]{1,0:T(8,128)(2,1)} %copy-done.6, bf16[1152,640]{1,0:T(8,128)(2,1)S(1)} %copy-done.1), kind=kOutput, calls=%fused_computation | convolution fusion | flops 377782272 | bytes 2392064 | tf_op jit(solution)/shard_map/dot_general | solution.py:263
  160.0 0.0 collective-permute-done.8.near_ref
  160.0 0.0 copy-done.5
  160.0 1.0 shard_map.91
  161.0 0.0 collective-permute-done.5.other_ref
  161.0 1.4 shard_map.90
  (1 shorter events, 0.0 us)
Async XLA Ops:
  0.6 21.8 %copy-start.7 = (bf16[256,1152]{1,0:T(8,128)(2,1)S(1)}, bf16[256,1152]{1,0:T(8,128)(2,1)}, u32[]{:S(2)}) copy-start(bf16[256,1152]{1,0:T(8,128)(2,1)} %own_ref.1) | copy-start | bytes 1769476
  0.6 10.4 %collective-permute-start.1 = (bf16[256,640]{1,0:T(8,128)(2,1)}, bf16[256,640]{1,0:T(8,128)(2,1)S(1)}, u32[]{:S(2)}, u32[]{:S(2)}) collective-permute-start(bf16[256,640]{1,0:T(8,128)(2,1)} %text_ref.3), channel_id=1, source_target_pairs={{0,1},{1,0},{2,3},{3,2},{4,5},{5,4},{6,7},{7,6},{8,9},{9,8},{10,11... | collective-permute-start | bytes 983048 | tf_op jit(solution)/shard_map/ppermute | solution.py:199
  12.0 17.9 %collective-permute-start.2 = (bf16[512,640]{1,0:T(8,128)(2,1)S(1)}, bf16[512,640]{1,0:T(8,128)(2,1)S(1)}, u32[]{:S(2)}, u32[]{:S(2)}) collective-permute-start(bf16[512,640]{1,0:T(8,128)(2,1)S(1)} %pad_maximum_fusion), channel_id=1, source_target_pairs={{0,2},{1,511},{2,4},{3,1},{4,6},{5,3},{6,8},{7,5},{8,10},{9,7},{10... | collective-permute-start | bytes 1966088 | tf_op jit(solution)/shard_map/ppermute | solution.py:202
  22.5 18.1 %collective-permute-start = (bf16[256,1152]{1,0:T(8,128)(2,1)S(1)}, bf16[256,1152]{1,0:T(8,128)(2,1)S(1)}, u32[]{:S(2)}, u32[]{:S(2)}) collective-permute-start(bf16[256,1152]{1,0:T(8,128)(2,1)S(1)} %copy-done.7), channel_id=1, source_target_pairs={{0,1},{1,0},{2,3},{3,2},{4,5},{5,4},{6,7},{7,6},{8,9},{9,8},{10,11... | collective-permute-start | bytes 1769480 | tf_op jit(solution)/shard_map/ppermute | solution.py:200
  30.0 20.4 %collective-permute-start.3 = (bf16[512,640]{1,0:T(8,128)(2,1)S(1)}, bf16[512,640]{1,0:T(8,128)(2,1)S(1)}, u32[]{:S(2)}, u32[]{:S(2)}) collective-permute-start(bf16[512,640]{1,0:T(8,128)(2,1)S(1)} %collective-permute-done.2.text_ref), channel_id=1, source_target_pairs={{0,2},{1,511},{2,4},{3,1},{4,6},{5,3},{6,8},{7,5},{8,10},{9,7},{10... | collective-permute-start | bytes 1966088 | tf_op jit(solution)/shard_map/ppermute | solution.py:203
  40.6 1.4 copy-start
  41.9 1.4 copy-start.2
  45.3 0.9 copy-start.4
  49.2 1.1 copy-start.3
  52.9 4.9 %collective-permute-start.4 = (f32[512,640]{1,0:T(8,128)S(1)}, f32[512,640]{1,0:T(8,128)S(1)}, u32[]{:S(2)}, u32[]{:S(2)}) collective-permute-start(f32[512,640]{1,0:T(8,128)S(1)} %get-tuple-element.25.dzi_ref), channel_id=1, source_target_pairs={{0,1},{1,0},{2,3},{3,2},{4,5},{5,4},{6,7},{7,6},{8,9},{9,8},{10,11... | collective-permute-start | bytes 3932168 | tf_op jit(solution)/shard_map/ppermute | solution.py:225
  60.1 0.7 copy-start.6
  60.8 34.9 %all-to-all-start = ((bf16[256,6,2,128]{3,2,1,0:T(2,128)(2,1)}), bf16[256,6,2,128]{3,2,1,0:T(2,128)(2,1)S(1)}, u32[]{:S(2)}, u32[]{:S(2)}) async-start(bf16[256,6,2,128]{3,2,1,0:T(2,128)(2,1)} %bitcast.2), calls=%async_computation | async-start | bytes 1572864 | tf_op jit(solution)/shard_map/all_to_all | solution.py:248
  96.9 43.5 %all-to-all-start.1 = ((bf16[256,6,2,128]{3,2,1,0:T(2,128)(2,1)}), bf16[256,6,2,128]{3,2,1,0:T(2,128)(2,1)S(1)}, u32[]{:S(2)}, u32[]{:S(2)}) async-start(bf16[256,6,2,128]{3,2,1,0:T(2,128)(2,1)} %bitcast.4), calls=%async_computation.1 | async-start | bytes 1572864 | tf_op jit(solution)/shard_map/all_to_all | solution.py:259
  106.1 30.0 %collective-permute-start.6 = (bf16[512,640]{1,0:T(8,128)(2,1)S(1)}, bf16[512,640]{1,0:T(8,128)(2,1)S(1)}, u32[]{:S(2)}, u32[]{:S(2)}) collective-permute-start(bf16[512,640]{1,0:T(8,128)(2,1)S(1)} %get-tuple-element.36), channel_id=1, source_target_pairs={{2,0},{511,1},{4,2},{1,3},{6,4},{3,5},{8,6},{5,7},{10,8},{7,9},{12... | collective-permute-start | bytes 1966088 | tf_op jit(solution)/shard_map/ppermute | solution.py:226
  108.0 49.5 %copy-start.1 = (bf16[1152,640]{1,0:T(8,128)(2,1)S(1)}, bf16[1152,640]{1,0:T(8,128)(2,1)}, u32[]{:S(2)}) copy-start(bf16[1152,640]{1,0:T(8,128)(2,1)} %weight_ref.1) | copy-start | bytes 4423684
  138.4 17.0 %collective-permute-start.7 = (bf16[512,640]{1,0:T(8,128)(2,1)}, bf16[512,640]{1,0:T(8,128)(2,1)S(1)}, u32[]{:S(2)}, u32[]{:S(2)}) collective-permute-start(bf16[512,640]{1,0:T(8,128)(2,1)} %add_convert_fusion), channel_id=1, source_target_pairs={{2,0},{511,1},{4,2},{1,3},{6,4},{3,5},{8,6},{5,7},{10,8},{7,9},{12... | collective-permute-start | bytes 1966088 | tf_op jit(solution)/shard_map/ppermute | solution.py:245
  140.4 20.6 %collective-permute-start.5 = (bf16[3072,128]{1,0:T(8,128)(2,1)S(1)}, bf16[3072,128]{1,0:T(8,128)(2,1)S(1)}, u32[]{:S(2)}, u32[]{:S(2)}) collective-permute-start(bf16[3072,128]{1,0:T(8,128)(2,1)S(1)} %bitcast.9), channel_id=1, source_target_pairs={{0,1},{1,0},{2,3},{3,2},{4,5},{5,4},{6,7},{7,6},{8,9},{9,8},{10,11... | collective-permute-start | bytes 2359304 | tf_op jit(solution)/shard_map/ppermute | solution.py:260
  155.4 4.5 %copy-start.5 = (f32[256,640]{1,0:T(8,128)S(1)}, f32[256,640]{1,0:T(8,128)}, u32[]{:S(2)}) copy-start(f32[256,640]{1,0:T(8,128)} %copy-done.4) | copy-start | bytes 1966084
  155.4 4.5 %collective-permute-start.8 = (bf16[256,640]{1,0:T(8,128)(2,1)S(1)}, bf16[256,640]{1,0:T(8,128)(2,1)S(1)}, u32[]{:S(2)}, u32[]{:S(2)}) collective-permute-start(bf16[256,640]{1,0:T(8,128)(2,1)S(1)} %slice.4), channel_id=1, source_target_pairs={{0,1},{1,0},{2,3},{3,2},{4,5},{5,4},{6,7},{7,6},{8,9},{9,8},{10,11... | collective-permute-start | bytes 983048 | tf_op jit(solution)/shard_map/ppermute | solution.py:262

commit v2 on v1

--- a/solution.py
+++ b/solution.py
@@ -19,7 +19,7 @@
 F32 = jnp.float32
 VMEM = pl.BlockSpec(memory_space=pltpu.VMEM)
 SMEM = pl.BlockSpec(memory_space=pltpu.SMEM)
-PARAMS = pltpu.CompilerParams(vmem_limit_bytes=32 * 1024 * 1024)
+PARAMS = pltpu.CompilerParams(vmem_limit_bytes=10 * 1024 * 1024)
 
 
 def call(body, out_shape, n_smem, n_vmem, out_specs, scratch=(), flops=0, bytes_accessed=0):
@@ -240,9 +240,7 @@
         bytes_accessed=7 << 20,
     )(dzi, dzi_sent, zi, inv_u, x_half, loss0, loss1, loss2)
 
-    dzt1, _ = lax.optimization_barrier((dzt1, flat))
     near = (far.astype(F32) + dzt1).astype(BF)
-    near = lax.ppermute(near, axes, back)
 
     share = flat_rows // chips
     pieces = lax.all_to_all(flat.reshape(chips, share // 2, 2, LANES), "chip", 0, 0)
@@ -256,10 +254,13 @@
         flops=flat_rows * LANES,
         bytes_accessed=2 << 20,
     )(chip_id, pieces.reshape(flat_rows, LANES)).reshape(chips, share // 2, 2, LANES)
+    spread, near = lax.optimization_barrier((spread, near))
+    near = lax.ppermute(near, axes, back)
     half = lax.all_to_all(spread, "chip", 0, 0).reshape(flat_rows, LANES)
+    near_other = lax.ppermute(near[ROWS:], axes, across)
+    half, near_other = lax.optimization_barrier((half, near_other))
     half_other = lax.ppermute(half, axes, across)
 
-    near_other = lax.ppermute(near[ROWS:], axes, across)
     image_grad = lax.dot_general(du, head_weight, (((1,), (1,)), ((), ())), preferred_element_type=F32).astype(BF)
     text_grad = call(
         text_kernel, jax.ShapeDtypeStruct((ROWS, E), BF), 0, 4, VMEM, flops=10 * ROWS * E, bytes_accessed=3 << 20

time: 165 us -> 161 us (0.976)
  waiting for transfers between devices: 74.4 us -> 67.6 us
    all_to_all x1, waiting for transfers between devices: 24.9 us -> 0.01 us  [per_device(): lax.all_to_all(flat.reshape(chips, share // 2, 2, LANES), 'chip', 0, 0)]
    ppermute x1, waiting for transfers between devices: 11.3 us -> 28.1 us  [per_device(): near = lax.ppermute(near, axes, back)]
    unnamed x16 -> x22, local copies, waits for them, and re-layouts: 4.03 us -> 5.59 us
where the time goes in v2:
time: 161 us; the launch traced here: 160 us
  waiting for transfers between devices  67.6 us (42%)
  starting transfers between devices  62.4 us (39%)
  Pallas kernels  14.9 us (9%)
  local copies, waits for them, and re-layouts  5.62 us (3%)
  between operations  3.88 us (2%)
  other arithmetic  3.16 us (2%)
  matrix products  2.45 us (2%)
    ppermute x1, waiting for transfers between devices, per_device(): near = lax.ppermute(near, axes, back)  28.1 us
    ppermute x1, waiting for transfers between devices, per_device(): far = lax.ppermute(dzt2, axes, back)  28.1 us
    all_to_all x1, starting transfers between devices, per_device(): half = lax.all_to_all(spread, 'chip', 0, 0).reshape(flat_rows, LANES)  10.8 us
    all_to_all x1, starting transfers between devices, per_device(): lax.all_to_all(flat.reshape(chips, share // 2, 2, LANES), 'chip', 0, 0)  10.8 us
    ppermute x1, starting transfers between devices, per_device(): texts1 = lax.ppermute(texts0, axes, onward)  10.4 us
    ppermute x1, starting transfers between devices, per_device(): texts2 = lax.ppermute(texts1, axes, onward)  9.23 us
    ppermute x1, starting transfers between devices, per_device(): text_other = lax.ppermute(text_embeds, axes, across)  8.92 us
    pallas_call x3, Pallas kernels, score(): call(functools.partial(score_kernel, parts, dzi is not None), (jax.ShapeD...  7.61 us
  transfers between devices with their start and end apart: 11, of which 6 were waited for; matrix products, arithmetic and copies ran while one was open for 3% of the time, Pallas kernels for 5%

profile of v2, /device:TPU:1, one launch (start us, length us, event | category | flops | bytes accessed | tf_op | source)
XLA Modules:
  0.0 160.0 jit_solution(4215495583394615923)
XLA Ops:
  0.6 0.0 copy-start.10
  0.6 8.9 %collective-permute-start.1 = (bf16[256,640]{1,0:T(8,128)(2,1)}, bf16[256,640]{1,0:T(8,128)(2,1)S(1)}, u32[]{:S(2)}, u32[]{:S(2)}) collective-permute-start(bf16[256,640]{1,0:T(8,128)(2,1)} %text_ref.3), channel_id=1, source_target_pairs={{0,1},{1,0},{2,3},{3,2},{4,5},{5,4},{6,7},{7,6},{8,9},{9,8},{10,11... | collective-permute-start | bytes 983048 | tf_op jit(solution)/shard_map/ppermute | solution.py:199
  9.6 1.4 collective-permute-done.1
  11.0 1.0 pad_maximum_fusion
  12.0 10.4 %collective-permute-start.2 = (bf16[512,640]{1,0:T(8,128)(2,1)S(1)}, bf16[512,640]{1,0:T(8,128)(2,1)S(1)}, u32[]{:S(2)}, u32[]{:S(2)}) collective-permute-start(bf16[512,640]{1,0:T(8,128)(2,1)S(1)} %pad_maximum_fusion), channel_id=1, source_target_pairs={{0,2},{1,511},{2,4},{3,1},{4,6},{5,3},{6,8},{7,5},{8,10},{9,7},{10... | collective-permute-start | bytes 1966088 | tf_op jit(solution)/shard_map/ppermute | solution.py:202
  22.4 0.0 copy-done.10
  22.5 1.9 %collective-permute-start = (bf16[256,1152]{1,0:T(8,128)(2,1)S(1)}, bf16[256,1152]{1,0:T(8,128)(2,1)S(1)}, u32[]{:S(2)}, u32[]{:S(2)}) collective-permute-start(bf16[256,1152]{1,0:T(8,128)(2,1)S(1)} %copy-done.10), channel_id=1, source_target_pairs={{0,1},{1,0},{2,3},{3,2},{4,5},{5,4},{6,7},{7,6},{8,9},{9,8},{10,11... | collective-permute-start | bytes 1769480 | tf_op jit(solution)/shard_map/ppermute | solution.py:200
  24.4 5.6 %collective-permute-done.2.text_ref = bf16[512,640]{1,0:T(8,128)(2,1)S(1)} collective-permute-done((bf16[512,640]{1,0:T(8,128)(2,1)S(1)}, bf16[512,640]{1,0:T(8,128)(2,1)S(1)}, u32[]{:S(2)}, u32[]{:S(2)}) %collective-permute-start.2) | collective-permute-done | bytes 655392 | tf_op jit(solution)/shard_map/ppermute | solution.py:202
  30.0 9.2 %collective-permute-start.3 = (bf16[512,640]{1,0:T(8,128)(2,1)S(1)}, bf16[512,640]{1,0:T(8,128)(2,1)S(1)}, u32[]{:S(2)}, u32[]{:S(2)}) collective-permute-start(bf16[512,640]{1,0:T(8,128)(2,1)S(1)} %collective-permute-done.2.text_ref), channel_id=1, source_target_pairs={{0,2},{1,511},{2,4},{3,1},{4,6},{5,3},{6,8},{7,5},{8,10},{9,7},{10... | collective-permute-start | bytes 1966088 | tf_op jit(solution)/shard_map/ppermute | solution.py:203
  40.5 0.1 pad_maximum_fusion.1.scal_ref
  40.6 0.0 collective-permute-done.other_ref
  40.6 0.0 copy-start
  40.6 1.4 copy-done
  41.9 0.0 copy-start.2
  41.9 1.4 shard_map.84
  43.3 0.0 copy-done.2
  43.4 2.0 %shard_map.85 = (f32[512,640]{1,0:T(8,128)S(1)}, f32[256,640]{1,0:T(8,128)S(1)}, f32[8,256]{1,0:T(8,128)S(1)}) custom-call(f32[2]{0:T(128)S(1)} %pad_maximum_fusion.1.scal_ref, bf16[512,640]{1,0:T(8,128)(2,1)S(1)} %get-tuple-element.25.zib_ref, bf16[256,640]{1,0:T(8,128)(2,1)S(1)} %copy-done.2), custom_call_target="tpu_custom_call" | custom-call | flops 503316480 | bytes 4194304 | tf_op jit(solution)/shard_map/pallas_call | solution.py:101
  45.3 0.0 copy-start.3
  45.3 0.8 copy-done.3
  46.2 3.1 %shard_map.86 = (f32[512,640]{1,0:T(8,128)S(1)}, f32[512,640]{1,0:T(8,128)S(1)}, f32[8,256]{1,0:T(8,128)S(1)}) custom-call(f32[2]{0:T(128)S(1)} %pad_maximum_fusion.1.scal_ref, bf16[512,640]{1,0:T(8,128)(2,1)S(1)} %get-tuple-element.25.zib_ref, bf16[512,640]{1,0:T(8,128)(2,1)S(1)} %collective-permute-done.2.text_ref, f32[512,640]{1,0:T(8,128)S(1)} %get-tuple-element.26.refs_0_), custom_call_target="tpu_custom_call" | custom-call | flops 1006632960 | bytes 4194304 | tf_op jit(solution)/shard_map/pallas_call | solution.py:101
  49.3 0.0 collective-permute-done.3.text_ref
  49.3 0.0 copy-start.8
  49.3 0.8 copy-done.8
  50.1 0.0 copy-start.9
  50.1 1.1 copy-done.9
  51.2 2.6 %shard_map.87 = (f32[512,640]{1,0:T(8,128)S(1)}, bf16[512,640]{1,0:T(8,128)(2,1)S(1)}, f32[8,256]{1,0:T(8,128)S(1)}) custom-call(f32[2]{0:T(128)S(1)} %pad_maximum_fusion.1.scal_ref, bf16[512,640]{1,0:T(8,128)(2,1)S(1)} %get-tuple-element.25.zib_ref, bf16[512,640]{1,0:T(8,128)(2,1)S(1)} %copy-done.9, f32[512,640]{1,0:T(8,128)S(1)} %get-tuple-element.27.refs_0_), custom_call_target="tpu_custom_call" | custom-call | flops 754974720 | bytes 4194304 | tf_op jit(solution)/shard_map/pallas_call | solution.py:101
  53.8 2.2 %collective-permute-start.4 = (f32[512,640]{1,0:T(8,128)S(1)}, f32[512,640]{1,0:T(8,128)S(1)}, u32[]{:S(2)}, u32[]{:S(2)}) collective-permute-start(f32[512,640]{1,0:T(8,128)S(1)} %get-tuple-element.28.dzi_ref), channel_id=1, source_target_pairs={{0,1},{1,0},{2,3},{3,2},{4,5},{5,4},{6,7},{7,6},{8,9},{9,8},{10,11... | collective-permute-start | bytes 3932168 | tf_op jit(solution)/shard_map/ppermute | solution.py:225
  55.9 2.7 %collective-permute-done.4.sent_ref = f32[512,640]{1,0:T(8,128)S(1)} collective-permute-done((f32[512,640]{1,0:T(8,128)S(1)}, f32[512,640]{1,0:T(8,128)S(1)}, u32[]{:S(2)}, u32[]{:S(2)}) %collective-permute-start.4) | collective-permute-done | bytes 1310752 | tf_op jit(solution)/shard_map/ppermute | solution.py:225
  58.7 2.3 %shard_map.88 = (bf16[256,640]{1,0:T(8,128)(2,1)S(1)}, bf16[3072,128]{1,0:T(8,128)(2,1)}) custom-call(f32[512,640]{1,0:T(8,128)S(1)} %get-tuple-element.28.dzi_ref, f32[512,640]{1,0:T(8,128)S(1)} %collective-permute-done.4.sent_ref, f32[512,640]{1,0:T(8,128)S(1)} %get-tuple-element.29.zi_ref, f32[512,128]{1,0:T(8,128)S(1)} %get-tuple-element.30.inv_ref, ...), custom_call_target="tpu_custom_call" | custom-call | flops 377487360 | bytes 7340032 | tf_op jit(solution)/shard_map/pallas_call | solution.py:229
  61.0 0.0 copy-start.5
  61.0 0.7 copy-done.5
  61.7 10.8 %all-to-all-start = ((bf16[256,6,2,128]{3,2,1,0:T(2,128)(2,1)}), bf16[256,6,2,128]{3,2,1,0:T(2,128)(2,1)S(1)}, u32[]{:S(2)}, u32[]{:S(2)}) async-start(bf16[256,6,2,128]{3,2,1,0:T(2,128)(2,1)} %bitcast.2), calls=%async_computation | async-start | bytes 1572864 | tf_op jit(solution)/shard_map/all_to_all | solution.py:246
  72.5 2.1 %collective-permute-start.5 = (bf16[512,640]{1,0:T(8,128)(2,1)S(1)}, bf16[512,640]{1,0:T(8,128)(2,1)}, u32[]{:S(2)}, u32[]{:S(2)}) collective-permute-start(bf16[512,640]{1,0:T(8,128)(2,1)S(1)} %get-tuple-element.36), channel_id=1, source_target_pairs={{2,0},{511,1},{4,2},{1,3},{6,4},{3,5},{8,6},{5,7},{10,8},{7,9},{12... | collective-permute-start | bytes 1966088 | tf_op jit(solution)/shard_map/ppermute | solution.py:226
  74.6 28.1 %collective-permute-done.5 = bf16[512,640]{1,0:T(8,128)(2,1)} collective-permute-done((bf16[512,640]{1,0:T(8,128)(2,1)S(1)}, bf16[512,640]{1,0:T(8,128)(2,1)}, u32[]{:S(2)}, u32[]{:S(2)}) %collective-permute-start.5) | collective-permute-done | bytes 655392 | tf_op jit(solution)/shard_map/ppermute | solution.py:226
  102.7 2.1 %add_convert_fusion = bf16[512,640]{1,0:T(8,128)(2,1)} fusion(f32[512,640]{1,0:T(8,128)S(1)} %get-tuple-element.37, bf16[512,640]{1,0:T(8,128)(2,1)} %collective-permute-done.5), kind=kLoop, calls=%fused_computation.1 | loop fusion | flops 983040 | bytes 2621440 | tf_op jit(solution)/shard_map/convert_element_type | solution.py:243
  104.8 0.0 all-to-all-done
  104.8 1.2 shard_map.89
  106.0 0.0 copy-start.1
  106.0 10.8 %all-to-all-start.1 = ((bf16[256,6,2,128]{3,2,1,0:T(2,128)(2,1)}), bf16[256,6,2,128]{3,2,1,0:T(2,128)(2,1)S(1)}, u32[]{:S(2)}, u32[]{:S(2)}) async-start(bf16[256,6,2,128]{3,2,1,0:T(2,128)(2,1)} %bitcast.4), calls=%async_computation.1 | async-start | bytes 1572864 | tf_op jit(solution)/shard_map/all_to_all | solution.py:259
  116.8 1.9 %collective-permute-start.6 = (bf16[512,640]{1,0:T(8,128)(2,1)}, bf16[512,640]{1,0:T(8,128)(2,1)S(1)}, u32[]{:S(2)}, u32[]{:S(2)}) collective-permute-start(bf16[512,640]{1,0:T(8,128)(2,1)} %add_convert_fusion), channel_id=1, source_target_pairs={{2,0},{511,1},{4,2},{1,3},{6,4},{3,5},{8,6},{5,7},{10,8},{7,9},{12... | collective-permute-start | bytes 1966088 | tf_op jit(solution)/shard_map/ppermute | solution.py:258
  118.7 28.1 %collective-permute-done.6.far_ref = bf16[512,640]{1,0:T(8,128)(2,1)S(1)} collective-permute-done((bf16[512,640]{1,0:T(8,128)(2,1)}, bf16[512,640]{1,0:T(8,128)(2,1)S(1)}, u32[]{:S(2)}, u32[]{:S(2)}) %collective-permute-start.6) | collective-permute-done | bytes 655392 | tf_op jit(solution)/shard_map/ppermute | solution.py:258
  146.9 1.9 %collective-permute-start.7 = (bf16[256,640]{1,0:T(8,128)(2,1)S(1)}, bf16[256,640]{1,0:T(8,128)(2,1)S(1)}, u32[]{:S(2)}, u32[]{:S(2)}) collective-permute-start(bf16[256,640]{1,0:T(8,128)(2,1)S(1)} %slice.4), channel_id=1, source_target_pairs={{0,1},{1,0},{2,3},{3,2},{4,5},{5,4},{6,7},{7,6},{8,9},{9,8},{10,11... | collective-permute-start | bytes 983048 | tf_op jit(solution)/shard_map/ppermute | solution.py:260
  148.8 1.6 collective-permute-done.7.near_ref
  150.4 0.0 copy-start.6
  150.4 0.7 copy-done.6
  151.1 0.0 all-to-all-done.1
  151.2 0.0 copy-start.4
  151.2 0.0 copy-start.7
  151.2 2.2 %collective-permute-start.8 = (bf16[3072,128]{1,0:T(8,128)(2,1)S(1)}, bf16[3072,128]{1,0:T(8,128)(2,1)S(1)}, u32[]{:S(2)}, u32[]{:S(2)}) collective-permute-start(bf16[3072,128]{1,0:T(8,128)(2,1)S(1)} %bitcast.9), channel_id=1, source_target_pairs={{0,1},{1,0},{2,3},{3,2},{4,5},{5,4},{6,7},{7,6},{8,9},{9,8},{10,11... | collective-permute-start | bytes 2359304 | tf_op jit(solution)/shard_map/ppermute | solution.py:262
  153.3 0.0 copy-done.1
  153.3 2.5 %convolution_convert_fusion = bf16[256,1152]{1,0:T(8,128)(2,1)} fusion(bf16[256,640]{1,0:T(8,128)(2,1)} %copy-done.5, bf16[1152,640]{1,0:T(8,128)(2,1)S(1)} %copy-done.1), kind=kOutput, calls=%fused_computation | convolution fusion | flops 377782272 | bytes 2392064 | tf_op jit(solution)/shard_map/dot_general | solution.py:264
  155.8 0.0 copy-done.4
  155.8 0.0 copy-done.7
  155.8 1.0 shard_map.91
  156.8 0.0 collective-permute-done.8.other_ref
  156.8 1.4 shard_map.90
  (1 shorter events, 0.0 us)
Async XLA Ops:
  0.6 21.8 %copy-start.10 = (bf16[256,1152]{1,0:T(8,128)(2,1)S(1)}, bf16[256,1152]{1,0:T(8,128)(2,1)}, u32[]{:S(2)}) copy-start(bf16[256,1152]{1,0:T(8,128)(2,1)} %own_ref.1) | copy-start | bytes 1769476
  0.6 10.4 %collective-permute-start.1 = (bf16[256,640]{1,0:T(8,128)(2,1)}, bf16[256,640]{1,0:T(8,128)(2,1)S(1)}, u32[]{:S(2)}, u32[]{:S(2)}) collective-permute-start(bf16[256,640]{1,0:T(8,128)(2,1)} %text_ref.3), channel_id=1, source_target_pairs={{0,1},{1,0},{2,3},{3,2},{4,5},{5,4},{6,7},{7,6},{8,9},{9,8},{10,11... | collective-permute-start | bytes 983048 | tf_op jit(solution)/shard_map/ppermute | solution.py:199
  12.0 17.9 %collective-permute-start.2 = (bf16[512,640]{1,0:T(8,128)(2,1)S(1)}, bf16[512,640]{1,0:T(8,128)(2,1)S(1)}, u32[]{:S(2)}, u32[]{:S(2)}) collective-permute-start(bf16[512,640]{1,0:T(8,128)(2,1)S(1)} %pad_maximum_fusion), channel_id=1, source_target_pairs={{0,2},{1,511},{2,4},{3,1},{4,6},{5,3},{6,8},{7,5},{8,10},{9,7},{10... | collective-permute-start | bytes 1966088 | tf_op jit(solution)/shard_map/ppermute | solution.py:202
  22.5 18.1 %collective-permute-start = (bf16[256,1152]{1,0:T(8,128)(2,1)S(1)}, bf16[256,1152]{1,0:T(8,128)(2,1)S(1)}, u32[]{:S(2)}, u32[]{:S(2)}) collective-permute-start(bf16[256,1152]{1,0:T(8,128)(2,1)S(1)} %copy-done.10), channel_id=1, source_target_pairs={{0,1},{1,0},{2,3},{3,2},{4,5},{5,4},{6,7},{7,6},{8,9},{9,8},{10,11... | collective-permute-start | bytes 1769480 | tf_op jit(solution)/shard_map/ppermute | solution.py:200
  30.0 19.3 %collective-permute-start.3 = (bf16[512,640]{1,0:T(8,128)(2,1)S(1)}, bf16[512,640]{1,0:T(8,128)(2,1)S(1)}, u32[]{:S(2)}, u32[]{:S(2)}) collective-permute-start(bf16[512,640]{1,0:T(8,128)(2,1)S(1)} %collective-permute-done.2.text_ref), channel_id=1, source_target_pairs={{0,2},{1,511},{2,4},{3,1},{4,6},{5,3},{6,8},{7,5},{8,10},{9,7},{10... | collective-permute-start | bytes 1966088 | tf_op jit(solution)/shard_map/ppermute | solution.py:203
  40.6 1.4 copy-start
  41.9 1.4 copy-start.2
  45.3 0.8 copy-start.3
  49.3 0.8 copy-start.8
  50.1 1.1 copy-start.9
  53.8 4.9 %collective-permute-start.4 = (f32[512,640]{1,0:T(8,128)S(1)}, f32[512,640]{1,0:T(8,128)S(1)}, u32[]{:S(2)}, u32[]{:S(2)}) collective-permute-start(f32[512,640]{1,0:T(8,128)S(1)} %get-tuple-element.28.dzi_ref), channel_id=1, source_target_pairs={{0,1},{1,0},{2,3},{3,2},{4,5},{5,4},{6,7},{7,6},{8,9},{9,8},{10,11... | collective-permute-start | bytes 3932168 | tf_op jit(solution)/shard_map/ppermute | solution.py:225
  61.0 0.7 copy-start.5
  61.7 43.1 %all-to-all-start = ((bf16[256,6,2,128]{3,2,1,0:T(2,128)(2,1)}), bf16[256,6,2,128]{3,2,1,0:T(2,128)(2,1)S(1)}, u32[]{:S(2)}, u32[]{:S(2)}) async-start(bf16[256,6,2,128]{3,2,1,0:T(2,128)(2,1)} %bitcast.2), calls=%async_computation | async-start | bytes 1572864 | tf_op jit(solution)/shard_map/all_to_all | solution.py:246
  72.5 30.2 %collective-permute-start.5 = (bf16[512,640]{1,0:T(8,128)(2,1)S(1)}, bf16[512,640]{1,0:T(8,128)(2,1)}, u32[]{:S(2)}, u32[]{:S(2)}) collective-permute-start(bf16[512,640]{1,0:T(8,128)(2,1)S(1)} %get-tuple-element.36), channel_id=1, source_target_pairs={{2,0},{511,1},{4,2},{1,3},{6,4},{3,5},{8,6},{5,7},{10,8},{7,9},{12... | collective-permute-start | bytes 1966088 | tf_op jit(solution)/shard_map/ppermute | solution.py:226
  106.0 47.4 %copy-start.1 = (bf16[1152,640]{1,0:T(8,128)(2,1)S(1)}, bf16[1152,640]{1,0:T(8,128)(2,1)}, u32[]{:S(2)}) copy-start(bf16[1152,640]{1,0:T(8,128)(2,1)} %weight_ref.1) | copy-start | bytes 4423684
  106.0 45.2 %all-to-all-start.1 = ((bf16[256,6,2,128]{3,2,1,0:T(2,128)(2,1)}), bf16[256,6,2,128]{3,2,1,0:T(2,128)(2,1)S(1)}, u32[]{:S(2)}, u32[]{:S(2)}) async-start(bf16[256,6,2,128]{3,2,1,0:T(2,128)(2,1)} %bitcast.4), calls=%async_computation.1 | async-start | bytes 1572864 | tf_op jit(solution)/shard_map/all_to_all | solution.py:259
  116.8 30.1 %collective-permute-start.6 = (bf16[512,640]{1,0:T(8,128)(2,1)}, bf16[512,640]{1,0:T(8,128)(2,1)S(1)}, u32[]{:S(2)}, u32[]{:S(2)}) collective-permute-start(bf16[512,640]{1,0:T(8,128)(2,1)} %add_convert_fusion), channel_id=1, source_target_pairs={{2,0},{511,1},{4,2},{1,3},{6,4},{3,5},{8,6},{5,7},{10,8},{7,9},{12... | collective-permute-start | bytes 1966088 | tf_op jit(solution)/shard_map/ppermute | solution.py:258
  146.9 3.5 %collective-permute-start.7 = (bf16[256,640]{1,0:T(8,128)(2,1)S(1)}, bf16[256,640]{1,0:T(8,128)(2,1)S(1)}, u32[]{:S(2)}, u32[]{:S(2)}) collective-permute-start(bf16[256,640]{1,0:T(8,128)(2,1)S(1)} %slice.4), channel_id=1, source_target_pairs={{0,1},{1,0},{2,3},{3,2},{4,5},{5,4},{6,7},{7,6},{8,9},{9,8},{10,11... | collective-permute-start | bytes 983048 | tf_op jit(solution)/shard_map/ppermute | solution.py:260
  150.4 0.7 copy-start.6
  151.2 4.6 %copy-start.4 = (f32[256,640]{1,0:T(8,128)S(1)}, f32[256,640]{1,0:T(8,128)}, u32[]{:S(2)}) copy-start(f32[256,640]{1,0:T(8,128)} %copy-done.3) | copy-start | bytes 1966084
  151.2 4.6 %copy-start.7 = (bf16[256,640]{1,0:T(8,128)(2,1)S(1)}, bf16[256,640]{1,0:T(8,128)(2,1)}, u32[]{:S(2)}) copy-start(bf16[256,640]{1,0:T(8,128)(2,1)} %copy-done.6) | copy-start | bytes 983044
  151.2 5.7 %collective-permute-start.8 = (bf16[3072,128]{1,0:T(8,128)(2,1)S(1)}, bf16[3072,128]{1,0:T(8,128)(2,1)S(1)}, u32[]{:S(2)}, u32[]{:S(2)}) collective-permute-start(bf16[3072,128]{1,0:T(8,128)(2,1)S(1)} %bitcast.9), channel_id=1, source_target_pairs={{0,1},{1,0},{2,3},{3,2},{4,5},{5,4},{6,7},{7,6},{8,9},{9,8},{10,11... | collective-permute-start | bytes 2359304 | tf_op jit(solution)/shard_map/ppermute | solution.py:262

commit v3 on v2

--- a/solution.py
+++ b/solution.py
@@ -14,6 +14,7 @@
 LANES = 128
 EPS = 1e-06
 CHUNK = 64
+LONG = 10**11
 
 BF = jnp.bfloat16
 F32 = jnp.float32
@@ -177,6 +178,14 @@
     loss_ref[0, 0] = jnp.sum(terms)
 
 
+def relay_kernel(far_ref, part_ref, out_ref):
+    out_ref[...] = (far_ref[...].astype(F32) + part_ref[...]).astype(BF)
+
+
+def second_kernel(pair_ref, out_ref):
+    out_ref[...] = pair_ref[ROWS:, :]
+
+
 def text_kernel(own_ref, far_ref, near_ref, text_ref, out_ref):
     dzt = own_ref[...] + far_ref[0:ROWS, :].astype(F32) + near_ref[...].astype(F32)
     text = text_ref[...].astype(F32)
@@ -200,7 +209,6 @@
     x_other = lax.ppermute(image_feats, axes, across)
     texts0 = jnp.concatenate([text_embeds, text_other])
     texts1 = lax.ppermute(texts0, axes, onward)
-    texts2 = lax.ppermute(texts1, axes, onward)
 
     zi, zib, inv_u, x_half = call(
         project_kernel,
@@ -220,6 +228,8 @@
 
     both = 2 * ROWS
     dzi, dzt0, loss0 = score([(0, both, True)], scal, zib, text_embeds, None, F32)
+    texts1, dzi = lax.optimization_barrier((texts1, dzi))
+    texts2 = lax.ppermute(texts1, axes, onward)
     dzi, dzt1, loss1 = score([(0, both, False), (1, both, False)], scal, zib, texts1, dzi, F32)
     dzi, dzt2, loss2 = score([(1, both, False), (0, ROWS, False)], scal, zib, texts2, dzi, BF)
     dzi_sent = lax.ppermute(dzi, axes, across)
@@ -240,10 +250,17 @@
         bytes_accessed=7 << 20,
     )(dzi, dzi_sent, zi, inv_u, x_half, loss0, loss1, loss2)
 
-    near = (far.astype(F32) + dzt1).astype(BF)
-
     share = flat_rows // chips
     pieces = lax.all_to_all(flat.reshape(chips, share // 2, 2, LANES), "chip", 0, 0)
+    near = call(
+        relay_kernel, jax.ShapeDtypeStruct((both, E), BF), 0, 2, VMEM, flops=LONG, bytes_accessed=3 << 20
+    )(far, dzt1)
+    pieces, near = lax.optimization_barrier((pieces, near))
+    near = lax.ppermute(near, axes, back)
+    theirs = call(
+        second_kernel, jax.ShapeDtypeStruct((ROWS, E), BF), 0, 1, VMEM, flops=LONG, bytes_accessed=1 << 20
+    )(near)
+    near_other = lax.ppermute(theirs, axes, across)
     spread = call(
         functools.partial(reduce_kernel, share),
         jax.ShapeDtypeStruct((flat_rows, LANES), BF),
@@ -254,17 +271,13 @@
         flops=flat_rows * LANES,
         bytes_accessed=2 << 20,
     )(chip_id, pieces.reshape(flat_rows, LANES)).reshape(chips, share // 2, 2, LANES)
-    spread, near = lax.optimization_barrier((spread, near))
-    near = lax.ppermute(near, axes, back)
     half = lax.all_to_all(spread, "chip", 0, 0).reshape(flat_rows, LANES)
-    near_other = lax.ppermute(near[ROWS:], axes, across)
-    half, near_other = lax.optimization_barrier((half, near_other))
-    half_other = lax.ppermute(half, axes, across)
-
-    image_grad = lax.dot_general(du, head_weight, (((1,), (1,)), ((), ())), preferred_element_type=F32).astype(BF)
     text_grad = call(
         text_kernel, jax.ShapeDtypeStruct((ROWS, E), BF), 0, 4, VMEM, flops=10 * ROWS * E, bytes_accessed=3 << 20
     )(dzt0, near, near_other, text_embeds)
+    image_grad = lax.dot_general(du, head_weight, (((1,), (1,)), ((), ())), preferred_element_type=F32).astype(BF)
+    half, text_grad = lax.optimization_barrier((half, text_grad))
+    half_other = lax.ppermute(half, axes, across)
 
     head_grad, loss = call(
         assemble_kernel,

time: 161 us -> 148 us (0.919)
  waiting for transfers between devices: 67.6 us -> 46.4 us
  starting transfers between devices: 62.4 us -> 72.1 us
    ppermute x1, waiting for transfers between devices: 28.1 us -> 0.01 us  [per_device(): near = lax.ppermute(near, axes, back)]
    ppermute x1, waiting for transfers between devices: 28.1 us -> 0.01 us  [per_device(): far = lax.ppermute(dzt2, axes, back)]
    all_to_all x1, waiting for transfers between devices: 0.01 us -> 21 us  [per_device(): lax.all_to_all(flat.reshape(chips, share // 2, 2, LANES), 'chip', 0, 0)]
    all_to_all x1, waiting for transfers between devices: 0.01 us -> 18.1 us  [per_device(): half = lax.all_to_all(spread, 'chip', 0, 0).reshape(flat_rows, LANES)]
    ppermute x1, waiting for transfers between devices: 5.57 us -> 1.68 us  [per_device(): texts1 = lax.ppermute(texts0, axes, onward)]
    ppermute x1, waiting for transfers between devices: 0.01 us -> 3.34 us  [per_device(): texts2 = lax.ppermute(texts1, axes, onward)]
    all_to_all x1, starting transfers between devices: 10.8 us -> 14.1 us  [per_device(): half = lax.all_to_all(spread, 'chip', 0, 0).reshape(flat_rows, LANES)]
    ppermute x1, starting transfers between devices: 2.18 us -> 4.88 us  [per_device(): dzi_sent = lax.ppermute(dzi, axes, across)]
  transfers between devices with their start and end apart: 11 -> 11, of which waited for: 6 -> 7; matrix products, arithmetic and copies ran while one was open for 3% -> 2% of each run, Pallas kernels for 5% -> 8%
where the time goes in v3:
time: 148 us
  starting transfers between devices  72.1 us (49%)
  waiting for transfers between devices  46.4 us (31%)
  Pallas kernels  15.1 us (10%)
  local copies, waits for them, and re-layouts  6.54 us (4%)
  between operations  3.97 us (3%)
  other arithmetic  1.94 us (1%)
  matrix products  1.48 us (1%)
    all_to_all x1, waiting for transfers between devices, per_device(): lax.all_to_all(flat.reshape(chips, share // 2, 2, LANES), 'chip', 0, 0)  21 us
    all_to_all x1, waiting for transfers between devices, per_device(): half = lax.all_to_all(spread, 'chip', 0, 0).reshape(flat_rows, LANES)  18.1 us
    all_to_all x1, starting transfers between devices, per_device(): half = lax.all_to_all(spread, 'chip', 0, 0).reshape(flat_rows, LANES)  14.1 us
    all_to_all x1, starting transfers between devices, per_device(): lax.all_to_all(flat.reshape(chips, share // 2, 2, LANES), 'chip', 0, 0)  12.4 us
    ppermute x1, starting transfers between devices, per_device(): texts1 = lax.ppermute(texts0, axes, onward)  10.4 us
    ppermute x1, starting transfers between devices, per_device(): texts2 = lax.ppermute(texts1, axes, onward)  9.13 us
    ppermute x1, starting transfers between devices, per_device(): text_other = lax.ppermute(text_embeds, axes, across)  8.92 us
    pallas_call x3, Pallas kernels, score(): call(functools.partial(score_kernel, parts, dzi is not None), (jax.ShapeD...  7.62 us
  transfers between devices with their start and end apart: 11, of which 7 were waited for; matrix products, arithmetic and copies ran while one was open for 2% of the time, Pallas kernels for 8%

profile of v3, /device:TPU:1, one launch (start us, length us, event | category | flops | bytes accessed | tf_op | source)
XLA Modules:
  0.0 147.6 jit_solution(15835747950583099164)
XLA Ops:
  0.6 0.0 copy-start.7
  0.6 8.9 %collective-permute-start.1 = (bf16[256,640]{1,0:T(8,128)(2,1)}, bf16[256,640]{1,0:T(8,128)(2,1)S(1)}, u32[]{:S(2)}, u32[]{:S(2)}) collective-permute-start(bf16[256,640]{1,0:T(8,128)(2,1)} %text_ref.3), channel_id=1, source_target_pairs={{0,1},{1,0},{2,3},{3,2},{4,5},{5,4},{6,7},{7,6},{8,9},{9,8},{10,11... | collective-permute-start | bytes 983048 | tf_op jit(solution)/shard_map/ppermute | solution.py:208
  9.6 1.9 %collective-permute-start = (bf16[256,1152]{1,0:T(8,128)(2,1)}, bf16[256,1152]{1,0:T(8,128)(2,1)S(1)}, u32[]{:S(2)}, u32[]{:S(2)}) collective-permute-start(bf16[256,1152]{1,0:T(8,128)(2,1)} %own_ref.1), channel_id=1, source_target_pairs={{0,1},{1,0},{2,3},{3,2},{4,5},{5,4},{6,7},{7,6},{8,9},{9,8},{10,11... | collective-permute-start | bytes 1769480 | tf_op jit(solution)/shard_map/ppermute | solution.py:209
  11.5 0.0 collective-permute-done.1
  11.5 1.9 %pad_maximum_fusion = bf16[512,640]{1,0:T(8,128)(2,1)} fusion(bf16[256,640]{1,0:T(8,128)(2,1)S(1)} %collective-permute-done.1, bf16[256,640]{1,0:T(8,128)(2,1)} %text_ref.3), kind=kLoop, calls=%fused_computation.1 | loop fusion | flops 1310720 | bytes 1310720 | tf_op jit(solution)/shard_map/concatenate | solution.py:210
  13.4 10.4 %collective-permute-start.2 = (bf16[512,640]{1,0:T(8,128)(2,1)}, bf16[512,640]{1,0:T(8,128)(2,1)S(1)}, u32[]{:S(2)}, u32[]{:S(2)}) collective-permute-start(bf16[512,640]{1,0:T(8,128)(2,1)} %pad_maximum_fusion), channel_id=1, source_target_pairs={{0,2},{1,511},{2,4},{3,1},{4,6},{5,3},{6,8},{7,5},{8,10},{9,7},{10... | collective-permute-start | bytes 1966088 | tf_op jit(solution)/shard_map/ppermute | solution.py:211
  25.1 0.1 pad_maximum_fusion.1.scal_ref
  25.1 0.0 collective-permute-done.other_ref
  25.1 0.0 copy-done.7
  25.1 0.0 copy-start
  25.1 1.4 copy-done
  26.5 0.0 copy-start.2
  26.5 1.4 shard_map.84
  27.9 0.0 copy-done.2
  27.9 2.0 %shard_map.85 = (f32[512,640]{1,0:T(8,128)S(1)}, f32[256,640]{1,0:T(8,128)S(1)}, f32[8,256]{1,0:T(8,128)S(1)}) custom-call(f32[2]{0:T(128)S(1)} %pad_maximum_fusion.1.scal_ref, bf16[512,640]{1,0:T(8,128)(2,1)S(1)} %get-tuple-element.27.zib_ref, bf16[256,640]{1,0:T(8,128)(2,1)S(1)} %copy-done.2), custom_call_target="tpu_custom_call" | custom-call | flops 503316480 | bytes 4194304 | tf_op jit(solution)/shard_map/pallas_call | solution.py:102
  29.9 1.7 %collective-permute-done.2.text_ref = bf16[512,640]{1,0:T(8,128)(2,1)S(1)} collective-permute-done((bf16[512,640]{1,0:T(8,128)(2,1)}, bf16[512,640]{1,0:T(8,128)(2,1)S(1)}, u32[]{:S(2)}, u32[]{:S(2)}) %collective-permute-start.2) | collective-permute-done | bytes 655392 | tf_op jit(solution)/shard_map/ppermute | solution.py:211
  31.6 9.1 %collective-permute-start.3 = (bf16[512,640]{1,0:T(8,128)(2,1)S(1)}, bf16[512,640]{1,0:T(8,128)(2,1)S(1)}, u32[]{:S(2)}, u32[]{:S(2)}) collective-permute-start(bf16[512,640]{1,0:T(8,128)(2,1)S(1)} %collective-permute-done.2.text_ref), channel_id=1, source_target_pairs={{0,2},{1,511},{2,4},{3,1},{4,6},{5,3},{6,8},{7,5},{8,10},{9,7},{10... | collective-permute-start | bytes 1966088 | tf_op jit(solution)/shard_map/ppermute | solution.py:232
  40.7 3.1 %shard_map.86 = (f32[512,640]{1,0:T(8,128)S(1)}, f32[512,640]{1,0:T(8,128)S(1)}, f32[8,256]{1,0:T(8,128)S(1)}) custom-call(f32[2]{0:T(128)S(1)} %pad_maximum_fusion.1.scal_ref, bf16[512,640]{1,0:T(8,128)(2,1)S(1)} %get-tuple-element.27.zib_ref, bf16[512,640]{1,0:T(8,128)(2,1)S(1)} %collective-permute-done.2.text_ref, f32[512,640]{1,0:T(8,128)S(1)} %get-tuple-element.30.refs_0_), custom_call_target="tpu_custom_call" | custom-call | flops 1006632960 | bytes 4194304 | tf_op jit(solution)/shard_map/pallas_call | solution.py:102
  43.8 0.0 copy-start.8
  43.8 1.0 copy-done.8
  44.9 3.3 %collective-permute-done.3.text_ref = bf16[512,640]{1,0:T(8,128)(2,1)S(1)} collective-permute-done((bf16[512,640]{1,0:T(8,128)(2,1)S(1)}, bf16[512,640]{1,0:T(8,128)(2,1)S(1)}, u32[]{:S(2)}, u32[]{:S(2)}) %collective-permute-start.3) | collective-permute-done | bytes 655392 | tf_op jit(solution)/shard_map/ppermute | solution.py:232
  48.2 2.5 %shard_map.87 = (f32[512,640]{1,0:T(8,128)S(1)}, bf16[512,640]{1,0:T(8,128)(2,1)S(1)}, f32[8,256]{1,0:T(8,128)S(1)}) custom-call(f32[2]{0:T(128)S(1)} %pad_maximum_fusion.1.scal_ref, bf16[512,640]{1,0:T(8,128)(2,1)S(1)} %get-tuple-element.27.zib_ref, bf16[512,640]{1,0:T(8,128)(2,1)S(1)} %collective-permute-done.3.text_ref, ...), custom_call_target="tpu_custom_call" | custom-call | flops 754974720 | bytes 4194304 | tf_op jit(solution)/shard_map/pallas_call | solution.py:102
  50.8 4.9 %collective-permute-start.4 = (f32[512,640]{1,0:T(8,128)S(1)}, f32[512,640]{1,0:T(8,128)S(1)}, u32[]{:S(2)}, u32[]{:S(2)}) collective-permute-start(f32[512,640]{1,0:T(8,128)S(1)} %get-tuple-element.32.dzi_ref), channel_id=1, source_target_pairs={{0,1},{1,0},{2,3},{3,2},{4,5},{5,4},{6,7},{7,6},{8,9},{9,8},{10,11... | collective-permute-start | bytes 3932168 | tf_op jit(solution)/shard_map/ppermute | solution.py:235
  55.7 1.9 %collective-permute-start.5 = (bf16[512,640]{1,0:T(8,128)(2,1)S(1)}, bf16[512,640]{1,0:T(8,128)(2,1)S(1)}, u32[]{:S(2)}, u32[]{:S(2)}) collective-permute-start(bf16[512,640]{1,0:T(8,128)(2,1)S(1)} %get-tuple-element.40), channel_id=1, source_target_pairs={{2,0},{511,1},{4,2},{1,3},{6,4},{3,5},{8,6},{5,7},{10,8},{7,9},{12... | collective-permute-start | bytes 1966088 | tf_op jit(solution)/shard_map/ppermute | solution.py:236
  57.6 0.7 collective-permute-done.4.sent_ref
  58.3 2.3 %shard_map.88 = (bf16[256,640]{1,0:T(8,128)(2,1)S(1)}, bf16[3072,128]{1,0:T(8,128)(2,1)}) custom-call(f32[512,640]{1,0:T(8,128)S(1)} %get-tuple-element.32.dzi_ref, f32[512,640]{1,0:T(8,128)S(1)} %collective-permute-done.4.sent_ref, f32[512,640]{1,0:T(8,128)S(1)} %get-tuple-element.33.zi_ref, f32[512,128]{1,0:T(8,128)S(1)} %get-tuple-element.34.inv_ref, ...), custom_call_target="tpu_custom_call" | custom-call | flops 377487360 | bytes 7340032 | tf_op jit(solution)/shard_map/pallas_call | solution.py:239
  60.7 12.4 %all-to-all-start = ((bf16[256,6,2,128]{3,2,1,0:T(2,128)(2,1)}), bf16[256,6,2,128]{3,2,1,0:T(2,128)(2,1)S(1)}, u32[]{:S(2)}, u32[]{:S(2)}) async-start(bf16[256,6,2,128]{3,2,1,0:T(2,128)(2,1)} %bitcast.2), calls=%async_computation | async-start | bytes 1572864 | tf_op jit(solution)/shard_map/all_to_all | solution.py:254
  73.0 0.0 collective-permute-done.5.far_ref
  73.1 0.0 copy-start.9
  73.1 1.3 copy-done.9
  74.4 0.1 shard_map.89
  74.5 0.0 copy-start.6
  74.5 0.9 copy-done.6
  75.4 21.0 %all-to-all-done = bf16[256,6,2,128]{3,2,1,0:T(2,128)(2,1)S(1)} async-done(((bf16[256,6,2,128]{3,2,1,0:T(2,128)(2,1)}), bf16[256,6,2,128]{3,2,1,0:T(2,128)(2,1)S(1)}, u32[]{:S(2)}, u32[]{:S(2)}) %all-to-all-start) | async-done | bytes 786464 | tf_op jit(solution)/shard_map/all_to_all | solution.py:254
  96.3 2.2 %collective-permute-start.6 = (bf16[512,640]{1,0:T(8,128)(2,1)}, bf16[512,640]{1,0:T(8,128)(2,1)S(1)}, u32[]{:S(2)}, u32[]{:S(2)}) collective-permute-start(bf16[512,640]{1,0:T(8,128)(2,1)} %copy-done.6), channel_id=1, source_target_pairs={{2,0},{511,1},{4,2},{1,3},{6,4},{3,5},{8,6},{5,7},{10,8},{7,9},{12... | collective-permute-start | bytes 1966088 | tf_op jit(solution)/shard_map/ppermute | solution.py:259
  98.6 1.2 shard_map.90
  99.8 14.1 %all-to-all-start.1 = ((bf16[256,6,2,128]{3,2,1,0:T(2,128)(2,1)}), bf16[256,6,2,128]{3,2,1,0:T(2,128)(2,1)S(1)}, u32[]{:S(2)}, u32[]{:S(2)}) async-start(bf16[256,6,2,128]{3,2,1,0:T(2,128)(2,1)} %bitcast.4), calls=%async_computation.1 | async-start | bytes 1572864 | tf_op jit(solution)/shard_map/all_to_all | solution.py:274
  113.9 0.0 copy-start.3
  113.9 0.0 collective-permute-done.6.pair_ref.far_ref
  113.9 0.0 copy-start.4
  113.9 0.8 copy-done.4
  114.8 0.0 copy-start.1
  114.8 2.7 %collective-permute-start.7 = (bf16[256,640]{1,0:T(8,128)(2,1)S(1)}, bf16[256,640]{1,0:T(8,128)(2,1)S(1)}, u32[]{:S(2)}, u32[]{:S(2)}) collective-permute-start(bf16[256,640]{1,0:T(8,128)(2,1)S(1)} %shard_map.91), channel_id=1, source_target_pairs={{0,1},{1,0},{2,3},{3,2},{4,5},{5,4},{6,7},{7,6},{8,9},{9,8},{10,11... | collective-permute-start | bytes 983048 | tf_op jit(solution)/shard_map/ppermute | solution.py:263
  117.5 1.2 collective-permute-done.7.near_ref
  118.7 0.0 copy-done.3
  118.7 0.0 copy-start.5
  118.7 1.1 copy-done.5
  119.8 1.0 shard_map.92
  120.8 18.1 %all-to-all-done.1 = bf16[256,6,2,128]{3,2,1,0:T(2,128)(2,1)S(1)} async-done(((bf16[256,6,2,128]{3,2,1,0:T(2,128)(2,1)}), bf16[256,6,2,128]{3,2,1,0:T(2,128)(2,1)S(1)}, u32[]{:S(2)}, u32[]{:S(2)}) %all-to-all-start.1) | async-done | bytes 786464 | tf_op jit(solution)/shard_map/all_to_all | solution.py:274
  138.9 3.6 %collective-permute-start.8 = (bf16[3072,128]{1,0:T(8,128)(2,1)S(1)}, bf16[3072,128]{1,0:T(8,128)(2,1)S(1)}, u32[]{:S(2)}, u32[]{:S(2)}) collective-permute-start(bf16[3072,128]{1,0:T(8,128)(2,1)S(1)} %bitcast.9), channel_id=1, source_target_pairs={{0,1},{1,0},{2,3},{3,2},{4,5},{5,4},{6,7},{7,6},{8,9},{9,8},{10,11... | collective-permute-start | bytes 2359304 | tf_op jit(solution)/shard_map/ppermute | solution.py:280
  142.5 0.0 copy-done.1
  142.5 1.5 %convolution_convert_fusion = bf16[256,1152]{1,0:T(8,128)(2,1)} fusion(bf16[256,640]{1,0:T(8,128)(2,1)S(1)} %get-tuple-element.47, bf16[1152,640]{1,0:T(8,128)(2,1)S(1)} %copy-done.1), kind=kOutput, calls=%fused_computation | convolution fusion | flops 377782272 | bytes 2392064 | tf_op jit(solution)/shard_map/dot_general | solution.py:278
  144.0 0.4 collective-permute-done.8.other_ref
  144.4 1.4 shard_map.93
  (1 shorter events, 0.0 us)
Async XLA Ops:
  0.6 24.5 %copy-start.7 = (bf16[256,1152]{1,0:T(8,128)(2,1)S(1)}, bf16[256,1152]{1,0:T(8,128)(2,1)}, u32[]{:S(2)}) copy-start(bf16[256,1152]{1,0:T(8,128)(2,1)} %own_ref.1) | copy-start | bytes 1769476
  0.6 10.9 %collective-permute-start.1 = (bf16[256,640]{1,0:T(8,128)(2,1)}, bf16[256,640]{1,0:T(8,128)(2,1)S(1)}, u32[]{:S(2)}, u32[]{:S(2)}) collective-permute-start(bf16[256,640]{1,0:T(8,128)(2,1)} %text_ref.3), channel_id=1, source_target_pairs={{0,1},{1,0},{2,3},{3,2},{4,5},{5,4},{6,7},{7,6},{8,9},{9,8},{10,11... | collective-permute-start | bytes 983048 | tf_op jit(solution)/shard_map/ppermute | solution.py:208
  9.6 15.6 %collective-permute-start = (bf16[256,1152]{1,0:T(8,128)(2,1)}, bf16[256,1152]{1,0:T(8,128)(2,1)S(1)}, u32[]{:S(2)}, u32[]{:S(2)}) collective-permute-start(bf16[256,1152]{1,0:T(8,128)(2,1)} %own_ref.1), channel_id=1, source_target_pairs={{0,1},{1,0},{2,3},{3,2},{4,5},{5,4},{6,7},{7,6},{8,9},{9,8},{10,11... | collective-permute-start | bytes 1769480 | tf_op jit(solution)/shard_map/ppermute | solution.py:209
  13.4 18.2 %collective-permute-start.2 = (bf16[512,640]{1,0:T(8,128)(2,1)}, bf16[512,640]{1,0:T(8,128)(2,1)S(1)}, u32[]{:S(2)}, u32[]{:S(2)}) collective-permute-start(bf16[512,640]{1,0:T(8,128)(2,1)} %pad_maximum_fusion), channel_id=1, source_target_pairs={{0,2},{1,511},{2,4},{3,1},{4,6},{5,3},{6,8},{7,5},{8,10},{9,7},{10... | collective-permute-start | bytes 1966088 | tf_op jit(solution)/shard_map/ppermute | solution.py:211
  25.1 1.4 copy-start
  26.5 1.4 copy-start.2
  31.6 16.6 %collective-permute-start.3 = (bf16[512,640]{1,0:T(8,128)(2,1)S(1)}, bf16[512,640]{1,0:T(8,128)(2,1)S(1)}, u32[]{:S(2)}, u32[]{:S(2)}) collective-permute-start(bf16[512,640]{1,0:T(8,128)(2,1)S(1)} %collective-permute-done.2.text_ref), channel_id=1, source_target_pairs={{0,2},{1,511},{2,4},{3,1},{4,6},{5,3},{6,8},{7,5},{8,10},{9,7},{10... | collective-permute-start | bytes 1966088 | tf_op jit(solution)/shard_map/ppermute | solution.py:232
  43.8 1.1 copy-start.8
  50.8 7.5 %collective-permute-start.4 = (f32[512,640]{1,0:T(8,128)S(1)}, f32[512,640]{1,0:T(8,128)S(1)}, u32[]{:S(2)}, u32[]{:S(2)}) collective-permute-start(f32[512,640]{1,0:T(8,128)S(1)} %get-tuple-element.32.dzi_ref), channel_id=1, source_target_pairs={{0,1},{1,0},{2,3},{3,2},{4,5},{5,4},{6,7},{7,6},{8,9},{9,8},{10,11... | collective-permute-start | bytes 3932168 | tf_op jit(solution)/shard_map/ppermute | solution.py:235
  55.7 17.4 %collective-permute-start.5 = (bf16[512,640]{1,0:T(8,128)(2,1)S(1)}, bf16[512,640]{1,0:T(8,128)(2,1)S(1)}, u32[]{:S(2)}, u32[]{:S(2)}) collective-permute-start(bf16[512,640]{1,0:T(8,128)(2,1)S(1)} %get-tuple-element.40), channel_id=1, source_target_pairs={{2,0},{511,1},{4,2},{1,3},{6,4},{3,5},{8,6},{5,7},{10,8},{7,9},{12... | collective-permute-start | bytes 1966088 | tf_op jit(solution)/shard_map/ppermute | solution.py:236
  60.7 35.7 %all-to-all-start = ((bf16[256,6,2,128]{3,2,1,0:T(2,128)(2,1)}), bf16[256,6,2,128]{3,2,1,0:T(2,128)(2,1)S(1)}, u32[]{:S(2)}, u32[]{:S(2)}) async-start(bf16[256,6,2,128]{3,2,1,0:T(2,128)(2,1)} %bitcast.2), calls=%async_computation | async-start | bytes 1572864 | tf_op jit(solution)/shard_map/all_to_all | solution.py:254
  73.1 1.3 copy-start.9
  74.5 0.9 copy-start.6
  96.3 17.5 %collective-permute-start.6 = (bf16[512,640]{1,0:T(8,128)(2,1)}, bf16[512,640]{1,0:T(8,128)(2,1)S(1)}, u32[]{:S(2)}, u32[]{:S(2)}) collective-permute-start(bf16[512,640]{1,0:T(8,128)(2,1)} %copy-done.6), channel_id=1, source_target_pairs={{2,0},{511,1},{4,2},{1,3},{6,4},{3,5},{8,6},{5,7},{10,8},{7,9},{12... | collective-permute-start | bytes 1966088 | tf_op jit(solution)/shard_map/ppermute | solution.py:259
  99.8 39.2 %all-to-all-start.1 = ((bf16[256,6,2,128]{3,2,1,0:T(2,128)(2,1)}), bf16[256,6,2,128]{3,2,1,0:T(2,128)(2,1)S(1)}, u32[]{:S(2)}, u32[]{:S(2)}) async-start(bf16[256,6,2,128]{3,2,1,0:T(2,128)(2,1)} %bitcast.4), calls=%async_computation.1 | async-start | bytes 1572864 | tf_op jit(solution)/shard_map/all_to_all | solution.py:274
  113.9 4.9 %copy-start.3 = (bf16[256,640]{1,0:T(8,128)(2,1)S(1)}, bf16[256,640]{1,0:T(8,128)(2,1)}, u32[]{:S(2)}) copy-start(bf16[256,640]{1,0:T(8,128)(2,1)} %text_ref.3) | copy-start | bytes 983044
  113.9 0.8 copy-start.4
  114.8 27.7 %copy-start.1 = (bf16[1152,640]{1,0:T(8,128)(2,1)S(1)}, bf16[1152,640]{1,0:T(8,128)(2,1)}, u32[]{:S(2)}) copy-start(bf16[1152,640]{1,0:T(8,128)(2,1)} %weight_ref.1) | copy-start | bytes 4423684
  114.8 4.0 %collective-permute-start.7 = (bf16[256,640]{1,0:T(8,128)(2,1)S(1)}, bf16[256,640]{1,0:T(8,128)(2,1)S(1)}, u32[]{:S(2)}, u32[]{:S(2)}) collective-permute-start(bf16[256,640]{1,0:T(8,128)(2,1)S(1)} %shard_map.91), channel_id=1, source_target_pairs={{0,1},{1,0},{2,3},{3,2},{4,5},{5,4},{6,7},{7,6},{8,9},{9,8},{10,11... | collective-permute-start | bytes 983048 | tf_op jit(solution)/shard_map/ppermute | solution.py:263
  118.7 1.1 copy-start.5
  138.9 5.5 %collective-permute-start.8 = (bf16[3072,128]{1,0:T(8,128)(2,1)S(1)}, bf16[3072,128]{1,0:T(8,128)(2,1)S(1)}, u32[]{:S(2)}, u32[]{:S(2)}) collective-permute-start(bf16[3072,128]{1,0:T(8,128)(2,1)S(1)} %bitcast.9), channel_id=1, source_target_pairs={{0,1},{1,0},{2,3},{3,2},{4,5},{5,4},{6,7},{7,6},{8,9},{9,8},{10,11... | collective-permute-start | bytes 2359304 | tf_op jit(solution)/shard_map/ppermute | solution.py:280

commit v4 on v3

--- a/solution.py
+++ b/solution.py
@@ -56,12 +56,13 @@
     scale = scal_ref[0]
     bias = scal_ref[1]
     loss = jnp.zeros((8, ROWS), F32)
-    for order, (q, n, diag) in enumerate(parts):
+    for order, (q, lo, hi, diag) in enumerate(parts):
+        n = hi - lo
         cols = pl.ds(q * ROWS, ROWS)
         text = text_ref[cols, :].astype(F32)
         inv = lax.rsqrt(jnp.sum(text * text, axis=1, keepdims=True) + EPS)
         ztb = (text * inv).astype(BF)
-        zib = zib_ref[0:n, :]
+        zib = zib_ref[lo:hi, :]
         s_ref[0:n, :] = lax.dot_general(zib, ztb, (((1,), (1,)), ((), ())), preferred_element_type=F32)
         for start in range(0, n, CHUNK):
             v = scale * s_ref[start : start + CHUNK, :] + bias
@@ -86,7 +87,7 @@
         coef = c_ref[0:n, :]
         dzi = scale * jnp.dot(coef, ztb, preferred_element_type=F32)
         if order:
-            dzi_ref[0:n, :] += dzi
+            dzi_ref[lo:hi, :] += dzi
         elif has_dzi:
             dzi_ref[...] = dzi_in[...] + dzi
         else:
@@ -110,7 +111,7 @@
         len(args) - 1,
         (VMEM, VMEM, VMEM),
         scratch=(pltpu.VMEM((2 * ROWS, ROWS), F32), pltpu.VMEM((2 * ROWS, ROWS), BF)),
-        flops=sum(6 * n * ROWS * E for _, n, _ in parts),
+        flops=sum(6 * (hi - lo) * ROWS * E for _, lo, hi, _ in parts),
         bytes_accessed=4 << 20,
     )(*args)
 
@@ -201,7 +202,8 @@
     core_id = core.astype(jnp.int32).reshape(1)
     chip_id = lax.axis_index("chip").astype(jnp.int32).reshape(1)
     across = [(i, i ^ 1) for i in range(2 * chips)]
-    onward = [(2 * k + b, 2 * ((k + 1 - 2 * b) % chips) + b) for k in range(chips) for b in range(2)]
+    onward = [(2 * k + b, 2 * ((k + 2 * b - 1) % chips) + b) for k in range(chips) for b in range(2)]
+    beyond = [(2 * k + b, 2 * ((k + 4 * b - 2) % chips) + b) for k in range(chips) for b in range(2)]
     back = [(d, s) for s, d in onward]
     scal = jnp.concatenate([logit_scale, logit_bias])
 
@@ -209,6 +211,7 @@
     x_other = lax.ppermute(image_feats, axes, across)
     texts0 = jnp.concatenate([text_embeds, text_other])
     texts1 = lax.ppermute(texts0, axes, onward)
+    texts2 = lax.ppermute(texts0, axes, beyond)
 
     zi, zib, inv_u, x_half = call(
         project_kernel,
@@ -227,11 +230,9 @@
     )(core_id, image_feats, x_other, head_weight)
 
     both = 2 * ROWS
-    dzi, dzt0, loss0 = score([(0, both, True)], scal, zib, text_embeds, None, F32)
-    texts1, dzi = lax.optimization_barrier((texts1, dzi))
-    texts2 = lax.ppermute(texts1, axes, onward)
-    dzi, dzt1, loss1 = score([(0, both, False), (1, both, False)], scal, zib, texts1, dzi, F32)
-    dzi, dzt2, loss2 = score([(1, both, False), (0, ROWS, False)], scal, zib, texts2, dzi, BF)
+    dzi, dzt0, loss0 = score([(0, 0, both, True)], scal, zib, text_embeds, None, F32)
+    dzi, dzt1, loss1 = score([(0, 0, both, False), (1, 0, both, False)], scal, zib, texts1, dzi, F32)
+    dzi, dzt2, loss2 = score([(0, 0, both, False), (1, ROWS, both, False)], scal, zib, texts2, dzi, BF)
     dzi_sent = lax.ppermute(dzi, axes, across)
     far = lax.ppermute(dzt2, axes, back)
 

time: 148 us -> 144 us (0.973)
  other arithmetic: 1.94 us -> 0.08 us
    all_to_all x1, waiting for transfers between devices: 18.1 us -> 7 us  [per_device(): half = lax.all_to_all(spread, 'chip', 0, 0).reshape(flat_rows, LANES)]
    ppermute x1, waiting for transfers between devices: 1.68 us -> 11.5 us  [per_device(): texts1 = lax.ppermute(texts0, axes, onward)]
    ppermute x1, starting transfers between devices: 10.4 us -> 1.92 us  [per_device(): texts1 = lax.ppermute(texts0, axes, onward)]
    ppermute x1, starting transfers between devices: 9.13 us -> 2.52 us  [per_device(): texts2 = lax.ppermute(texts0, axes, beyond)]
    ppermute x1, starting transfers between devices: 2.71 us -> 8.8 us  [per_device(): near_other = lax.ppermute(theirs, axes, across)]
    ppermute x1, starting transfers between devices: 3.55 us -> 8.59 us  [per_device(): half_other = lax.ppermute(half, axes, across)]
    ppermute x1, starting transfers between devices: 1.92 us -> 6.53 us  [per_device(): far = lax.ppermute(dzt2, axes, back)]
    all_to_all x1, starting transfers between devices: 14.1 us -> 9.5 us  [per_device(): half = lax.all_to_all(spread, 'chip', 0, 0).reshape(flat_rows, LANES)]
  transfers between devices with their start and end apart: 11 -> 11, of which waited for: 7 -> 6; matrix products, arithmetic and copies ran while one was open for 2% -> 2% of each run, Pallas kernels for 8% -> 8%
where the time goes in v4:
time: 144 us
  starting transfers between devices  71 us (49%)
  waiting for transfers between devices  45.5 us (32%)
  Pallas kernels  15.8 us (11%)
  local copies, waits for them, and re-layouts  5.68 us (4%)
  between operations  3.97 us (3%)
  matrix products  1.48 us (1%)
    all_to_all x1, waiting for transfers between devices, per_device(): lax.all_to_all(flat.reshape(chips, share // 2, 2, LANES), 'chip', 0, 0)  21.6 us
    all_to_all x1, starting transfers between devices, per_device(): lax.all_to_all(flat.reshape(chips, share // 2, 2, LANES), 'chip', 0, 0)  11.7 us
    ppermute x1, waiting for transfers between devices, per_device(): texts1 = lax.ppermute(texts0, axes, onward)  11.5 us
    all_to_all x1, starting transfers between devices, per_device(): half = lax.all_to_all(spread, 'chip', 0, 0).reshape(flat_rows, LANES)  9.5 us
    ppermute x1, starting transfers between devices, per_device(): text_other = lax.ppermute(text_embeds, axes, across)  8.92 us
    ppermute x1, starting transfers between devices, per_device(): near_other = lax.ppermute(theirs, axes, across)  8.8 us
    ppermute x1, starting transfers between devices, per_device(): half_other = lax.ppermute(half, axes, across)  8.59 us
    pallas_call x3, Pallas kernels, score(): call(functools.partial(score_kernel, parts, dzi is not None), (jax.ShapeD...  7.6 us
  transfers between devices with their start and end apart: 11, of which 6 were waited for; matrix products, arithmetic and copies ran while one was open for 2% of the time, Pallas kernels for 8%

profile of v4, /device:TPU:1, one launch (start us, length us, event | category | flops | bytes accessed | tf_op | source)
XLA Modules:
  0.0 143.5 jit_solution(4599491314662380016)
XLA Ops:
  0.6 0.0 copy-start.6
  0.6 8.9 %collective-permute-start.1 = (bf16[256,640]{1,0:T(8,128)(2,1)}, bf16[256,640]{1,0:T(8,128)(2,1)S(1)}, u32[]{:S(2)}, u32[]{:S(2)}) collective-permute-start(bf16[256,640]{1,0:T(8,128)(2,1)} %text_ref.3), channel_id=1, source_target_pairs={{0,1},{1,0},{2,3},{3,2},{4,5},{5,4},{6,7},{7,6},{8,9},{9,8},{10,11... | collective-permute-start | bytes 983048 | tf_op jit(solution)/shard_map/ppermute | solution.py:210
  9.6 1.9 %collective-permute-start = (bf16[256,1152]{1,0:T(8,128)(2,1)}, bf16[256,1152]{1,0:T(8,128)(2,1)S(1)}, u32[]{:S(2)}, u32[]{:S(2)}) collective-permute-start(bf16[256,1152]{1,0:T(8,128)(2,1)} %own_ref.1), channel_id=1, source_target_pairs={{0,1},{1,0},{2,3},{3,2},{4,5},{5,4},{6,7},{7,6},{8,9},{9,8},{10,11... | collective-permute-start | bytes 1769480 | tf_op jit(solution)/shard_map/ppermute | solution.py:211
  11.5 1.0 constant_dynamic-update-slice_fusion.1
  12.5 0.0 collective-permute-done.1
  12.6 1.9 %collective-permute-start.3 = (bf16[512,640]{1,0:T(8,128)(2,1)S(1)}, bf16[512,640]{1,0:T(8,128)(2,1)S(1)}, u32[]{:S(2)}, u32[]{:S(2)}) collective-permute-start(bf16[512,640]{1,0:T(8,128)(2,1)S(1)} %constant_dynamic-update-slice_fusion), channel_id=1, source_target_pairs={{0,510},{1,3},{2,0},{3,5},{4,2},{5,7},{6,4},{7,9},{8,6},{9,11},{10... | collective-permute-start | bytes 1966088 | tf_op jit(solution)/shard_map/ppermute | solution.py:213
  14.5 2.5 %collective-permute-start.2 = (bf16[512,640]{1,0:T(8,128)(2,1)S(1)}, bf16[512,640]{1,0:T(8,128)(2,1)S(1)}, u32[]{:S(2)}, u32[]{:S(2)}) collective-permute-start(bf16[512,640]{1,0:T(8,128)(2,1)S(1)} %constant_dynamic-update-slice_fusion), channel_id=1, source_target_pairs={{0,508},{1,5},{2,510},{3,7},{4,0},{5,9},{6,2},{7,11},{8,4},{9,13},... | collective-permute-start | bytes 1966088 | tf_op jit(solution)/shard_map/ppermute | solution.py:214
  18.3 0.1 pad_maximum_fusion.scal_ref
  18.4 0.0 collective-permute-done.other_ref
  18.4 0.0 copy-done.6
  18.4 0.0 copy-start
  18.4 1.4 copy-done
  19.8 0.0 copy-start.2
  19.8 1.3 shard_map.84
  21.1 0.0 copy-done.2
  21.1 2.0 %shard_map.85 = (f32[512,640]{1,0:T(8,128)S(1)}, f32[256,640]{1,0:T(8,128)S(1)}, f32[8,256]{1,0:T(8,128)S(1)}) custom-call(f32[2]{0:T(128)S(1)} %pad_maximum_fusion.scal_ref, bf16[512,640]{1,0:T(8,128)(2,1)S(1)} %get-tuple-element.25.zib_ref, bf16[256,640]{1,0:T(8,128)(2,1)S(1)} %copy-done.2), custom_call_target="tpu_custom_call" | custom-call | flops 503316480 | bytes 4194304 | tf_op jit(solution)/shard_map/pallas_call | solution.py:103
  23.1 11.5 %collective-permute-done.3.text_ref = bf16[512,640]{1,0:T(8,128)(2,1)S(1)} collective-permute-done((bf16[512,640]{1,0:T(8,128)(2,1)S(1)}, bf16[512,640]{1,0:T(8,128)(2,1)S(1)}, u32[]{:S(2)}, u32[]{:S(2)}) %collective-permute-start.3) | collective-permute-done | bytes 655392 | tf_op jit(solution)/shard_map/ppermute | solution.py:213
  34.6 3.1 %shard_map.86 = (f32[512,640]{1,0:T(8,128)S(1)}, f32[512,640]{1,0:T(8,128)S(1)}, f32[8,256]{1,0:T(8,128)S(1)}) custom-call(f32[2]{0:T(128)S(1)} %pad_maximum_fusion.scal_ref, bf16[512,640]{1,0:T(8,128)(2,1)S(1)} %get-tuple-element.25.zib_ref, bf16[512,640]{1,0:T(8,128)(2,1)S(1)} %collective-permute-done.3.text_ref, f32[512,640]{1,0:T(8,128)S(1)} %get-tuple-element.26.refs_0_), custom_call_target="tpu_custom_call" | custom-call | flops 1006632960 | bytes 4194304 | tf_op jit(solution)/shard_map/pallas_call | solution.py:103
  37.6 0.0 copy-start.7
  37.7 3.8 %collective-permute-done.2.text_ref = bf16[512,640]{1,0:T(8,128)(2,1)S(1)} collective-permute-done((bf16[512,640]{1,0:T(8,128)(2,1)S(1)}, bf16[512,640]{1,0:T(8,128)(2,1)S(1)}, u32[]{:S(2)}, u32[]{:S(2)}) %collective-permute-start.2) | collective-permute-done | bytes 655392 | tf_op jit(solution)/shard_map/ppermute | solution.py:214
  41.5 2.6 %shard_map.87 = (f32[512,640]{1,0:T(8,128)S(1)}, bf16[512,640]{1,0:T(8,128)(2,1)S(1)}, f32[8,256]{1,0:T(8,128)S(1)}) custom-call(f32[2]{0:T(128)S(1)} %pad_maximum_fusion.scal_ref, bf16[512,640]{1,0:T(8,128)(2,1)S(1)} %get-tuple-element.25.zib_ref, bf16[512,640]{1,0:T(8,128)(2,1)S(1)} %collective-permute-done.2.text_ref, ...), custom_call_target="tpu_custom_call" | custom-call | flops 754974720 | bytes 4194304 | tf_op jit(solution)/shard_map/pallas_call | solution.py:103
  44.0 0.0 copy-done.7
  44.0 6.3 %collective-permute-start.4 = (f32[512,640]{1,0:T(8,128)S(1)}, f32[512,640]{1,0:T(8,128)S(1)}, u32[]{:S(2)}, u32[]{:S(2)}) collective-permute-start(f32[512,640]{1,0:T(8,128)S(1)} %get-tuple-element.28.dzi_ref), channel_id=1, source_target_pairs={{0,1},{1,0},{2,3},{3,2},{4,5},{5,4},{6,7},{7,6},{8,9},{9,8},{10,11... | collective-permute-start | bytes 3932168 | tf_op jit(solution)/shard_map/ppermute | solution.py:236
  50.3 6.5 %collective-permute-start.5 = (bf16[512,640]{1,0:T(8,128)(2,1)S(1)}, bf16[512,640]{1,0:T(8,128)(2,1)S(1)}, u32[]{:S(2)}, u32[]{:S(2)}) collective-permute-start(bf16[512,640]{1,0:T(8,128)(2,1)S(1)} %get-tuple-element.36), channel_id=1, source_target_pairs={{510,0},{3,1},{0,2},{5,3},{2,4},{7,5},{4,6},{9,7},{6,8},{11,9},{8,... | collective-permute-start | bytes 1966088 | tf_op jit(solution)/shard_map/ppermute | solution.py:237
  56.8 0.0 collective-permute-done.4.sent_ref
  56.9 2.3 %shard_map.88 = (bf16[256,640]{1,0:T(8,128)(2,1)S(1)}, bf16[3072,128]{1,0:T(8,128)(2,1)}) custom-call(f32[512,640]{1,0:T(8,128)S(1)} %get-tuple-element.28.dzi_ref, f32[512,640]{1,0:T(8,128)S(1)} %collective-permute-done.4.sent_ref, f32[512,640]{1,0:T(8,128)S(1)} %get-tuple-element.29.zi_ref, f32[512,128]{1,0:T(8,128)S(1)} %get-tuple-element.30.inv_ref, ...), custom_call_target="tpu_custom_call" | custom-call | flops 377487360 | bytes 7340032 | tf_op jit(solution)/shard_map/pallas_call | solution.py:240
  59.2 11.7 %all-to-all-start = ((bf16[256,6,2,128]{3,2,1,0:T(2,128)(2,1)}), bf16[256,6,2,128]{3,2,1,0:T(2,128)(2,1)S(1)}, u32[]{:S(2)}, u32[]{:S(2)}) async-start(bf16[256,6,2,128]{3,2,1,0:T(2,128)(2,1)} %bitcast.2), calls=%async_computation | async-start | bytes 1572864 | tf_op jit(solution)/shard_map/all_to_all | solution.py:255
  70.9 0.0 collective-permute-done.5.far_ref
  70.9 0.0 copy-start.8
  70.9 1.3 copy-done.8
  72.2 1.0 shard_map.89
  73.2 21.6 %all-to-all-done = bf16[256,6,2,128]{3,2,1,0:T(2,128)(2,1)S(1)} async-done(((bf16[256,6,2,128]{3,2,1,0:T(2,128)(2,1)}), bf16[256,6,2,128]{3,2,1,0:T(2,128)(2,1)S(1)}, u32[]{:S(2)}, u32[]{:S(2)}) %all-to-all-start) | async-done | bytes 786464 | tf_op jit(solution)/shard_map/all_to_all | solution.py:255
  94.8 4.3 %collective-permute-start.6 = (bf16[512,640]{1,0:T(8,128)(2,1)}, bf16[512,640]{1,0:T(8,128)(2,1)S(1)}, u32[]{:S(2)}, u32[]{:S(2)}) collective-permute-start(bf16[512,640]{1,0:T(8,128)(2,1)} %shard_map.89), channel_id=1, source_target_pairs={{510,0},{3,1},{0,2},{5,3},{2,4},{7,5},{4,6},{9,7},{6,8},{11,9},{8,... | collective-permute-start | bytes 1966088 | tf_op jit(solution)/shard_map/ppermute | solution.py:260
  99.1 1.2 shard_map.90
  100.3 9.5 %all-to-all-start.1 = ((bf16[256,6,2,128]{3,2,1,0:T(2,128)(2,1)}), bf16[256,6,2,128]{3,2,1,0:T(2,128)(2,1)S(1)}, u32[]{:S(2)}, u32[]{:S(2)}) async-start(bf16[256,6,2,128]{3,2,1,0:T(2,128)(2,1)} %bitcast.4), calls=%async_computation.1 | async-start | bytes 1572864 | tf_op jit(solution)/shard_map/all_to_all | solution.py:275
  109.8 0.0 copy-start.3
  109.8 0.0 collective-permute-done.6.pair_ref.far_ref
  109.9 0.0 copy-start.4
  109.9 0.8 copy-done.4
  110.7 0.0 copy-start.1
  110.7 8.8 %collective-permute-start.7 = (bf16[256,640]{1,0:T(8,128)(2,1)S(1)}, bf16[256,640]{1,0:T(8,128)(2,1)S(1)}, u32[]{:S(2)}, u32[]{:S(2)}) collective-permute-start(bf16[256,640]{1,0:T(8,128)(2,1)S(1)} %shard_map.91), channel_id=1, source_target_pairs={{0,1},{1,0},{2,3},{3,2},{4,5},{5,4},{6,7},{7,6},{8,9},{9,8},{10,11... | collective-permute-start | bytes 983048 | tf_op jit(solution)/shard_map/ppermute | solution.py:264
  119.5 1.2 collective-permute-done.7.near_ref
  120.7 0.0 copy-done.3
  120.7 0.0 copy-start.5
  120.7 1.1 copy-done.5
  121.8 1.0 shard_map.92
  122.9 7.0 %all-to-all-done.1 = bf16[256,6,2,128]{3,2,1,0:T(2,128)(2,1)S(1)} async-done(((bf16[256,6,2,128]{3,2,1,0:T(2,128)(2,1)}), bf16[256,6,2,128]{3,2,1,0:T(2,128)(2,1)S(1)}, u32[]{:S(2)}, u32[]{:S(2)}) %all-to-all-start.1) | async-done | bytes 786464 | tf_op jit(solution)/shard_map/all_to_all | solution.py:275
  129.9 8.6 %collective-permute-start.8 = (bf16[3072,128]{1,0:T(8,128)(2,1)S(1)}, bf16[3072,128]{1,0:T(8,128)(2,1)S(1)}, u32[]{:S(2)}, u32[]{:S(2)}) collective-permute-start(bf16[3072,128]{1,0:T(8,128)(2,1)S(1)} %bitcast.9), channel_id=1, source_target_pairs={{0,1},{1,0},{2,3},{3,2},{4,5},{5,4},{6,7},{7,6},{8,9},{9,8},{10,11... | collective-permute-start | bytes 2359304 | tf_op jit(solution)/shard_map/ppermute | solution.py:281
  138.5 0.0 copy-done.1
  138.5 1.5 %convolution_convert_fusion = bf16[256,1152]{1,0:T(8,128)(2,1)} fusion(bf16[256,640]{1,0:T(8,128)(2,1)S(1)} %get-tuple-element.43, bf16[1152,640]{1,0:T(8,128)(2,1)S(1)} %copy-done.1), kind=kOutput, calls=%fused_computation | convolution fusion | flops 377782272 | bytes 2392064 | tf_op jit(solution)/shard_map/dot_general | solution.py:279
  139.9 0.4 collective-permute-done.8.other_ref
  140.3 1.4 shard_map.93
  (2 shorter events, 0.1 us)
Async XLA Ops:
  0.6 17.8 %copy-start.6 = (bf16[256,1152]{1,0:T(8,128)(2,1)S(1)}, bf16[256,1152]{1,0:T(8,128)(2,1)}, u32[]{:S(2)}) copy-start(bf16[256,1152]{1,0:T(8,128)(2,1)} %own_ref.1) | copy-start | bytes 1769476
  0.6 11.9 %collective-permute-start.1 = (bf16[256,640]{1,0:T(8,128)(2,1)}, bf16[256,640]{1,0:T(8,128)(2,1)S(1)}, u32[]{:S(2)}, u32[]{:S(2)}) collective-permute-start(bf16[256,640]{1,0:T(8,128)(2,1)} %text_ref.3), channel_id=1, source_target_pairs={{0,1},{1,0},{2,3},{3,2},{4,5},{5,4},{6,7},{7,6},{8,9},{9,8},{10,11... | collective-permute-start | bytes 983048 | tf_op jit(solution)/shard_map/ppermute | solution.py:210
  9.6 8.8 %collective-permute-start = (bf16[256,1152]{1,0:T(8,128)(2,1)}, bf16[256,1152]{1,0:T(8,128)(2,1)S(1)}, u32[]{:S(2)}, u32[]{:S(2)}) collective-permute-start(bf16[256,1152]{1,0:T(8,128)(2,1)} %own_ref.1), channel_id=1, source_target_pairs={{0,1},{1,0},{2,3},{3,2},{4,5},{5,4},{6,7},{7,6},{8,9},{9,8},{10,11... | collective-permute-start | bytes 1769480 | tf_op jit(solution)/shard_map/ppermute | solution.py:211
  12.6 22.0 %collective-permute-start.3 = (bf16[512,640]{1,0:T(8,128)(2,1)S(1)}, bf16[512,640]{1,0:T(8,128)(2,1)S(1)}, u32[]{:S(2)}, u32[]{:S(2)}) collective-permute-start(bf16[512,640]{1,0:T(8,128)(2,1)S(1)} %constant_dynamic-update-slice_fusion), channel_id=1, source_target_pairs={{0,510},{1,3},{2,0},{3,5},{4,2},{5,7},{6,4},{7,9},{8,6},{9,11},{10... | collective-permute-start | bytes 1966088 | tf_op jit(solution)/shard_map/ppermute | solution.py:213
  14.5 27.0 %collective-permute-start.2 = (bf16[512,640]{1,0:T(8,128)(2,1)S(1)}, bf16[512,640]{1,0:T(8,128)(2,1)S(1)}, u32[]{:S(2)}, u32[]{:S(2)}) collective-permute-start(bf16[512,640]{1,0:T(8,128)(2,1)S(1)} %constant_dynamic-update-slice_fusion), channel_id=1, source_target_pairs={{0,508},{1,5},{2,510},{3,7},{4,0},{5,9},{6,2},{7,11},{8,4},{9,13},... | collective-permute-start | bytes 1966088 | tf_op jit(solution)/shard_map/ppermute | solution.py:214
  18.4 1.4 copy-start
  19.8 1.4 copy-start.2
  37.6 6.4 %copy-start.7 = (f32[512,640]{1,0:T(8,128)}, f32[512,640]{1,0:T(8,128)S(1)}, u32[]{:S(2)}) copy-start(f32[512,640]{1,0:T(8,128)S(1)} %get-tuple-element.37.part_ref) | copy-start | bytes 3932164
  44.0 12.8 %collective-permute-start.4 = (f32[512,640]{1,0:T(8,128)S(1)}, f32[512,640]{1,0:T(8,128)S(1)}, u32[]{:S(2)}, u32[]{:S(2)}) collective-permute-start(f32[512,640]{1,0:T(8,128)S(1)} %get-tuple-element.28.dzi_ref), channel_id=1, source_target_pairs={{0,1},{1,0},{2,3},{3,2},{4,5},{5,4},{6,7},{7,6},{8,9},{9,8},{10,11... | collective-permute-start | bytes 3932168 | tf_op jit(solution)/shard_map/ppermute | solution.py:236
  50.3 20.6 %collective-permute-start.5 = (bf16[512,640]{1,0:T(8,128)(2,1)S(1)}, bf16[512,640]{1,0:T(8,128)(2,1)S(1)}, u32[]{:S(2)}, u32[]{:S(2)}) collective-permute-start(bf16[512,640]{1,0:T(8,128)(2,1)S(1)} %get-tuple-element.36), channel_id=1, source_target_pairs={{510,0},{3,1},{0,2},{5,3},{2,4},{7,5},{4,6},{9,7},{6,8},{11,9},{8,... | collective-permute-start | bytes 1966088 | tf_op jit(solution)/shard_map/ppermute | solution.py:237
  59.2 35.6 %all-to-all-start = ((bf16[256,6,2,128]{3,2,1,0:T(2,128)(2,1)}), bf16[256,6,2,128]{3,2,1,0:T(2,128)(2,1)S(1)}, u32[]{:S(2)}, u32[]{:S(2)}) async-start(bf16[256,6,2,128]{3,2,1,0:T(2,128)(2,1)} %bitcast.2), calls=%async_computation | async-start | bytes 1572864 | tf_op jit(solution)/shard_map/all_to_all | solution.py:255
  70.9 1.3 copy-start.8
  94.8 15.0 %collective-permute-start.6 = (bf16[512,640]{1,0:T(8,128)(2,1)}, bf16[512,640]{1,0:T(8,128)(2,1)S(1)}, u32[]{:S(2)}, u32[]{:S(2)}) collective-permute-start(bf16[512,640]{1,0:T(8,128)(2,1)} %shard_map.89), channel_id=1, source_target_pairs={{510,0},{3,1},{0,2},{5,3},{2,4},{7,5},{4,6},{9,7},{6,8},{11,9},{8,... | collective-permute-start | bytes 1966088 | tf_op jit(solution)/shard_map/ppermute | solution.py:260
  100.3 29.6 %all-to-all-start.1 = ((bf16[256,6,2,128]{3,2,1,0:T(2,128)(2,1)}), bf16[256,6,2,128]{3,2,1,0:T(2,128)(2,1)S(1)}, u32[]{:S(2)}, u32[]{:S(2)}) async-start(bf16[256,6,2,128]{3,2,1,0:T(2,128)(2,1)} %bitcast.4), calls=%async_computation.1 | async-start | bytes 1572864 | tf_op jit(solution)/shard_map/all_to_all | solution.py:275
  109.8 10.9 %copy-start.3 = (bf16[256,640]{1,0:T(8,128)(2,1)S(1)}, bf16[256,640]{1,0:T(8,128)(2,1)}, u32[]{:S(2)}) copy-start(bf16[256,640]{1,0:T(8,128)(2,1)} %text_ref.3) | copy-start | bytes 983044
  109.9 0.8 copy-start.4
  110.7 27.8 %copy-start.1 = (bf16[1152,640]{1,0:T(8,128)(2,1)S(1)}, bf16[1152,640]{1,0:T(8,128)(2,1)}, u32[]{:S(2)}) copy-start(bf16[1152,640]{1,0:T(8,128)(2,1)} %weight_ref.1) | copy-start | bytes 4423684
  110.7 10.0 %collective-permute-start.7 = (bf16[256,640]{1,0:T(8,128)(2,1)S(1)}, bf16[256,640]{1,0:T(8,128)(2,1)S(1)}, u32[]{:S(2)}, u32[]{:S(2)}) collective-permute-start(bf16[256,640]{1,0:T(8,128)(2,1)S(1)} %shard_map.91), channel_id=1, source_target_pairs={{0,1},{1,0},{2,3},{3,2},{4,5},{5,4},{6,7},{7,6},{8,9},{9,8},{10,11... | collective-permute-start | bytes 983048 | tf_op jit(solution)/shard_map/ppermute | solution.py:264
  120.7 1.1 copy-start.5
  129.9 10.5 %collective-permute-start.8 = (bf16[3072,128]{1,0:T(8,128)(2,1)S(1)}, bf16[3072,128]{1,0:T(8,128)(2,1)S(1)}, u32[]{:S(2)}, u32[]{:S(2)}) collective-permute-start(bf16[3072,128]{1,0:T(8,128)(2,1)S(1)} %bitcast.9), channel_id=1, source_target_pairs={{0,1},{1,0},{2,3},{3,2},{4,5},{5,4},{6,7},{7,6},{8,9},{9,8},{10,11... | collective-permute-start | bytes 2359304 | tf_op jit(solution)/shard_map/ppermute | solution.py:281

commit v5 on v4

--- a/solution.py
+++ b/solution.py
@@ -1,4 +1,5 @@
 import functools
+import math
 
 import jax
 import jax.numpy as jnp
@@ -14,7 +15,9 @@
 LANES = 128
 EPS = 1e-06
 CHUNK = 64
+FLAT = 3072
 LONG = 10**11
+GRID = (8, 4, 8)
 
 BF = jnp.bfloat16
 F32 = jnp.float32
@@ -52,7 +55,7 @@
     dzi_in = None
     if has_dzi:
         dzi_in, *refs = refs
-    dzi_ref, dzt_ref, loss_ref, s_ref, c_ref = refs
+    dzi_ref, dzt_refs, (loss_ref, s_ref, c_ref) = refs[0], refs[1:-3], refs[-3:]
     scale = scal_ref[0]
     bias = scal_ref[1]
     loss = jnp.zeros((8, ROWS), F32)
@@ -93,23 +96,22 @@
         else:
             dzi_ref[...] = dzi
         dzt = scale * lax.dot_general(coef, zib, (((0,), (0,)), ((), ())), preferred_element_type=F32)
-        dzt_ref[cols, :] = dzt.astype(dzt_ref.dtype)
+        dzt_refs[q][...] = dzt.astype(dzt_refs[q].dtype)
     loss_ref[...] = loss
 
 
 def score(parts, scal, zib, text, dzi, dzt_dtype):
-    n = len(parts) * ROWS
     args = (scal, zib, text) + (() if dzi is None else (dzi,))
     return call(
         functools.partial(score_kernel, parts, dzi is not None),
         (
             jax.ShapeDtypeStruct((2 * ROWS, E), F32),
-            jax.ShapeDtypeStruct((n, E), dzt_dtype),
+            *(jax.ShapeDtypeStruct((ROWS, E), dzt_dtype) for _ in parts),
             jax.ShapeDtypeStruct((8, ROWS), F32),
         ),
         1,
         len(args) - 1,
-        (VMEM, VMEM, VMEM),
+        (VMEM,) * (len(parts) + 2),
         scratch=(pltpu.VMEM((2 * ROWS, ROWS), F32), pltpu.VMEM((2 * ROWS, ROWS), BF)),
         flops=sum(6 * (hi - lo) * ROWS * E for _, lo, hi, _ in parts),
         bytes_accessed=4 << 20,
@@ -142,26 +144,36 @@
     flat_ref[base + 16 :, :] = jnp.zeros((flat_ref.shape[0] - base - 16, LANES), BF)
 
 
-def reduce_kernel(share, chip_ref, pieces_ref, out_ref, sum_ref):
-    group = 4 * share
+def sum_kernel(pieces_ref, out_ref):
+    n = out_ref.shape[0]
+    for lo in range(0, n, n // 4):
+        total = pieces_ref[lo : lo + n // 4, :].astype(F32)
+        for first in range(n, pieces_ref.shape[0], n):
+            total = total + pieces_ref[first + lo : first + lo + n // 4, :].astype(F32)
+        out_ref[lo : lo + n // 4, :] = total.astype(BF)
+
+
+def reduce_kernel(share, place_ref, pieces_ref, out_ref, sum_ref):
+    group = sum_ref.shape[0]
     groups = pieces_ref.shape[0] // group
     total = jnp.zeros((group, LANES), F32)
     for g in range(groups):
         total = total + pieces_ref[g * group : (g + 1) * group, :].astype(F32)
     sum_ref[...] = total
-    total = sum_ref[0:share, :] + sum_ref[share : 2 * share, :]
-    total = total + (sum_ref[2 * share : 3 * share, :] + sum_ref[3 * share :, :])
+    total = sum_ref[0:share, :]
+    for k in range(1, group // share):
+        total = total + sum_ref[k * share : (k + 1) * share, :]
     total = total * (1.0 / ROWS)
     loss_row = (E // LANES) * HALF
     row = lax.broadcasted_iota(jnp.int32, (share, LANES), 0)
     lane = lax.broadcasted_iota(jnp.int32, (share, LANES), 1)
-    is_loss = (row == loss_row % share) & (chip_ref[0] == loss_row // share)
+    is_loss = (row == loss_row % share) & (place_ref[0] == loss_row // share)
     loss = jnp.sum(jnp.where(row == loss_row % share, total, 0.0), axis=(0, 1), keepdims=True)
     loss = jnp.broadcast_to(loss, (share, LANES))
     high = loss.astype(BF).astype(F32)
     terms = jnp.where(lane == 0, high, jnp.where(lane == 1, loss - high, 0.0))
     total = jnp.where(is_loss, terms, total)
-    for k in range(4):
+    for k in range(group // share):
         sum_ref[k * share : (k + 1) * share, :] = total
     tile = sum_ref[...].astype(BF)
     for g in range(groups):
@@ -179,16 +191,17 @@
     loss_ref[0, 0] = jnp.sum(terms)
 
 
-def relay_kernel(far_ref, part_ref, out_ref):
-    out_ref[...] = (far_ref[...].astype(F32) + part_ref[...]).astype(BF)
-
-
-def second_kernel(pair_ref, out_ref):
-    out_ref[...] = pair_ref[ROWS:, :]
-
-
-def text_kernel(own_ref, far_ref, near_ref, text_ref, out_ref):
-    dzt = own_ref[...] + far_ref[0:ROWS, :].astype(F32) + near_ref[...].astype(F32)
+def relay_kernel(far_same_ref, far_other_ref, near_same_ref, near_other_ref, same_ref, other_ref):
+    same_ref[...] = (far_same_ref[...].astype(F32) + near_same_ref[...]).astype(BF)
+    other_ref[...] = (far_other_ref[...].astype(F32) + near_other_ref[...]).astype(BF)
+
+
+def join_kernel(own_ref, same_ref, out_ref):
+    out_ref[...] = own_ref[...] + same_ref[...].astype(F32)
+
+
+def text_kernel(joined_ref, other_ref, text_ref, out_ref):
+    dzt = joined_ref[...] + other_ref[...].astype(F32)
     text = text_ref[...].astype(F32)
     inv = lax.rsqrt(jnp.sum(text * text, axis=1, keepdims=True) + EPS)
     zt = text * inv
@@ -196,11 +209,13 @@
     out_ref[...] = ((dzt - zt * along) * inv).astype(BF)
 
 
-def per_device(chips, image_feats, text_embeds, head_weight, logit_scale, logit_bias):
-    axes = ("chip", "core")
+def per_device(image_feats, text_embeds, head_weight, logit_scale, logit_bias):
+    axes = ("y", "x", "z", "core")
+    ny, nx, nz = GRID
+    chips = ny * nx * nz
     core = lax.axis_index("core")
     core_id = core.astype(jnp.int32).reshape(1)
-    chip_id = lax.axis_index("chip").astype(jnp.int32).reshape(1)
+    place = lax.axis_index(("x", "y", "z")).astype(jnp.int32).reshape(1)
     across = [(i, i ^ 1) for i in range(2 * chips)]
     onward = [(2 * k + b, 2 * ((k + 2 * b - 1) % chips) + b) for k in range(chips) for b in range(2)]
     beyond = [(2 * k + b, 2 * ((k + 4 * b - 2) % chips) + b) for k in range(chips) for b in range(2)]
@@ -231,17 +246,15 @@
 
     both = 2 * ROWS
     dzi, dzt0, loss0 = score([(0, 0, both, True)], scal, zib, text_embeds, None, F32)
-    dzi, dzt1, loss1 = score([(0, 0, both, False), (1, 0, both, False)], scal, zib, texts1, dzi, F32)
-    dzi, dzt2, loss2 = score([(0, 0, both, False), (1, ROWS, both, False)], scal, zib, texts2, dzi, BF)
+    dzi, near_same, near_other, loss1 = score([(0, 0, both, False), (1, 0, both, False)], scal, zib, texts1, dzi, F32)
+    dzi, far_same, far_other, loss2 = score([(0, 0, both, False), (1, ROWS, both, False)], scal, zib, texts2, dzi, BF)
     dzi_sent = lax.ppermute(dzi, axes, across)
-    far = lax.ppermute(dzt2, axes, back)
-
-    flat_rows = 3072
+
     du, flat = call(
         head_kernel,
         (
             jax.ShapeDtypeStruct((ROWS, E), BF),
-            jax.ShapeDtypeStruct((flat_rows, LANES), BF),
+            jax.ShapeDtypeStruct((FLAT, LANES), BF),
         ),
         0,
         8,
@@ -251,33 +264,48 @@
         bytes_accessed=7 << 20,
     )(dzi, dzi_sent, zi, inv_u, x_half, loss0, loss1, loss2)
 
-    share = flat_rows // chips
-    pieces = lax.all_to_all(flat.reshape(chips, share // 2, 2, LANES), "chip", 0, 0)
-    near = call(
-        relay_kernel, jax.ShapeDtypeStruct((both, E), BF), 0, 2, VMEM, flops=LONG, bytes_accessed=3 << 20
-    )(far, dzt1)
-    pieces, near = lax.optimization_barrier((pieces, near))
-    near = lax.ppermute(near, axes, back)
-    theirs = call(
-        second_kernel, jax.ShapeDtypeStruct((ROWS, E), BF), 0, 1, VMEM, flops=LONG, bytes_accessed=1 << 20
-    )(near)
-    near_other = lax.ppermute(theirs, axes, across)
+    part = FLAT // nx
+    share = FLAT // chips
+    along_x = lax.all_to_all(flat.reshape(nx, part, LANES), "x", 0, 0)
+    summed = call(
+        sum_kernel, jax.ShapeDtypeStruct((part, LANES), BF), 0, 1, VMEM, flops=FLAT * LANES, bytes_accessed=1 << 20
+    )(along_x.reshape(FLAT, LANES))
+    summed, far_same, far_other = lax.optimization_barrier((summed, far_same, far_other))
+    far_same = lax.ppermute(far_same, axes, back)
+    far_other = lax.ppermute(far_other, axes, back)
+    pieces = lax.all_to_all(summed.reshape(ny * nz, share // 2, 2, LANES), ("y", "z"), 0, 0)
+    same, other = call(
+        relay_kernel,
+        (jax.ShapeDtypeStruct((ROWS, E), BF), jax.ShapeDtypeStruct((ROWS, E), BF)),
+        0,
+        4,
+        (VMEM, VMEM),
+        flops=both * E,
+        bytes_accessed=3 << 20,
+    )(far_same, far_other, near_same, near_other)
     spread = call(
         functools.partial(reduce_kernel, share),
-        jax.ShapeDtypeStruct((flat_rows, LANES), BF),
+        jax.ShapeDtypeStruct((part, LANES), BF),
         1,
         1,
         VMEM,
-        scratch=(pltpu.VMEM((4 * share, LANES), F32),),
-        flops=flat_rows * LANES,
-        bytes_accessed=2 << 20,
-    )(chip_id, pieces.reshape(flat_rows, LANES)).reshape(chips, share // 2, 2, LANES)
-    half = lax.all_to_all(spread, "chip", 0, 0).reshape(flat_rows, LANES)
+        scratch=(pltpu.VMEM((math.lcm(share, 48), LANES), F32),),
+        flops=part * LANES,
+        bytes_accessed=1 << 20,
+    )(place, pieces.reshape(part, LANES))
+    home_same = lax.ppermute(same, axes, back)
+    home_other = lax.ppermute(other, axes, [(s, d ^ 1) for s, d in back])
+    mine = lax.all_to_all(spread.reshape(ny * nz, share // 2, 2, LANES), ("y", "z"), 0, 0).reshape(part, LANES)
+    joined = call(
+        join_kernel, jax.ShapeDtypeStruct((ROWS, E), F32), 0, 2, VMEM, flops=LONG, bytes_accessed=2 << 20
+    )(dzt0, home_same)
     text_grad = call(
-        text_kernel, jax.ShapeDtypeStruct((ROWS, E), BF), 0, 4, VMEM, flops=10 * ROWS * E, bytes_accessed=3 << 20
-    )(dzt0, near, near_other, text_embeds)
+        text_kernel, jax.ShapeDtypeStruct((ROWS, E), BF), 0, 3, VMEM, flops=10 * ROWS * E, bytes_accessed=2 << 20
+    )(joined, home_other, text_embeds)
+    mine, du = lax.optimization_barrier((mine, du))
     image_grad = lax.dot_general(du, head_weight, (((1,), (1,)), ((), ())), preferred_element_type=F32).astype(BF)
-    half, text_grad = lax.optimization_barrier((half, text_grad))
+    half = lax.all_to_all(jnp.broadcast_to(mine, (nx, part, LANES)), "x", 0, 0).reshape(FLAT, LANES)
+    half, text_grad, image_grad = lax.optimization_barrier((half, text_grad, image_grad))
     half_other = lax.ppermute(half, axes, across)
 
     head_grad, loss = call(
@@ -294,12 +322,11 @@
 
 
 def solution(mesh):
-    chips = mesh.devices.size // 2
-    by_chip = Mesh(mesh.devices.reshape(chips, 2), ("chip", "core"))
-    rows = P(("chip", "core"), None)
+    by_place = Mesh(mesh.devices.reshape(*GRID, 2), ("y", "x", "z", "core"))
+    rows = P(("y", "x", "z", "core"), None)
     return jax.shard_map(
-        functools.partial(per_device, chips),
-        mesh=by_chip,
+        per_device,
+        mesh=by_place,
         in_specs=(rows, rows, P(), P(), P()),
         out_specs=(P(), rows, rows, P()),
         check_vma=False,

time: 144 us -> 140 us (0.972)
  waiting for transfers between devices: 45.5 us -> 30 us
  blocking collectives: 0 us -> 14.4 us
  starting transfers between devices: 71 us -> 68.8 us
    all_to_all x2 -> x3, waiting for transfers between devices: 28.6 us -> 8.1 us  [the longest x1 6.46 us: per_device(): lax.all_to_all(jnp.broadcast_to(mine, (nx, part, LANES)), 'x', 0, 0)]
    all_to_all x0 -> x1, blocking collectives: none -> 14.4 us  [per_device(): along_x = lax.all_to_all(flat.reshape(nx, part, LANES), 'x', 0, 0)]
    ppermute x3 -> x4, starting transfers between devices: 19.7 us -> 24.7 us  [the longest x1 7.27 us: per_device(): home_same = lax.ppermute(same, axes, back)]
    ppermute x1, starting transfers between devices: 8.59 us -> 4.05 us  [per_device(): half_other = lax.ppermute(half, axes, across)]
    all_to_all x2 -> x3, starting transfers between devices: 21.2 us -> 18.4 us  [the longest x1 10.2 us: per_device(): lax.all_to_all(summed.reshape(ny * nz, share // 2, 2, LANES), ('y', 'z'),...]
    ppermute x1, waiting for transfers between devices: 0.01 us -> 2.64 us  [per_device(): dzi_sent = lax.ppermute(dzi, axes, across)]
    unnamed x19 -> x13, local copies, waits for them, and re-layouts: 5.64 us -> 3.12 us
    ppermute x1, waiting for transfers between devices: 0.4 us -> 1.89 us  [per_device(): half_other = lax.ppermute(half, axes, across)]
  transfers between devices with their start and end apart: 11 -> 13, of which waited for: 6 -> 7; matrix products, arithmetic and copies ran while one was open for 2% -> 4% of each run, Pallas kernels for 8% -> 7%
where the time goes in v5:
time: 140 us
  starting transfers between devices  68.8 us (49%)
  waiting for transfers between devices  30 us (21%)
  Pallas kernels  16 us (11%)
  blocking collectives  14.4 us (10%)
  local copies, waits for them, and re-layouts  4.86 us (3%)
  between operations  3.98 us (3%)
  matrix products  1.49 us (1%)
    all_to_all x1, blocking collectives, per_device(): along_x = lax.all_to_all(flat.reshape(nx, part, LANES), 'x', 0, 0)  14.4 us
    ppermute x1, waiting for transfers between devices, per_device(): texts1 = lax.ppermute(texts0, axes, onward)  11.6 us
    all_to_all x1, starting transfers between devices, per_device(): lax.all_to_all(summed.reshape(ny * nz, share // 2, 2, LANES), ('y', 'z'),...  10.2 us
    ppermute x1, starting transfers between devices, per_device(): text_other = lax.ppermute(text_embeds, axes, across)  8.92 us
    pallas_call x3, Pallas kernels, score(): call(functools.partial(score_kernel, parts, dzi is not None), (jax.ShapeD...  8.26 us
    ppermute x1, starting transfers between devices, per_device(): home_same = lax.ppermute(same, axes, back)  7.27 us
    ppermute x1, starting transfers between devices, per_device(): home_other = lax.ppermute(other, axes, [(s, d ^ 1) for s, d in back])  7.23 us
    ppermute x1, starting transfers between devices, per_device(): far_same = lax.ppermute(far_same, axes, back)  7.15 us
  transfers between devices with their start and end apart: 13, of which 7 were waited for; matrix products, arithmetic and copies ran while one was open for 4% of the time, Pallas kernels for 7%

profile of v5, /device:TPU:1, one launch (start us, length us, event | category | flops | bytes accessed | tf_op | source)
XLA Modules:
  0.0 139.7 jit_solution(12508315683153468602)
XLA Ops:
  0.6 0.0 copy-start.3
  0.6 8.9 %collective-permute-start.1 = (bf16[256,640]{1,0:T(8,128)(2,1)}, bf16[256,640]{1,0:T(8,128)(2,1)S(1)}, u32[]{:S(2)}, u32[]{:S(2)}) collective-permute-start(bf16[256,640]{1,0:T(8,128)(2,1)} %text_ref.3), channel_id=1, source_target_pairs={{0,1},{1,0},{2,3},{3,2},{4,5},{5,4},{6,7},{7,6},{8,9},{9,8},{10,11... | collective-permute-start | bytes 983048 | tf_op jit(solution)/shard_map/ppermute | solution.py:225
  9.6 1.9 %collective-permute-start = (bf16[256,1152]{1,0:T(8,128)(2,1)}, bf16[256,1152]{1,0:T(8,128)(2,1)S(1)}, u32[]{:S(2)}, u32[]{:S(2)}) collective-permute-start(bf16[256,1152]{1,0:T(8,128)(2,1)} %own_ref.1), channel_id=1, source_target_pairs={{0,1},{1,0},{2,3},{3,2},{4,5},{5,4},{6,7},{7,6},{8,9},{9,8},{10,11... | collective-permute-start | bytes 1769480 | tf_op jit(solution)/shard_map/ppermute | solution.py:226
  11.5 1.7 %constant_dynamic-update-slice_fusion.1 = bf16[512,640]{1,0:T(8,128)(2,1)} fusion(bf16[256,640]{1,0:T(8,128)(2,1)} %text_ref.3), kind=kLoop, calls=%fused_computation.2 | loop fusion | bytes 655360
  13.2 0.0 collective-permute-done.1
  13.2 0.8 constant_dynamic-update-slice_fusion
  14.0 1.9 %collective-permute-start.3 = (bf16[512,640]{1,0:T(8,128)(2,1)}, bf16[512,640]{1,0:T(8,128)(2,1)S(1)}, u32[]{:S(2)}, u32[]{:S(2)}) collective-permute-start(bf16[512,640]{1,0:T(8,128)(2,1)} %constant_dynamic-update-slice_fusion), channel_id=1, source_target_pairs={{0,510},{1,3},{2,0},{3,5},{4,2},{5,7},{6,4},{7,9},{8,6},{9,11},{10... | collective-permute-start | bytes 1966088 | tf_op jit(solution)/shard_map/ppermute | solution.py:228
  15.9 2.5 %collective-permute-start.2 = (bf16[512,640]{1,0:T(8,128)(2,1)}, bf16[512,640]{1,0:T(8,128)(2,1)S(1)}, u32[]{:S(2)}, u32[]{:S(2)}) collective-permute-start(bf16[512,640]{1,0:T(8,128)(2,1)} %constant_dynamic-update-slice_fusion), channel_id=1, source_target_pairs={{0,508},{1,5},{2,510},{3,7},{4,0},{5,9},{6,2},{7,11},{8,4},{9,13},... | collective-permute-start | bytes 1966088 | tf_op jit(solution)/shard_map/ppermute | solution.py:229
  19.7 0.1 pad_maximum_fusion.scal_ref
  19.8 0.0 collective-permute-done.other_ref
  19.8 0.0 copy-done.3
  19.8 0.0 copy-start
  19.8 1.4 copy-done
  21.2 0.0 copy-start.2
  21.2 1.4 shard_map.84
  22.6 0.0 copy-done.2
  22.6 2.0 %shard_map.85 = (f32[512,640]{1,0:T(8,128)S(1)}, f32[256,640]{1,0:T(8,128)S(1)}, f32[8,256]{1,0:T(8,128)S(1)}) custom-call(f32[2]{0:T(128)S(1)} %pad_maximum_fusion.scal_ref, bf16[512,640]{1,0:T(8,128)(2,1)S(1)} %get-tuple-element.33.zib_ref, bf16[256,640]{1,0:T(8,128)(2,1)S(1)} %copy-done.2), custom_call_target="tpu_custom_call" | custom-call | flops 503316480 | bytes 4194304 | tf_op jit(solution)/shard_map/pallas_call | solution.py:105
  24.6 0.0 copy-start.4
  24.6 11.6 %collective-permute-done.3.text_ref = bf16[512,640]{1,0:T(8,128)(2,1)S(1)} collective-permute-done((bf16[512,640]{1,0:T(8,128)(2,1)}, bf16[512,640]{1,0:T(8,128)(2,1)S(1)}, u32[]{:S(2)}, u32[]{:S(2)}) %collective-permute-start.3) | collective-permute-done | bytes 655392 | tf_op jit(solution)/shard_map/ppermute | solution.py:228
  36.2 3.1 %shard_map.86 = (f32[512,640]{1,0:T(8,128)S(1)}, f32[256,640]{1,0:T(8,128)S(1)}, f32[256,640]{1,0:T(8,128)S(1)}, f32[8,256]{1,0:T(8,128)S(1)}) custom-call(f32[2]{0:T(128)S(1)} %pad_maximum_fusion.scal_ref, bf16[512,640]{1,0:T(8,128)(2,1)S(1)} %get-tuple-element.33.zib_ref, bf16[512,640]{1,0:T(8,128)(2,1)S(1)} %collective-permute-done.3.text_ref, ...), custom_call_target="tpu_custom_call" | custom-call | flops 1006632960 | bytes 4194304 | tf_op jit(solution)/shard_map/pallas_call | solution.py:105
  39.3 0.0 copy-done.4
  39.3 3.8 %collective-permute-done.2.text_ref = bf16[512,640]{1,0:T(8,128)(2,1)S(1)} collective-permute-done((bf16[512,640]{1,0:T(8,128)(2,1)}, bf16[512,640]{1,0:T(8,128)(2,1)S(1)}, u32[]{:S(2)}, u32[]{:S(2)}) %collective-permute-start.2) | collective-permute-done | bytes 655392 | tf_op jit(solution)/shard_map/ppermute | solution.py:229
  43.1 3.2 %shard_map.87 = (f32[512,640]{1,0:T(8,128)S(1)}, bf16[256,640]{1,0:T(8,128)(2,1)}, bf16[256,640]{1,0:T(8,128)(2,1)S(1)}, f32[8,256]{1,0:T(8,128)S(1)}) custom-call(f32[2]{0:T(128)S(1)} %pad_maximum_fusion.scal_ref, bf16[512,640]{1,0:T(8,128)(2,1)S(1)} %get-tuple-element.33.zib_ref, bf16[512,640]{1,0:T(8,128)(2,1)S(1)} %collective-permute-done.2.text_ref, ...), custom_call_target="tpu_custom_call" | custom-call | flops 754974720 | bytes 4194304 | tf_op jit(solution)/shard_map/pallas_call | solution.py:105
  46.3 6.4 %collective-permute-start.4 = (f32[512,640]{1,0:T(8,128)S(1)}, f32[512,640]{1,0:T(8,128)S(1)}, u32[]{:S(2)}, u32[]{:S(2)}) collective-permute-start(f32[512,640]{1,0:T(8,128)S(1)} %get-tuple-element.36.dzi_ref), channel_id=1, source_target_pairs={{0,1},{1,0},{2,3},{3,2},{4,5},{5,4},{6,7},{7,6},{8,9},{9,8},{10,11... | collective-permute-start | bytes 3932168 | tf_op jit(solution)/shard_map/ppermute | solution.py:251
  52.6 2.6 %collective-permute-done.4.sent_ref = f32[512,640]{1,0:T(8,128)S(1)} collective-permute-done((f32[512,640]{1,0:T(8,128)S(1)}, f32[512,640]{1,0:T(8,128)S(1)}, u32[]{:S(2)}, u32[]{:S(2)}) %collective-permute-start.4) | collective-permute-done | bytes 1310752 | tf_op jit(solution)/shard_map/ppermute | solution.py:251
  55.3 1.4 %shard_map.88 = (bf16[256,640]{1,0:T(8,128)(2,1)S(1)}, bf16[3072,128]{1,0:T(8,128)(2,1)S(1)}) custom-call(f32[512,640]{1,0:T(8,128)S(1)} %get-tuple-element.36.dzi_ref, f32[512,640]{1,0:T(8,128)S(1)} %collective-permute-done.4.sent_ref, f32[512,640]{1,0:T(8,128)S(1)} %get-tuple-element.37.zi_ref, f32[512,128]{1,0:T(8,128)S(1)} %get-tuple-element.38.inv_ref, ...), custom_call_target="tpu_custom_call" | custom-call | flops 377487360 | bytes 7340032 | tf_op jit(solution)/shard_map/pallas_call | solution.py:253
  56.7 14.4 %all_to_all.20 = bf16[4,768,128]{2,1,0:T(8,128)(2,1)S(1)} all-to-all(bf16[4,768,128]{2,1,0:T(8,128)(2,1)S(1)} %bitcast.15), channel_id=1, replica_groups=mesh['y'=8,'x'=4,'z'=8,'core'=2] {'x'}, dimensions={0} | all-to-all | bytes 1572864 | tf_op jit(solution)/shard_map/all_to_all | solution.py:269
  71.2 0.8 shard_map.89
  71.9 10.2 %all-to-all-start.1 = ((bf16[64,6,2,128]{3,2,1,0:T(2,128)(2,1)}), bf16[64,6,2,128]{3,2,1,0:T(2,128)(2,1)S(1)}, u32[]{:S(2)}, u32[]{:S(2)}) async-start(bf16[64,6,2,128]{3,2,1,0:T(2,128)(2,1)} %bitcast.4), calls=%async_computation.1 | async-start | bytes 393216 | tf_op jit(solution)/shard_map/all_to_all | solution.py:276
  82.2 7.2 %collective-permute-start.5 = (bf16[256,640]{1,0:T(8,128)(2,1)}, bf16[256,640]{1,0:T(8,128)(2,1)S(1)}, u32[]{:S(2)}, u32[]{:S(2)}) collective-permute-start(bf16[256,640]{1,0:T(8,128)(2,1)} %get-tuple-element.50), channel_id=1, source_target_pairs={{510,0},{3,1},{0,2},{5,3},{2,4},{7,5},{4,6},{9,7},{6,8},{11,9},{8,... | collective-permute-start | bytes 983048 | tf_op jit(solution)/shard_map/ppermute | solution.py:274
  89.4 3.1 %collective-permute-start.6 = (bf16[256,640]{1,0:T(8,128)(2,1)S(1)}, bf16[256,640]{1,0:T(8,128)(2,1)S(1)}, u32[]{:S(2)}, u32[]{:S(2)}) collective-permute-start(bf16[256,640]{1,0:T(8,128)(2,1)S(1)} %get-tuple-element.51), channel_id=1, source_target_pairs={{510,0},{3,1},{0,2},{5,3},{2,4},{7,5},{4,6},{9,7},{6,8},{11,9},{8,... | collective-permute-start | bytes 983048 | tf_op jit(solution)/shard_map/ppermute | solution.py:275
  92.5 1.6 %all-to-all-done.1 = bf16[64,6,2,128]{3,2,1,0:T(2,128)(2,1)S(1)} async-done(((bf16[64,6,2,128]{3,2,1,0:T(2,128)(2,1)}), bf16[64,6,2,128]{3,2,1,0:T(2,128)(2,1)S(1)}, u32[]{:S(2)}, u32[]{:S(2)}) %all-to-all-start.1) | async-done | bytes 196640 | tf_op jit(solution)/shard_map/all_to_all | solution.py:276
  94.1 0.9 shard_map.90
  94.9 4.7 %all-to-all-start.2 = ((bf16[64,6,2,128]{3,2,1,0:T(2,128)(2,1)}), bf16[64,6,2,128]{3,2,1,0:T(2,128)(2,1)S(1)}, u32[]{:S(2)}, u32[]{:S(2)}) async-start(bf16[64,6,2,128]{3,2,1,0:T(2,128)(2,1)} %bitcast.6), calls=%async_computation.2 | async-start | bytes 393216 | tf_op jit(solution)/shard_map/all_to_all | solution.py:298
  99.6 0.0 collective-permute-done.5.far_same_ref
  99.6 0.0 collective-permute-done.6.far_other_ref
  99.6 0.8 shard_map.91
  100.4 0.0 copy-start.5
  100.4 7.3 %collective-permute-start.7 = (bf16[256,640]{1,0:T(8,128)(2,1)}, bf16[256,640]{1,0:T(8,128)(2,1)S(1)}, u32[]{:S(2)}, u32[]{:S(2)}) collective-permute-start(bf16[256,640]{1,0:T(8,128)(2,1)} %get-tuple-element.54), channel_id=1, source_target_pairs={{510,0},{3,1},{0,2},{5,3},{2,4},{7,5},{4,6},{9,7},{6,8},{11,9},{8,... | collective-permute-start | bytes 983048 | tf_op jit(solution)/shard_map/ppermute | solution.py:296
  107.7 7.2 %collective-permute-start.8 = (bf16[256,640]{1,0:T(8,128)(2,1)S(1)}, bf16[256,640]{1,0:T(8,128)(2,1)S(1)}, u32[]{:S(2)}, u32[]{:S(2)}) collective-permute-start(bf16[256,640]{1,0:T(8,128)(2,1)S(1)} %get-tuple-element.55), channel_id=1, source_target_pairs={{510,1},{3,0},{0,3},{5,2},{2,5},{7,4},{4,7},{9,6},{6,9},{11,8},{8,... | collective-permute-start | bytes 983048 | tf_op jit(solution)/shard_map/ppermute | solution.py:297
  115.0 0.0 all-to-all-done.2
  115.0 1.0 broadcast_in_dim.3
  116.0 3.5 %all-to-all-start.3 = ((bf16[4,768,128]{2,1,0:T(8,128)(2,1)}), bf16[4,768,128]{2,1,0:T(8,128)(2,1)S(1)}, u32[]{:S(2)}, u32[]{:S(2)}) async-start(bf16[4,768,128]{2,1,0:T(8,128)(2,1)} %broadcast_in_dim.3), calls=%async_computation.3 | async-start | bytes 1572864 | tf_op jit(solution)/shard_map/all_to_all | solution.py:307
  119.5 0.0 collective-permute-done.7.same_ref
  119.5 0.0 copy-done.5
  119.5 0.1 shard_map.92.joined_ref
  119.6 0.0 copy-start.1
  119.6 2.0 %collective-permute-done.8.other_ref = bf16[256,640]{1,0:T(8,128)(2,1)S(1)} collective-permute-done((bf16[256,640]{1,0:T(8,128)(2,1)S(1)}, bf16[256,640]{1,0:T(8,128)(2,1)S(1)}, u32[]{:S(2)}, u32[]{:S(2)}) %collective-permute-start.8) | collective-permute-done | bytes 327712 | tf_op jit(solution)/shard_map/ppermute | solution.py:297
  121.6 1.0 shard_map.93
  122.6 0.0 copy-done.1
  122.6 1.5 %convolution_convert_fusion = bf16[256,1152]{1,0:T(8,128)(2,1)} fusion(bf16[256,640]{1,0:T(8,128)(2,1)S(1)} %get-tuple-element.56, bf16[1152,640]{1,0:T(8,128)(2,1)S(1)} %copy-done.1), kind=kOutput, calls=%fused_computation | convolution fusion | flops 377782272 | bytes 2392064 | tf_op jit(solution)/shard_map/dot_general | solution.py:306
  124.1 6.5 %all-to-all-done.3 = bf16[4,768,128]{2,1,0:T(8,128)(2,1)S(1)} async-done(((bf16[4,768,128]{2,1,0:T(8,128)(2,1)}), bf16[4,768,128]{2,1,0:T(8,128)(2,1)S(1)}, u32[]{:S(2)}, u32[]{:S(2)}) %all-to-all-start.3) | async-done | bytes 786464 | tf_op jit(solution)/shard_map/all_to_all | solution.py:307
  130.5 4.1 %collective-permute-start.9 = (bf16[3072,128]{1,0:T(8,128)(2,1)S(1)}, bf16[3072,128]{1,0:T(8,128)(2,1)S(1)}, u32[]{:S(2)}, u32[]{:S(2)}) collective-permute-start(bf16[3072,128]{1,0:T(8,128)(2,1)S(1)} %bitcast.12), channel_id=1, source_target_pairs={{0,1},{1,0},{2,3},{3,2},{4,5},{5,4},{6,7},{7,6},{8,9},{9,8},{10,11... | collective-permute-start | bytes 2359304 | tf_op jit(solution)/shard_map/ppermute | solution.py:309
  134.6 1.9 %collective-permute-done.9.other_ref = bf16[3072,128]{1,0:T(8,128)(2,1)S(1)} collective-permute-done((bf16[3072,128]{1,0:T(8,128)(2,1)S(1)}, bf16[3072,128]{1,0:T(8,128)(2,1)S(1)}, u32[]{:S(2)}, u32[]{:S(2)}) %collective-permute-start.9) | collective-permute-done | bytes 786464 | tf_op jit(solution)/shard_map/ppermute | solution.py:309
  136.5 1.4 shard_map.94
Async XLA Ops:
  0.6 19.2 %copy-start.3 = (bf16[256,1152]{1,0:T(8,128)(2,1)S(1)}, bf16[256,1152]{1,0:T(8,128)(2,1)}, u32[]{:S(2)}) copy-start(bf16[256,1152]{1,0:T(8,128)(2,1)} %own_ref.1) | copy-start | bytes 1769476
  0.6 12.6 %collective-permute-start.1 = (bf16[256,640]{1,0:T(8,128)(2,1)}, bf16[256,640]{1,0:T(8,128)(2,1)S(1)}, u32[]{:S(2)}, u32[]{:S(2)}) collective-permute-start(bf16[256,640]{1,0:T(8,128)(2,1)} %text_ref.3), channel_id=1, source_target_pairs={{0,1},{1,0},{2,3},{3,2},{4,5},{5,4},{6,7},{7,6},{8,9},{9,8},{10,11... | collective-permute-start | bytes 983048 | tf_op jit(solution)/shard_map/ppermute | solution.py:225
  9.6 10.2 %collective-permute-start = (bf16[256,1152]{1,0:T(8,128)(2,1)}, bf16[256,1152]{1,0:T(8,128)(2,1)S(1)}, u32[]{:S(2)}, u32[]{:S(2)}) collective-permute-start(bf16[256,1152]{1,0:T(8,128)(2,1)} %own_ref.1), channel_id=1, source_target_pairs={{0,1},{1,0},{2,3},{3,2},{4,5},{5,4},{6,7},{7,6},{8,9},{9,8},{10,11... | collective-permute-start | bytes 1769480 | tf_op jit(solution)/shard_map/ppermute | solution.py:226
  14.0 22.2 %collective-permute-start.3 = (bf16[512,640]{1,0:T(8,128)(2,1)}, bf16[512,640]{1,0:T(8,128)(2,1)S(1)}, u32[]{:S(2)}, u32[]{:S(2)}) collective-permute-start(bf16[512,640]{1,0:T(8,128)(2,1)} %constant_dynamic-update-slice_fusion), channel_id=1, source_target_pairs={{0,510},{1,3},{2,0},{3,5},{4,2},{5,7},{6,4},{7,9},{8,6},{9,11},{10... | collective-permute-start | bytes 1966088 | tf_op jit(solution)/shard_map/ppermute | solution.py:228
  15.9 27.2 %collective-permute-start.2 = (bf16[512,640]{1,0:T(8,128)(2,1)}, bf16[512,640]{1,0:T(8,128)(2,1)S(1)}, u32[]{:S(2)}, u32[]{:S(2)}) collective-permute-start(bf16[512,640]{1,0:T(8,128)(2,1)} %constant_dynamic-update-slice_fusion), channel_id=1, source_target_pairs={{0,508},{1,5},{2,510},{3,7},{4,0},{5,9},{6,2},{7,11},{8,4},{9,13},... | collective-permute-start | bytes 1966088 | tf_op jit(solution)/shard_map/ppermute | solution.py:229
  19.8 1.4 copy-start
  21.2 1.4 %copy-start.2 = (bf16[256,640]{1,0:T(8,128)(2,1)S(1)}, bf16[256,640]{1,0:T(8,128)(2,1)}, u32[]{:S(2)}) copy-start(bf16[256,640]{1,0:T(8,128)(2,1)} %text_ref.3) | copy-start | bytes 983044
  24.6 14.7 %copy-start.4 = (f32[256,640]{1,0:T(8,128)}, f32[256,640]{1,0:T(8,128)S(1)}, u32[]{:S(2)}) copy-start(f32[256,640]{1,0:T(8,128)S(1)} %get-tuple-element.49.own_ref) | copy-start | bytes 1966084
  46.3 9.0 %collective-permute-start.4 = (f32[512,640]{1,0:T(8,128)S(1)}, f32[512,640]{1,0:T(8,128)S(1)}, u32[]{:S(2)}, u32[]{:S(2)}) collective-permute-start(f32[512,640]{1,0:T(8,128)S(1)} %get-tuple-element.36.dzi_ref), channel_id=1, source_target_pairs={{0,1},{1,0},{2,3},{3,2},{4,5},{5,4},{6,7},{7,6},{8,9},{9,8},{10,11... | collective-permute-start | bytes 3932168 | tf_op jit(solution)/shard_map/ppermute | solution.py:251
  71.9 22.2 %all-to-all-start.1 = ((bf16[64,6,2,128]{3,2,1,0:T(2,128)(2,1)}), bf16[64,6,2,128]{3,2,1,0:T(2,128)(2,1)S(1)}, u32[]{:S(2)}, u32[]{:S(2)}) async-start(bf16[64,6,2,128]{3,2,1,0:T(2,128)(2,1)} %bitcast.4), calls=%async_computation.1 | async-start | bytes 393216 | tf_op jit(solution)/shard_map/all_to_all | solution.py:276
  82.2 17.4 %collective-permute-start.5 = (bf16[256,640]{1,0:T(8,128)(2,1)}, bf16[256,640]{1,0:T(8,128)(2,1)S(1)}, u32[]{:S(2)}, u32[]{:S(2)}) collective-permute-start(bf16[256,640]{1,0:T(8,128)(2,1)} %get-tuple-element.50), channel_id=1, source_target_pairs={{510,0},{3,1},{0,2},{5,3},{2,4},{7,5},{4,6},{9,7},{6,8},{11,9},{8,... | collective-permute-start | bytes 983048 | tf_op jit(solution)/shard_map/ppermute | solution.py:274
  89.4 10.3 %collective-permute-start.6 = (bf16[256,640]{1,0:T(8,128)(2,1)S(1)}, bf16[256,640]{1,0:T(8,128)(2,1)S(1)}, u32[]{:S(2)}, u32[]{:S(2)}) collective-permute-start(bf16[256,640]{1,0:T(8,128)(2,1)S(1)} %get-tuple-element.51), channel_id=1, source_target_pairs={{510,0},{3,1},{0,2},{5,3},{2,4},{7,5},{4,6},{9,7},{6,8},{11,9},{8,... | collective-permute-start | bytes 983048 | tf_op jit(solution)/shard_map/ppermute | solution.py:275
  94.9 20.0 %all-to-all-start.2 = ((bf16[64,6,2,128]{3,2,1,0:T(2,128)(2,1)}), bf16[64,6,2,128]{3,2,1,0:T(2,128)(2,1)S(1)}, u32[]{:S(2)}, u32[]{:S(2)}) async-start(bf16[64,6,2,128]{3,2,1,0:T(2,128)(2,1)} %bitcast.6), calls=%async_computation.2 | async-start | bytes 393216 | tf_op jit(solution)/shard_map/all_to_all | solution.py:298
  100.4 19.0 %copy-start.5 = (f32[256,640]{1,0:T(8,128)S(1)}, f32[256,640]{1,0:T(8,128)}, u32[]{:S(2)}) copy-start(f32[256,640]{1,0:T(8,128)} %copy-done.4) | copy-start | bytes 1966084
  100.4 19.0 %collective-permute-start.7 = (bf16[256,640]{1,0:T(8,128)(2,1)}, bf16[256,640]{1,0:T(8,128)(2,1)S(1)}, u32[]{:S(2)}, u32[]{:S(2)}) collective-permute-start(bf16[256,640]{1,0:T(8,128)(2,1)} %get-tuple-element.54), channel_id=1, source_target_pairs={{510,0},{3,1},{0,2},{5,3},{2,4},{7,5},{4,6},{9,7},{6,8},{11,9},{8,... | collective-permute-start | bytes 983048 | tf_op jit(solution)/shard_map/ppermute | solution.py:296
  107.7 13.8 %collective-permute-start.8 = (bf16[256,640]{1,0:T(8,128)(2,1)S(1)}, bf16[256,640]{1,0:T(8,128)(2,1)S(1)}, u32[]{:S(2)}, u32[]{:S(2)}) collective-permute-start(bf16[256,640]{1,0:T(8,128)(2,1)S(1)} %get-tuple-element.55), channel_id=1, source_target_pairs={{510,1},{3,0},{0,3},{5,2},{2,5},{7,4},{4,7},{9,6},{6,9},{11,8},{8,... | collective-permute-start | bytes 983048 | tf_op jit(solution)/shard_map/ppermute | solution.py:297
  116.0 14.6 %all-to-all-start.3 = ((bf16[4,768,128]{2,1,0:T(8,128)(2,1)}), bf16[4,768,128]{2,1,0:T(8,128)(2,1)S(1)}, u32[]{:S(2)}, u32[]{:S(2)}) async-start(bf16[4,768,128]{2,1,0:T(8,128)(2,1)} %broadcast_in_dim.3), calls=%async_computation.3 | async-start | bytes 1572864 | tf_op jit(solution)/shard_map/all_to_all | solution.py:307
  119.6 3.0 %copy-start.1 = (bf16[1152,640]{1,0:T(8,128)(2,1)S(1)}, bf16[1152,640]{1,0:T(8,128)(2,1)}, u32[]{:S(2)}) copy-start(bf16[1152,640]{1,0:T(8,128)(2,1)} %weight_ref.1) | copy-start | bytes 4423684
  130.5 6.0 %collective-permute-start.9 = (bf16[3072,128]{1,0:T(8,128)(2,1)S(1)}, bf16[3072,128]{1,0:T(8,128)(2,1)S(1)}, u32[]{:S(2)}, u32[]{:S(2)}) collective-permute-start(bf16[3072,128]{1,0:T(8,128)(2,1)S(1)} %bitcast.12), channel_id=1, source_target_pairs={{0,1},{1,0},{2,3},{3,2},{4,5},{5,4},{6,7},{7,6},{8,9},{9,8},{10,11... | collective-permute-start | bytes 2359304 | tf_op jit(solution)/shard_map/ppermute | solution.py:309

commit v6 on v5

--- a/solution.py
+++ b/solution.py
@@ -51,7 +51,8 @@
     xt_ref[...] = all_ref[pl.ds(pl.multiple_of(core_ref[0] * HALF, HALF), HALF), :]
 
 
-def score_kernel(parts, has_dzi, scal_ref, zib_ref, text_ref, *refs):
+def score_kernel(parts, has_dzi, scal_ref, zib_ref, *refs):
+    text_refs, refs = refs[: len(parts)], refs[len(parts) :]
     dzi_in = None
     if has_dzi:
         dzi_in, *refs = refs
@@ -59,10 +60,9 @@
     scale = scal_ref[0]
     bias = scal_ref[1]
     loss = jnp.zeros((8, ROWS), F32)
-    for order, (q, lo, hi, diag) in enumerate(parts):
+    for q, (lo, hi, diag) in enumerate(parts):
         n = hi - lo
-        cols = pl.ds(q * ROWS, ROWS)
-        text = text_ref[cols, :].astype(F32)
+        text = text_refs[q][...].astype(F32)
         inv = lax.rsqrt(jnp.sum(text * text, axis=1, keepdims=True) + EPS)
         ztb = (text * inv).astype(BF)
         zib = zib_ref[lo:hi, :]
@@ -89,10 +89,12 @@
             loss = loss + jnp.sum(jnp.log(prod).reshape(k // 8, 8, ROWS), axis=0)
         coef = c_ref[0:n, :]
         dzi = scale * jnp.dot(coef, ztb, preferred_element_type=F32)
-        if order:
+        if q:
             dzi_ref[lo:hi, :] += dzi
         elif has_dzi:
-            dzi_ref[...] = dzi_in[...] + dzi
+            dzi_ref[lo:hi, :] = dzi_in[lo:hi, :] + dzi
+            if lo:
+                dzi_ref[0:lo, :] = dzi_in[0:lo, :]
         else:
             dzi_ref[...] = dzi
         dzt = scale * lax.dot_general(coef, zib, (((0,), (0,)), ((), ())), preferred_element_type=F32)
@@ -100,8 +102,8 @@
     loss_ref[...] = loss
 
 
-def score(parts, scal, zib, text, dzi, dzt_dtype):
-    args = (scal, zib, text) + (() if dzi is None else (dzi,))
+def score(parts, scal, zib, texts, dzi, dzt_dtype):
+    args = (scal, zib, *texts) + (() if dzi is None else (dzi,))
     return call(
         functools.partial(score_kernel, parts, dzi is not None),
         (
@@ -113,12 +115,13 @@
         len(args) - 1,
         (VMEM,) * (len(parts) + 2),
         scratch=(pltpu.VMEM((2 * ROWS, ROWS), F32), pltpu.VMEM((2 * ROWS, ROWS), BF)),
-        flops=sum(6 * (hi - lo) * ROWS * E for _, lo, hi, _ in parts),
+        flops=sum(6 * (hi - lo) * ROWS * E for lo, hi, _ in parts),
         bytes_accessed=4 << 20,
     )(*args)
 
 
-def head_kernel(dzi_ref, sent_ref, zi_ref, inv_ref, xt_ref, la_ref, lb_ref, lc_ref, du_ref, flat_ref, all_ref):
+def head_kernel(dzi_ref, sent_ref, zi_ref, inv_ref, xt_ref, *refs):
+    *loss_refs, du_ref, flat_ref, all_ref = refs
     for part in range(2):
         rows = pl.ds(part * ROWS, ROWS)
         swapped = pl.ds((1 - part) * ROWS, ROWS)
@@ -132,7 +135,7 @@
     for slab in range(E // LANES):
         part = jnp.dot(xt_ref[...], all_ref[:, slab * LANES : (slab + 1) * LANES], preferred_element_type=F32)
         flat_ref[slab * HALF : (slab + 1) * HALF, :] = part.astype(BF)
-    loss = jnp.sum(la_ref[...] + lb_ref[...] + lc_ref[...])
+    loss = jnp.sum(sum(ref[...] for ref in loss_refs))
     total = jnp.full((16, LANES), loss, F32)
     high = total.astype(BF).astype(F32)
     low = (total - high).astype(BF).astype(F32)
@@ -222,11 +225,12 @@
     back = [(d, s) for s, d in onward]
     scal = jnp.concatenate([logit_scale, logit_bias])
 
+    near_same = lax.ppermute(text_embeds, axes, onward)
     text_other = lax.ppermute(text_embeds, axes, across)
     x_other = lax.ppermute(image_feats, axes, across)
-    texts0 = jnp.concatenate([text_embeds, text_other])
-    texts1 = lax.ppermute(texts0, axes, onward)
-    texts2 = lax.ppermute(texts0, axes, beyond)
+    near_other = lax.ppermute(text_other, axes, onward)
+    far_same = lax.ppermute(text_embeds, axes, beyond)
+    far_other = lax.ppermute(text_other, axes, beyond)
 
     zi, zib, inv_u, x_half = call(
         project_kernel,
@@ -245,9 +249,12 @@
     )(core_id, image_feats, x_other, head_weight)
 
     both = 2 * ROWS
-    dzi, dzt0, loss0 = score([(0, 0, both, True)], scal, zib, text_embeds, None, F32)
-    dzi, near_same, near_other, loss1 = score([(0, 0, both, False), (1, 0, both, False)], scal, zib, texts1, dzi, F32)
-    dzi, far_same, far_other, loss2 = score([(0, 0, both, False), (1, ROWS, both, False)], scal, zib, texts2, dzi, BF)
+    whole = (0, both, False)
+    dzi, dzt0, loss0 = score([(0, both, True)], scal, zib, [text_embeds], None, F32)
+    dzi, far_same, loss1 = score([whole], scal, zib, [far_same], dzi, BF)
+    dzi, far_other, loss2 = score([(ROWS, both, False)], scal, zib, [far_other], dzi, BF)
+    dzi, near_same, loss3 = score([whole], scal, zib, [near_same], dzi, F32)
+    dzi, near_other, loss4 = score([whole], scal, zib, [near_other], dzi, F32)
     dzi_sent = lax.ppermute(dzi, axes, across)
 
     du, flat = call(
@@ -257,12 +264,12 @@
             jax.ShapeDtypeStruct((FLAT, LANES), BF),
         ),
         0,
-        8,
+        10,
         (VMEM, VMEM),
         scratch=(pltpu.VMEM((2 * ROWS, E), BF),),
         flops=2 * 2 * ROWS * HALF * E,
         bytes_accessed=7 << 20,
-    )(dzi, dzi_sent, zi, inv_u, x_half, loss0, loss1, loss2)
+    )(dzi, dzi_sent, zi, inv_u, x_half, loss0, loss1, loss2, loss3, loss4)
 
     part = FLAT // nx
     share = FLAT // chips

time: 140 us -> 135 us (0.964)
  waiting for transfers between devices: 30 us -> 20 us
  starting transfers between devices: 68.8 us -> 74.5 us
  local copies, waits for them, and re-layouts: 4.86 us -> 3.44 us
    ppermute x2 -> x4, starting transfers between devices: 4.42 us -> 13.7 us  [the longest x1 5.53 us: per_device(): far_other = lax.ppermute(text_other, axes, beyond)]
    ppermute x2 -> x4, waiting for transfers between devices: 15.4 us -> 6.31 us  [the longest x1 3.08 us: per_device(): far_other = lax.ppermute(text_other, axes, beyond)]
    ppermute x1, starting transfers between devices: 8.92 us -> 1.92 us  [per_device(): text_other = lax.ppermute(text_embeds, axes, across)]
    ppermute x1, starting transfers between devices: 1.92 us -> 8.79 us  [per_device(): x_other = lax.ppermute(image_feats, axes, across)]
    ppermute x1, starting transfers between devices: 6.36 us -> 2.75 us  [per_device(): dzi_sent = lax.ppermute(dzi, axes, across)]
    pallas_call x3 -> x5, Pallas kernels: 8.26 us -> 9.27 us  [score(): call(functools.partial(score_kernel, parts, dzi is not None), (jax.ShapeD...]
    unnamed x13 -> x12, local copies, waits for them, and re-layouts: 3.12 us -> 2.46 us
  transfers between devices with their start and end apart: 13 -> 15, of which waited for: 7 -> 8; matrix products, arithmetic and copies ran while one was open for 4% -> 2% of each run, Pallas kernels for 7% -> 8%
where the time goes in v6:
time: 135 us; the launch traced here: 134 us
  starting transfers between devices  74.5 us (55%)
  waiting for transfers between devices  20 us (15%)
  Pallas kernels  16.3 us (12%)
  blocking collectives  14.4 us (11%)
  between operations  3.91 us (3%)
  local copies, waits for them, and re-layouts  3.44 us (3%)
  matrix products  1.49 us (1%)
    all_to_all x1, blocking collectives, per_device(): along_x = lax.all_to_all(flat.reshape(nx, part, LANES), 'x', 0, 0)  14.4 us
    all_to_all x1, starting transfers between devices, per_device(): lax.all_to_all(summed.reshape(ny * nz, share // 2, 2, LANES), ('y', 'z'),...  9.45 us
    pallas_call x5, Pallas kernels, score(): call(functools.partial(score_kernel, parts, dzi is not None), (jax.ShapeD...  9.27 us
    ppermute x1, starting transfers between devices, per_device(): x_other = lax.ppermute(image_feats, axes, across)  8.79 us
    ppermute x1, starting transfers between devices, per_device(): home_same = lax.ppermute(same, axes, back)  7.28 us
    ppermute x1, starting transfers between devices, per_device(): home_other = lax.ppermute(other, axes, [(s, d ^ 1) for s, d in back])  7.24 us
    ppermute x1, starting transfers between devices, per_device(): far_same = lax.ppermute(far_same, axes, back)  7.15 us
    ppermute x1, starting transfers between devices, per_device(): far_other = lax.ppermute(text_other, axes, beyond)  5.53 us
  transfers between devices with their start and end apart: 15, of which 8 were waited for; matrix products, arithmetic and copies ran while one was open for 2% of the time, Pallas kernels for 8%

profile of v6, /device:TPU:1, one launch (start us, length us, event | category | flops | bytes accessed | tf_op | source)
XLA Modules:
  0.0 134.1 jit_solution(16046269288123512843)
XLA Ops:
  0.6 8.8 %collective-permute-start = (bf16[256,1152]{1,0:T(8,128)(2,1)}, bf16[256,1152]{1,0:T(8,128)(2,1)S(1)}, u32[]{:S(2)}, u32[]{:S(2)}) collective-permute-start(bf16[256,1152]{1,0:T(8,128)(2,1)} %own_ref.1), channel_id=1, source_target_pairs={{0,1},{1,0},{2,3},{3,2},{4,5},{5,4},{6,7},{7,6},{8,9},{9,8},{10,11... | collective-permute-start | bytes 1769480 | tf_op jit(solution)/shard_map/ppermute | solution.py:230
  9.4 1.9 %collective-permute-start.1 = (bf16[256,640]{1,0:T(8,128)(2,1)}, bf16[256,640]{1,0:T(8,128)(2,1)S(1)}, u32[]{:S(2)}, u32[]{:S(2)}) collective-permute-start(bf16[256,640]{1,0:T(8,128)(2,1)} %text_ref.1), channel_id=1, source_target_pairs={{0,1},{1,0},{2,3},{3,2},{4,5},{5,4},{6,7},{7,6},{8,9},{9,8},{10,11... | collective-permute-start | bytes 983048 | tf_op jit(solution)/shard_map/ppermute | solution.py:229
  11.4 1.9 %collective-permute-start.5 = (bf16[256,640]{1,0:T(8,128)(2,1)}, bf16[256,640]{1,0:T(8,128)(2,1)S(1)}, u32[]{:S(2)}, u32[]{:S(2)}) collective-permute-start(bf16[256,640]{1,0:T(8,128)(2,1)} %text_ref.1), channel_id=1, source_target_pairs={{0,508},{1,5},{2,510},{3,7},{4,0},{5,9},{6,2},{7,11},{8,4},{9,13},... | collective-permute-start | bytes 983048 | tf_op jit(solution)/shard_map/ppermute | solution.py:232
  13.3 0.0 collective-permute-done.1
  13.3 5.5 %collective-permute-start.4 = (bf16[256,640]{1,0:T(8,128)(2,1)S(1)}, bf16[256,640]{1,0:T(8,128)(2,1)S(1)}, u32[]{:S(2)}, u32[]{:S(2)}) collective-permute-start(bf16[256,640]{1,0:T(8,128)(2,1)S(1)} %collective-permute-done.1), channel_id=1, source_target_pairs={{0,508},{1,5},{2,510},{3,7},{4,0},{5,9},{6,2},{7,11},{8,4},{9,13},... | collective-permute-start | bytes 983048 | tf_op jit(solution)/shard_map/ppermute | solution.py:233
  18.8 3.1 %collective-permute-start.3 = (bf16[256,640]{1,0:T(8,128)(2,1)}, bf16[256,640]{1,0:T(8,128)(2,1)S(1)}, u32[]{:S(2)}, u32[]{:S(2)}) collective-permute-start(bf16[256,640]{1,0:T(8,128)(2,1)} %text_ref.1), channel_id=1, source_target_pairs={{0,510},{1,3},{2,0},{3,5},{4,2},{5,7},{6,4},{7,9},{8,6},{9,11},{10... | collective-permute-start | bytes 983048 | tf_op jit(solution)/shard_map/ppermute | solution.py:228
  23.2 3.1 %collective-permute-start.2 = (bf16[256,640]{1,0:T(8,128)(2,1)S(1)}, bf16[256,640]{1,0:T(8,128)(2,1)S(1)}, u32[]{:S(2)}, u32[]{:S(2)}) collective-permute-start(bf16[256,640]{1,0:T(8,128)(2,1)S(1)} %collective-permute-done.1), channel_id=1, source_target_pairs={{0,510},{1,3},{2,0},{3,5},{4,2},{5,7},{6,4},{7,9},{8,6},{9,11},{10... | collective-permute-start | bytes 983048 | tf_op jit(solution)/shard_map/ppermute | solution.py:231
  26.4 0.1 pad_maximum_fusion.scal_ref
  26.4 0.0 collective-permute-done.other_ref
  26.4 0.0 copy-start
  26.4 1.4 %copy-done = bf16[1152,640]{1,0:T(8,128)(2,1)S(1)} copy-done((bf16[1152,640]{1,0:T(8,128)(2,1)S(1)}, bf16[1152,640]{1,0:T(8,128)(2,1)}, u32[]{:S(2)}) %copy-start) | copy-done | bytes 1474584
  27.8 0.0 copy-start.3
  27.8 1.1 copy-done.3
  28.9 0.0 copy-start.2
  28.9 1.4 %shard_map.84 = (f32[512,640]{1,0:T(8,128)S(1)}, bf16[512,640]{1,0:T(8,128)(2,1)S(1)}, f32[512,128]{1,0:T(8,128)S(1)}, bf16[576,512]{1,0:T(8,128)(2,1)S(1)}) custom-call(s32[1]{0:T(128)} %bitcast.core_ref, bf16[256,1152]{1,0:T(8,128)(2,1)S(1)} %copy-done.3, bf16[256,1152]{1,0:T(8,128)(2,1)S(1)} %collective-permute-done.other_ref, bf16[1152,640]{1,0:T(8,128)(2,1)S(1)} %copy-done), custom_call_target="tpu_custom_call" | custom-call | flops 754974720 | bytes 5242880 | tf_op jit(solution)/shard_map/pallas_call | solution.py:235
  30.3 0.0 copy-done.2
  30.3 2.0 %shard_map.85 = (f32[512,640]{1,0:T(8,128)S(1)}, f32[256,640]{1,0:T(8,128)S(1)}, f32[8,256]{1,0:T(8,128)S(1)}) custom-call(f32[2]{0:T(128)S(1)} %pad_maximum_fusion.scal_ref, bf16[512,640]{1,0:T(8,128)(2,1)S(1)} %get-tuple-element.37.zib_ref, bf16[256,640]{1,0:T(8,128)(2,1)S(1)} %copy-done.2), custom_call_target="tpu_custom_call" | custom-call | flops 503316480 | bytes 4194304 | tf_op jit(solution)/shard_map/pallas_call | solution.py:107
  32.3 0.0 copy-start.4
  32.3 0.0 collective-permute-done.5.refs_0_
  32.3 1.9 %shard_map.86 = (f32[512,640]{1,0:T(8,128)S(1)}, bf16[256,640]{1,0:T(8,128)(2,1)S(1)}, f32[8,256]{1,0:T(8,128)S(1)}) custom-call(f32[2]{0:T(128)S(1)} %pad_maximum_fusion.scal_ref, bf16[512,640]{1,0:T(8,128)(2,1)S(1)} %get-tuple-element.37.zib_ref, bf16[256,640]{1,0:T(8,128)(2,1)S(1)} %collective-permute-done.5.refs_0_, f32[512,640]{1,0:T(8,128)S(1)} %get-tuple-element.38.refs_1_), custom_call_target="tpu_custom_call" | custom-call | flops 503316480 | bytes 4194304 | tf_op jit(solution)/shard_map/pallas_call | solution.py:107
  34.2 3.1 %collective-permute-done.4.refs_0_ = bf16[256,640]{1,0:T(8,128)(2,1)S(1)} collective-permute-done((bf16[256,640]{1,0:T(8,128)(2,1)S(1)}, bf16[256,640]{1,0:T(8,128)(2,1)S(1)}, u32[]{:S(2)}, u32[]{:S(2)}) %collective-permute-start.4) | collective-permute-done | bytes 327712 | tf_op jit(solution)/shard_map/ppermute | solution.py:233
  37.3 1.5 %shard_map.87 = (f32[512,640]{1,0:T(8,128)S(1)}, bf16[256,640]{1,0:T(8,128)(2,1)S(1)}, f32[8,256]{1,0:T(8,128)S(1)}) custom-call(f32[2]{0:T(128)S(1)} %pad_maximum_fusion.scal_ref, bf16[512,640]{1,0:T(8,128)(2,1)S(1)} %get-tuple-element.37.zib_ref, bf16[256,640]{1,0:T(8,128)(2,1)S(1)} %collective-permute-done.4.refs_0_, f32[512,640]{1,0:T(8,128)S(1)} %get-tuple-element.39.refs_1_), custom_call_target="tpu_custom_call" | custom-call | flops 251658240 | bytes 4194304 | tf_op jit(solution)/shard_map/pallas_call | solution.py:107
  38.8 0.0 copy-done.4
  38.8 1.7 %collective-permute-done.3.refs_0_ = bf16[256,640]{1,0:T(8,128)(2,1)S(1)} collective-permute-done((bf16[256,640]{1,0:T(8,128)(2,1)}, bf16[256,640]{1,0:T(8,128)(2,1)S(1)}, u32[]{:S(2)}, u32[]{:S(2)}) %collective-permute-start.3) | collective-permute-done | bytes 327712 | tf_op jit(solution)/shard_map/ppermute | solution.py:228
  40.5 1.9 %shard_map.88 = (f32[512,640]{1,0:T(8,128)S(1)}, f32[256,640]{1,0:T(8,128)S(1)}, f32[8,256]{1,0:T(8,128)S(1)}) custom-call(f32[2]{0:T(128)S(1)} %pad_maximum_fusion.scal_ref, bf16[512,640]{1,0:T(8,128)(2,1)S(1)} %get-tuple-element.37.zib_ref, bf16[256,640]{1,0:T(8,128)(2,1)S(1)} %collective-permute-done.3.refs_0_, f32[512,640]{1,0:T(8,128)S(1)} %get-tuple-element.40.refs_1_), custom_call_target="tpu_custom_call" | custom-call | flops 503316480 | bytes 4194304 | tf_op jit(solution)/shard_map/pallas_call | solution.py:107
  42.4 1.6 %collective-permute-done.2.refs_0_ = bf16[256,640]{1,0:T(8,128)(2,1)S(1)} collective-permute-done((bf16[256,640]{1,0:T(8,128)(2,1)S(1)}, bf16[256,640]{1,0:T(8,128)(2,1)S(1)}, u32[]{:S(2)}, u32[]{:S(2)}) %collective-permute-start.2) | collective-permute-done | bytes 327712 | tf_op jit(solution)/shard_map/ppermute | solution.py:231
  44.0 1.9 %shard_map.89 = (f32[512,640]{1,0:T(8,128)S(1)}, f32[256,640]{1,0:T(8,128)S(1)}, f32[8,256]{1,0:T(8,128)S(1)}) custom-call(f32[2]{0:T(128)S(1)} %pad_maximum_fusion.scal_ref, bf16[512,640]{1,0:T(8,128)(2,1)S(1)} %get-tuple-element.37.zib_ref, bf16[256,640]{1,0:T(8,128)(2,1)S(1)} %collective-permute-done.2.refs_0_, f32[512,640]{1,0:T(8,128)S(1)} %get-tuple-element.41.refs_1_), custom_call_target="tpu_custom_call" | custom-call | flops 503316480 | bytes 4194304 | tf_op jit(solution)/shard_map/pallas_call | solution.py:107
  45.9 2.7 %collective-permute-start.6 = (f32[512,640]{1,0:T(8,128)S(1)}, f32[512,640]{1,0:T(8,128)S(1)}, u32[]{:S(2)}, u32[]{:S(2)}) collective-permute-start(f32[512,640]{1,0:T(8,128)S(1)} %get-tuple-element.42.dzi_ref), channel_id=1, source_target_pairs={{0,1},{1,0},{2,3},{3,2},{4,5},{5,4},{6,7},{7,6},{8,9},{9,8},{10,11... | collective-permute-start | bytes 3932168 | tf_op jit(solution)/shard_map/ppermute | solution.py:258
  48.7 2.6 %collective-permute-done.6.sent_ref = f32[512,640]{1,0:T(8,128)S(1)} collective-permute-done((f32[512,640]{1,0:T(8,128)S(1)}, f32[512,640]{1,0:T(8,128)S(1)}, u32[]{:S(2)}, u32[]{:S(2)}) %collective-permute-start.6) | collective-permute-done | bytes 1310752 | tf_op jit(solution)/shard_map/ppermute | solution.py:258
  51.3 1.4 %shard_map.90 = (bf16[256,640]{1,0:T(8,128)(2,1)S(1)}, bf16[3072,128]{1,0:T(8,128)(2,1)S(1)}) custom-call(f32[512,640]{1,0:T(8,128)S(1)} %get-tuple-element.42.dzi_ref, f32[512,640]{1,0:T(8,128)S(1)} %collective-permute-done.6.sent_ref, f32[512,640]{1,0:T(8,128)S(1)} %get-tuple-element.43.zi_ref, f32[512,128]{1,0:T(8,128)S(1)} %get-tuple-element.44.inv_ref, ...), custom_call_target="tpu_custom_call" | custom-call | flops 377487360 | bytes 7340032 | tf_op jit(solution)/shard_map/pallas_call | solution.py:260
  52.8 14.4 %all_to_all.20 = bf16[4,768,128]{2,1,0:T(8,128)(2,1)S(1)} all-to-all(bf16[4,768,128]{2,1,0:T(8,128)(2,1)S(1)} %bitcast.15), channel_id=1, replica_groups=mesh['y'=8,'x'=4,'z'=8,'core'=2] {'x'}, dimensions={0} | all-to-all | bytes 1572864 | tf_op jit(solution)/shard_map/all_to_all | solution.py:276
  67.2 0.8 shard_map.91
  68.0 9.4 %all-to-all-start.1 = ((bf16[64,6,2,128]{3,2,1,0:T(2,128)(2,1)}), bf16[64,6,2,128]{3,2,1,0:T(2,128)(2,1)S(1)}, u32[]{:S(2)}, u32[]{:S(2)}) async-start(bf16[64,6,2,128]{3,2,1,0:T(2,128)(2,1)} %bitcast.4), calls=%async_computation.1 | async-start | bytes 393216 | tf_op jit(solution)/shard_map/all_to_all | solution.py:283
  77.4 7.2 %collective-permute-start.7 = (bf16[256,640]{1,0:T(8,128)(2,1)S(1)}, bf16[256,640]{1,0:T(8,128)(2,1)S(1)}, u32[]{:S(2)}, u32[]{:S(2)}) collective-permute-start(bf16[256,640]{1,0:T(8,128)(2,1)S(1)} %get-tuple-element.58), channel_id=1, source_target_pairs={{510,0},{3,1},{0,2},{5,3},{2,4},{7,5},{4,6},{9,7},{6,8},{11,9},{8,... | collective-permute-start | bytes 983048 | tf_op jit(solution)/shard_map/ppermute | solution.py:281
  84.6 3.1 %collective-permute-start.8 = (bf16[256,640]{1,0:T(8,128)(2,1)S(1)}, bf16[256,640]{1,0:T(8,128)(2,1)S(1)}, u32[]{:S(2)}, u32[]{:S(2)}) collective-permute-start(bf16[256,640]{1,0:T(8,128)(2,1)S(1)} %get-tuple-element.59), channel_id=1, source_target_pairs={{510,0},{3,1},{0,2},{5,3},{2,4},{7,5},{4,6},{9,7},{6,8},{11,9},{8,... | collective-permute-start | bytes 983048 | tf_op jit(solution)/shard_map/ppermute | solution.py:282
  87.7 1.6 %all-to-all-done.1 = bf16[64,6,2,128]{3,2,1,0:T(2,128)(2,1)S(1)} async-done(((bf16[64,6,2,128]{3,2,1,0:T(2,128)(2,1)}), bf16[64,6,2,128]{3,2,1,0:T(2,128)(2,1)S(1)}, u32[]{:S(2)}, u32[]{:S(2)}) %all-to-all-start.1) | async-done | bytes 196640 | tf_op jit(solution)/shard_map/all_to_all | solution.py:283
  89.3 0.9 shard_map.92
  90.2 4.7 %all-to-all-start.2 = ((bf16[64,6,2,128]{3,2,1,0:T(2,128)(2,1)}), bf16[64,6,2,128]{3,2,1,0:T(2,128)(2,1)S(1)}, u32[]{:S(2)}, u32[]{:S(2)}) async-start(bf16[64,6,2,128]{3,2,1,0:T(2,128)(2,1)} %bitcast.6), calls=%async_computation.2 | async-start | bytes 393216 | tf_op jit(solution)/shard_map/all_to_all | solution.py:305
  94.9 0.0 collective-permute-done.7.far_same_ref
  94.9 0.0 collective-permute-done.8.far_other_ref
  94.9 0.1 shard_map.93
  95.0 0.0 copy-start.5
  95.0 7.3 %collective-permute-start.9 = (bf16[256,640]{1,0:T(8,128)(2,1)S(1)}, bf16[256,640]{1,0:T(8,128)(2,1)S(1)}, u32[]{:S(2)}, u32[]{:S(2)}) collective-permute-start(bf16[256,640]{1,0:T(8,128)(2,1)S(1)} %get-tuple-element.62), channel_id=1, source_target_pairs={{510,0},{3,1},{0,2},{5,3},{2,4},{7,5},{4,6},{9,7},{6,8},{11,9},{8,... | collective-permute-start | bytes 983048 | tf_op jit(solution)/shard_map/ppermute | solution.py:303
  102.3 7.2 %collective-permute-start.10 = (bf16[256,640]{1,0:T(8,128)(2,1)S(1)}, bf16[256,640]{1,0:T(8,128)(2,1)S(1)}, u32[]{:S(2)}, u32[]{:S(2)}) collective-permute-start(bf16[256,640]{1,0:T(8,128)(2,1)S(1)} %get-tuple-element.63), channel_id=1, source_target_pairs={{510,1},{3,0},{0,3},{5,2},{2,5},{7,4},{4,7},{9,6},{6,9},{11,8},{8,... | collective-permute-start | bytes 983048 | tf_op jit(solution)/shard_map/ppermute | solution.py:304
  109.5 0.0 all-to-all-done.2
  109.6 1.0 broadcast_in_dim.3
  110.5 3.5 %all-to-all-start.3 = ((bf16[4,768,128]{2,1,0:T(8,128)(2,1)}), bf16[4,768,128]{2,1,0:T(8,128)(2,1)S(1)}, u32[]{:S(2)}, u32[]{:S(2)}) async-start(bf16[4,768,128]{2,1,0:T(8,128)(2,1)} %broadcast_in_dim.3), calls=%async_computation.3 | async-start | bytes 1572864 | tf_op jit(solution)/shard_map/all_to_all | solution.py:314
  114.0 0.0 collective-permute-done.9.same_ref
  114.0 0.0 copy-done.5
  114.1 0.1 shard_map.94.joined_ref
  114.1 0.0 copy-start.1
  114.1 2.0 %collective-permute-done.10.other_ref = bf16[256,640]{1,0:T(8,128)(2,1)S(1)} collective-permute-done((bf16[256,640]{1,0:T(8,128)(2,1)S(1)}, bf16[256,640]{1,0:T(8,128)(2,1)S(1)}, u32[]{:S(2)}, u32[]{:S(2)}) %collective-permute-start.10) | collective-permute-done | bytes 327712 | tf_op jit(solution)/shard_map/ppermute | solution.py:304
  116.2 1.0 shard_map.95
  117.1 0.0 copy-done.1
  117.2 1.5 %convolution_convert_fusion = bf16[256,1152]{1,0:T(8,128)(2,1)} fusion(bf16[256,640]{1,0:T(8,128)(2,1)S(1)} %get-tuple-element.64, bf16[1152,640]{1,0:T(8,128)(2,1)S(1)} %copy-done.1), kind=kOutput, calls=%fused_computation | convolution fusion | flops 377782272 | bytes 2392064 | tf_op jit(solution)/shard_map/dot_general | solution.py:313
  118.6 5.5 %all-to-all-done.3 = bf16[4,768,128]{2,1,0:T(8,128)(2,1)S(1)} async-done(((bf16[4,768,128]{2,1,0:T(8,128)(2,1)}), bf16[4,768,128]{2,1,0:T(8,128)(2,1)S(1)}, u32[]{:S(2)}, u32[]{:S(2)}) %all-to-all-start.3) | async-done | bytes 786464 | tf_op jit(solution)/shard_map/all_to_all | solution.py:314
  124.1 5.0 %collective-permute-start.11 = (bf16[3072,128]{1,0:T(8,128)(2,1)S(1)}, bf16[3072,128]{1,0:T(8,128)(2,1)S(1)}, u32[]{:S(2)}, u32[]{:S(2)}) collective-permute-start(bf16[3072,128]{1,0:T(8,128)(2,1)S(1)} %bitcast.12), channel_id=1, source_target_pairs={{0,1},{1,0},{2,3},{3,2},{4,5},{5,4},{6,7},{7,6},{8,9},{9,8},{10,11... | collective-permute-start | bytes 2359304 | tf_op jit(solution)/shard_map/ppermute | solution.py:316
  129.1 1.9 %collective-permute-done.11.other_ref = bf16[3072,128]{1,0:T(8,128)(2,1)S(1)} collective-permute-done((bf16[3072,128]{1,0:T(8,128)(2,1)S(1)}, bf16[3072,128]{1,0:T(8,128)(2,1)S(1)}, u32[]{:S(2)}, u32[]{:S(2)}) %collective-permute-start.11) | collective-permute-done | bytes 786464 | tf_op jit(solution)/shard_map/ppermute | solution.py:316
  131.0 1.4 %shard_map.96 = (bf16[1152,640]{1,0:T(8,128)(2,1)}, f32[1,1]{1,0:T(1,128)}) custom-call(s32[1]{0:T(128)} %bitcast.core_ref, bf16[3072,128]{1,0:T(8,128)(2,1)S(1)} %bitcast.13, bf16[3072,128]{1,0:T(8,128)(2,1)S(1)} %collective-permute-done.11.other_ref), custom_call_target="tpu_custom_call" | custom-call | flops 1 | bytes 3145728 | tf_op jit(solution)/shard_map/pallas_call | solution.py:318
Async XLA Ops:
  0.6 25.8 %collective-permute-start = (bf16[256,1152]{1,0:T(8,128)(2,1)}, bf16[256,1152]{1,0:T(8,128)(2,1)S(1)}, u32[]{:S(2)}, u32[]{:S(2)}) collective-permute-start(bf16[256,1152]{1,0:T(8,128)(2,1)} %own_ref.1), channel_id=1, source_target_pairs={{0,1},{1,0},{2,3},{3,2},{4,5},{5,4},{6,7},{7,6},{8,9},{9,8},{10,11... | collective-permute-start | bytes 1769480 | tf_op jit(solution)/shard_map/ppermute | solution.py:230
  9.4 3.9 %collective-permute-start.1 = (bf16[256,640]{1,0:T(8,128)(2,1)}, bf16[256,640]{1,0:T(8,128)(2,1)S(1)}, u32[]{:S(2)}, u32[]{:S(2)}) collective-permute-start(bf16[256,640]{1,0:T(8,128)(2,1)} %text_ref.1), channel_id=1, source_target_pairs={{0,1},{1,0},{2,3},{3,2},{4,5},{5,4},{6,7},{7,6},{8,9},{9,8},{10,11... | collective-permute-start | bytes 983048 | tf_op jit(solution)/shard_map/ppermute | solution.py:229
  11.4 20.9 %collective-permute-start.5 = (bf16[256,640]{1,0:T(8,128)(2,1)}, bf16[256,640]{1,0:T(8,128)(2,1)S(1)}, u32[]{:S(2)}, u32[]{:S(2)}) collective-permute-start(bf16[256,640]{1,0:T(8,128)(2,1)} %text_ref.1), channel_id=1, source_target_pairs={{0,508},{1,5},{2,510},{3,7},{4,0},{5,9},{6,2},{7,11},{8,4},{9,13},... | collective-permute-start | bytes 983048 | tf_op jit(solution)/shard_map/ppermute | solution.py:232
  13.3 24.0 %collective-permute-start.4 = (bf16[256,640]{1,0:T(8,128)(2,1)S(1)}, bf16[256,640]{1,0:T(8,128)(2,1)S(1)}, u32[]{:S(2)}, u32[]{:S(2)}) collective-permute-start(bf16[256,640]{1,0:T(8,128)(2,1)S(1)} %collective-permute-done.1), channel_id=1, source_target_pairs={{0,508},{1,5},{2,510},{3,7},{4,0},{5,9},{6,2},{7,11},{8,4},{9,13},... | collective-permute-start | bytes 983048 | tf_op jit(solution)/shard_map/ppermute | solution.py:233
  18.8 21.6 %collective-permute-start.3 = (bf16[256,640]{1,0:T(8,128)(2,1)}, bf16[256,640]{1,0:T(8,128)(2,1)S(1)}, u32[]{:S(2)}, u32[]{:S(2)}) collective-permute-start(bf16[256,640]{1,0:T(8,128)(2,1)} %text_ref.1), channel_id=1, source_target_pairs={{0,510},{1,3},{2,0},{3,5},{4,2},{5,7},{6,4},{7,9},{8,6},{9,11},{10... | collective-permute-start | bytes 983048 | tf_op jit(solution)/shard_map/ppermute | solution.py:228
  23.2 20.7 %collective-permute-start.2 = (bf16[256,640]{1,0:T(8,128)(2,1)S(1)}, bf16[256,640]{1,0:T(8,128)(2,1)S(1)}, u32[]{:S(2)}, u32[]{:S(2)}) collective-permute-start(bf16[256,640]{1,0:T(8,128)(2,1)S(1)} %collective-permute-done.1), channel_id=1, source_target_pairs={{0,510},{1,3},{2,0},{3,5},{4,2},{5,7},{6,4},{7,9},{8,6},{9,11},{10... | collective-permute-start | bytes 983048 | tf_op jit(solution)/shard_map/ppermute | solution.py:231
  26.4 1.4 %copy-start = (bf16[1152,640]{1,0:T(8,128)(2,1)S(1)}, bf16[1152,640]{1,0:T(8,128)(2,1)}, u32[]{:S(2)}) copy-start(bf16[1152,640]{1,0:T(8,128)(2,1)} %weight_ref.1) | copy-start | bytes 4423684
  27.8 1.1 copy-start.3
  28.9 1.4 %copy-start.2 = (bf16[256,640]{1,0:T(8,128)(2,1)S(1)}, bf16[256,640]{1,0:T(8,128)(2,1)}, u32[]{:S(2)}) copy-start(bf16[256,640]{1,0:T(8,128)(2,1)} %text_ref.1) | copy-start | bytes 983044
  32.3 6.5 %copy-start.4 = (f32[256,640]{1,0:T(8,128)}, f32[256,640]{1,0:T(8,128)S(1)}, u32[]{:S(2)}) copy-start(f32[256,640]{1,0:T(8,128)S(1)} %get-tuple-element.57.own_ref) | copy-start | bytes 1966084
  45.9 5.4 %collective-permute-start.6 = (f32[512,640]{1,0:T(8,128)S(1)}, f32[512,640]{1,0:T(8,128)S(1)}, u32[]{:S(2)}, u32[]{:S(2)}) collective-permute-start(f32[512,640]{1,0:T(8,128)S(1)} %get-tuple-element.42.dzi_ref), channel_id=1, source_target_pairs={{0,1},{1,0},{2,3},{3,2},{4,5},{5,4},{6,7},{7,6},{8,9},{9,8},{10,11... | collective-permute-start | bytes 3932168 | tf_op jit(solution)/shard_map/ppermute | solution.py:258
  68.0 21.3 %all-to-all-start.1 = ((bf16[64,6,2,128]{3,2,1,0:T(2,128)(2,1)}), bf16[64,6,2,128]{3,2,1,0:T(2,128)(2,1)S(1)}, u32[]{:S(2)}, u32[]{:S(2)}) async-start(bf16[64,6,2,128]{3,2,1,0:T(2,128)(2,1)} %bitcast.4), calls=%async_computation.1 | async-start | bytes 393216 | tf_op jit(solution)/shard_map/all_to_all | solution.py:283
  77.4 17.4 %collective-permute-start.7 = (bf16[256,640]{1,0:T(8,128)(2,1)S(1)}, bf16[256,640]{1,0:T(8,128)(2,1)S(1)}, u32[]{:S(2)}, u32[]{:S(2)}) collective-permute-start(bf16[256,640]{1,0:T(8,128)(2,1)S(1)} %get-tuple-element.58), channel_id=1, source_target_pairs={{510,0},{3,1},{0,2},{5,3},{2,4},{7,5},{4,6},{9,7},{6,8},{11,9},{8,... | collective-permute-start | bytes 983048 | tf_op jit(solution)/shard_map/ppermute | solution.py:281
  84.6 10.3 %collective-permute-start.8 = (bf16[256,640]{1,0:T(8,128)(2,1)S(1)}, bf16[256,640]{1,0:T(8,128)(2,1)S(1)}, u32[]{:S(2)}, u32[]{:S(2)}) collective-permute-start(bf16[256,640]{1,0:T(8,128)(2,1)S(1)} %get-tuple-element.59), channel_id=1, source_target_pairs={{510,0},{3,1},{0,2},{5,3},{2,4},{7,5},{4,6},{9,7},{6,8},{11,9},{8,... | collective-permute-start | bytes 983048 | tf_op jit(solution)/shard_map/ppermute | solution.py:282
  90.2 19.4 %all-to-all-start.2 = ((bf16[64,6,2,128]{3,2,1,0:T(2,128)(2,1)}), bf16[64,6,2,128]{3,2,1,0:T(2,128)(2,1)S(1)}, u32[]{:S(2)}, u32[]{:S(2)}) async-start(bf16[64,6,2,128]{3,2,1,0:T(2,128)(2,1)} %bitcast.6), calls=%async_computation.2 | async-start | bytes 393216 | tf_op jit(solution)/shard_map/all_to_all | solution.py:305
  95.0 19.1 %copy-start.5 = (f32[256,640]{1,0:T(8,128)S(1)}, f32[256,640]{1,0:T(8,128)}, u32[]{:S(2)}) copy-start(f32[256,640]{1,0:T(8,128)} %copy-done.4) | copy-start | bytes 1966084
  95.0 19.0 %collective-permute-start.9 = (bf16[256,640]{1,0:T(8,128)(2,1)S(1)}, bf16[256,640]{1,0:T(8,128)(2,1)S(1)}, u32[]{:S(2)}, u32[]{:S(2)}) collective-permute-start(bf16[256,640]{1,0:T(8,128)(2,1)S(1)} %get-tuple-element.62), channel_id=1, source_target_pairs={{510,0},{3,1},{0,2},{5,3},{2,4},{7,5},{4,6},{9,7},{6,8},{11,9},{8,... | collective-permute-start | bytes 983048 | tf_op jit(solution)/shard_map/ppermute | solution.py:303
  102.3 13.9 %collective-permute-start.10 = (bf16[256,640]{1,0:T(8,128)(2,1)S(1)}, bf16[256,640]{1,0:T(8,128)(2,1)S(1)}, u32[]{:S(2)}, u32[]{:S(2)}) collective-permute-start(bf16[256,640]{1,0:T(8,128)(2,1)S(1)} %get-tuple-element.63), channel_id=1, source_target_pairs={{510,1},{3,0},{0,3},{5,2},{2,5},{7,4},{4,7},{9,6},{6,9},{11,8},{8,... | collective-permute-start | bytes 983048 | tf_op jit(solution)/shard_map/ppermute | solution.py:304
  110.5 13.6 %all-to-all-start.3 = ((bf16[4,768,128]{2,1,0:T(8,128)(2,1)}), bf16[4,768,128]{2,1,0:T(8,128)(2,1)S(1)}, u32[]{:S(2)}, u32[]{:S(2)}) async-start(bf16[4,768,128]{2,1,0:T(8,128)(2,1)} %broadcast_in_dim.3), calls=%async_computation.3 | async-start | bytes 1572864 | tf_op jit(solution)/shard_map/all_to_all | solution.py:314
  114.1 3.0 %copy-start.1 = (bf16[1152,640]{1,0:T(8,128)(2,1)S(1)}, bf16[1152,640]{1,0:T(8,128)(2,1)}, u32[]{:S(2)}) copy-start(bf16[1152,640]{1,0:T(8,128)(2,1)} %weight_ref.1) | copy-start | bytes 4423684
  124.1 6.9 %collective-permute-start.11 = (bf16[3072,128]{1,0:T(8,128)(2,1)S(1)}, bf16[3072,128]{1,0:T(8,128)(2,1)S(1)}, u32[]{:S(2)}, u32[]{:S(2)}) collective-permute-start(bf16[3072,128]{1,0:T(8,128)(2,1)S(1)} %bitcast.12), channel_id=1, source_target_pairs={{0,1},{1,0},{2,3},{3,2},{4,5},{5,4},{6,7},{7,6},{8,9},{9,8},{10,11... | collective-permute-start | bytes 2359304 | tf_op jit(solution)/shard_map/ppermute | solution.py:316

commit v7 on v6

--- a/solution.py
+++ b/solution.py
@@ -223,14 +223,17 @@
     onward = [(2 * k + b, 2 * ((k + 2 * b - 1) % chips) + b) for k in range(chips) for b in range(2)]
     beyond = [(2 * k + b, 2 * ((k + 4 * b - 2) % chips) + b) for k in range(chips) for b in range(2)]
     back = [(d, s) for s, d in onward]
+
+    def crossing(step):
+        return [(2 * k + b, 2 * ((k + step * (1 - 2 * b)) % chips) + 1 - b) for k in range(chips) for b in range(2)]
+
     scal = jnp.concatenate([logit_scale, logit_bias])
 
     near_same = lax.ppermute(text_embeds, axes, onward)
-    text_other = lax.ppermute(text_embeds, axes, across)
     x_other = lax.ppermute(image_feats, axes, across)
-    near_other = lax.ppermute(text_other, axes, onward)
+    near_other = lax.ppermute(text_embeds, axes, crossing(1))
     far_same = lax.ppermute(text_embeds, axes, beyond)
-    far_other = lax.ppermute(text_other, axes, beyond)
+    far_other = lax.ppermute(text_embeds, axes, crossing(2))
 
     zi, zib, inv_u, x_half = call(
         project_kernel,

time: 135 us -> 133 us (0.985)
  waiting for transfers between devices: 20 us -> 16.2 us
    ppermute x3 -> x2, waiting for transfers between devices: 4.64 us -> 0.01 us  [the longest x1 0.01 us: per_device(): far_other = lax.ppermute(text_embeds, axes, crossing(2))]
    ppermute x3 -> x2, starting transfers between devices: 10.6 us -> 12.7 us  [the longest x1 10.8 us: per_device(): far_other = lax.ppermute(text_embeds, axes, crossing(2))]
  transfers between devices with their start and end apart: 15 -> 14, of which waited for: 8 -> 6; matrix products, arithmetic and copies ran while one was open for 2% -> 2% of each run, Pallas kernels for 8% -> 8%
where the time goes in v7:
time: 133 us; the launch traced here: 132 us
  starting transfers between devices  75.8 us (57%)
  Pallas kernels  16.3 us (12%)
  waiting for transfers between devices  16.2 us (12%)
  blocking collectives  14.5 us (11%)
  between operations  4.03 us (3%)
  local copies, waits for them, and re-layouts  3.44 us (3%)
  matrix products  1.49 us (1%)
    all_to_all x1, blocking collectives, per_device(): along_x = lax.all_to_all(flat.reshape(nx, part, LANES), 'x', 0, 0)  14.5 us
    ppermute x1, starting transfers between devices, per_device(): far_other = lax.ppermute(text_embeds, axes, crossing(2))  10.8 us
    pallas_call x5, Pallas kernels, score(): call(functools.partial(score_kernel, parts, dzi is not None), (jax.ShapeD...  9.27 us
    all_to_all x1, starting transfers between devices, per_device(): lax.all_to_all(summed.reshape(ny * nz, share // 2, 2, LANES), ('y', 'z'),...  9.15 us
    ppermute x1, starting transfers between devices, per_device(): x_other = lax.ppermute(image_feats, axes, across)  8.79 us
    ppermute x1, starting transfers between devices, per_device(): home_same = lax.ppermute(same, axes, back)  7.28 us
    ppermute x1, starting transfers between devices, per_device(): home_other = lax.ppermute(other, axes, [(s, d ^ 1) for s, d in back])  7.24 us
    ppermute x1, starting transfers between devices, per_device(): far_same = lax.ppermute(far_same, axes, back)  7.15 us
  transfers between devices with their start and end apart: 14, of which 6 were waited for; matrix products, arithmetic and copies ran while one was open for 2% of the time, Pallas kernels for 8%

profile of v7, /device:TPU:1, one launch (start us, length us, event | category | flops | bytes accessed | tf_op | source)
XLA Modules:
  0.0 131.8 jit_solution(18370684766277619523)
XLA Ops:
  0.6 8.8 %collective-permute-start = (bf16[256,1152]{1,0:T(8,128)(2,1)}, bf16[256,1152]{1,0:T(8,128)(2,1)S(1)}, u32[]{:S(2)}, u32[]{:S(2)}) collective-permute-start(bf16[256,1152]{1,0:T(8,128)(2,1)} %own_ref.1), channel_id=1, source_target_pairs={{0,1},{1,0},{2,3},{3,2},{4,5},{5,4},{6,7},{7,6},{8,9},{9,8},{10,11... | collective-permute-start | bytes 1769480 | tf_op jit(solution)/shard_map/ppermute | solution.py:233
  9.4 1.9 %collective-permute-start.4 = (bf16[256,640]{1,0:T(8,128)(2,1)}, bf16[256,640]{1,0:T(8,128)(2,1)S(1)}, u32[]{:S(2)}, u32[]{:S(2)}) collective-permute-start(bf16[256,640]{1,0:T(8,128)(2,1)} %text_ref.1), channel_id=1, source_target_pairs={{0,508},{1,5},{2,510},{3,7},{4,0},{5,9},{6,2},{7,11},{8,4},{9,13},... | collective-permute-start | bytes 983048 | tf_op jit(solution)/shard_map/ppermute | solution.py:235
  11.4 10.8 %collective-permute-start.3 = (bf16[256,640]{1,0:T(8,128)(2,1)}, bf16[256,640]{1,0:T(8,128)(2,1)S(1)}, u32[]{:S(2)}, u32[]{:S(2)}) collective-permute-start(bf16[256,640]{1,0:T(8,128)(2,1)} %text_ref.1), channel_id=1, source_target_pairs={{0,5},{1,508},{2,7},{3,510},{4,9},{5,0},{6,11},{7,2},{8,13},{9,4},... | collective-permute-start | bytes 983048 | tf_op jit(solution)/shard_map/ppermute | solution.py:236
  22.2 3.1 %collective-permute-start.2 = (bf16[256,640]{1,0:T(8,128)(2,1)}, bf16[256,640]{1,0:T(8,128)(2,1)S(1)}, u32[]{:S(2)}, u32[]{:S(2)}) collective-permute-start(bf16[256,640]{1,0:T(8,128)(2,1)} %text_ref.1), channel_id=1, source_target_pairs={{0,510},{1,3},{2,0},{3,5},{4,2},{5,7},{6,4},{7,9},{8,6},{9,11},{10... | collective-permute-start | bytes 983048 | tf_op jit(solution)/shard_map/ppermute | solution.py:232
  25.3 1.9 %collective-permute-start.1 = (bf16[256,640]{1,0:T(8,128)(2,1)}, bf16[256,640]{1,0:T(8,128)(2,1)S(1)}, u32[]{:S(2)}, u32[]{:S(2)}) collective-permute-start(bf16[256,640]{1,0:T(8,128)(2,1)} %text_ref.1), channel_id=1, source_target_pairs={{0,3},{1,510},{2,5},{3,0},{4,7},{5,2},{6,9},{7,4},{8,11},{9,6},{10... | collective-permute-start | bytes 983048 | tf_op jit(solution)/shard_map/ppermute | solution.py:234
  28.5 0.1 pad_maximum_fusion.scal_ref
  28.6 0.0 collective-permute-done.other_ref
  28.6 0.0 copy-start
  28.6 1.4 %copy-done = bf16[1152,640]{1,0:T(8,128)(2,1)S(1)} copy-done((bf16[1152,640]{1,0:T(8,128)(2,1)S(1)}, bf16[1152,640]{1,0:T(8,128)(2,1)}, u32[]{:S(2)}) %copy-start) | copy-done | bytes 1474584
  30.0 0.0 copy-start.3
  30.0 1.1 copy-done.3
  31.0 0.0 copy-start.2
  31.0 1.4 %shard_map.84 = (f32[512,640]{1,0:T(8,128)S(1)}, bf16[512,640]{1,0:T(8,128)(2,1)S(1)}, f32[512,128]{1,0:T(8,128)S(1)}, bf16[576,512]{1,0:T(8,128)(2,1)S(1)}) custom-call(s32[1]{0:T(128)} %bitcast.core_ref, bf16[256,1152]{1,0:T(8,128)(2,1)S(1)} %copy-done.3, bf16[256,1152]{1,0:T(8,128)(2,1)S(1)} %collective-permute-done.other_ref, bf16[1152,640]{1,0:T(8,128)(2,1)S(1)} %copy-done), custom_call_target="tpu_custom_call" | custom-call | flops 754974720 | bytes 5242880 | tf_op jit(solution)/shard_map/pallas_call | solution.py:238
  32.4 0.0 copy-done.2
  32.4 2.0 %shard_map.85 = (f32[512,640]{1,0:T(8,128)S(1)}, f32[256,640]{1,0:T(8,128)S(1)}, f32[8,256]{1,0:T(8,128)S(1)}) custom-call(f32[2]{0:T(128)S(1)} %pad_maximum_fusion.scal_ref, bf16[512,640]{1,0:T(8,128)(2,1)S(1)} %get-tuple-element.37.zib_ref, bf16[256,640]{1,0:T(8,128)(2,1)S(1)} %copy-done.2), custom_call_target="tpu_custom_call" | custom-call | flops 503316480 | bytes 4194304 | tf_op jit(solution)/shard_map/pallas_call | solution.py:107
  34.4 0.0 copy-start.4
  34.4 0.0 collective-permute-done.4.refs_0_
  34.4 1.9 %shard_map.86 = (f32[512,640]{1,0:T(8,128)S(1)}, bf16[256,640]{1,0:T(8,128)(2,1)S(1)}, f32[8,256]{1,0:T(8,128)S(1)}) custom-call(f32[2]{0:T(128)S(1)} %pad_maximum_fusion.scal_ref, bf16[512,640]{1,0:T(8,128)(2,1)S(1)} %get-tuple-element.37.zib_ref, bf16[256,640]{1,0:T(8,128)(2,1)S(1)} %collective-permute-done.4.refs_0_, f32[512,640]{1,0:T(8,128)S(1)} %get-tuple-element.38.refs_1_), custom_call_target="tpu_custom_call" | custom-call | flops 503316480 | bytes 4194304 | tf_op jit(solution)/shard_map/pallas_call | solution.py:107
  36.4 0.0 collective-permute-done.3.refs_0_
  36.4 1.5 %shard_map.87 = (f32[512,640]{1,0:T(8,128)S(1)}, bf16[256,640]{1,0:T(8,128)(2,1)S(1)}, f32[8,256]{1,0:T(8,128)S(1)}) custom-call(f32[2]{0:T(128)S(1)} %pad_maximum_fusion.scal_ref, bf16[512,640]{1,0:T(8,128)(2,1)S(1)} %get-tuple-element.37.zib_ref, bf16[256,640]{1,0:T(8,128)(2,1)S(1)} %collective-permute-done.3.refs_0_, f32[512,640]{1,0:T(8,128)S(1)} %get-tuple-element.39.refs_1_), custom_call_target="tpu_custom_call" | custom-call | flops 251658240 | bytes 4194304 | tf_op jit(solution)/shard_map/pallas_call | solution.py:107
  37.9 0.0 copy-done.4
  37.9 2.4 %collective-permute-done.2.refs_0_ = bf16[256,640]{1,0:T(8,128)(2,1)S(1)} collective-permute-done((bf16[256,640]{1,0:T(8,128)(2,1)}, bf16[256,640]{1,0:T(8,128)(2,1)S(1)}, u32[]{:S(2)}, u32[]{:S(2)}) %collective-permute-start.2) | collective-permute-done | bytes 327712 | tf_op jit(solution)/shard_map/ppermute | solution.py:232
  40.3 1.9 %shard_map.88 = (f32[512,640]{1,0:T(8,128)S(1)}, f32[256,640]{1,0:T(8,128)S(1)}, f32[8,256]{1,0:T(8,128)S(1)}) custom-call(f32[2]{0:T(128)S(1)} %pad_maximum_fusion.scal_ref, bf16[512,640]{1,0:T(8,128)(2,1)S(1)} %get-tuple-element.37.zib_ref, bf16[256,640]{1,0:T(8,128)(2,1)S(1)} %collective-permute-done.2.refs_0_, f32[512,640]{1,0:T(8,128)S(1)} %get-tuple-element.40.refs_1_), custom_call_target="tpu_custom_call" | custom-call | flops 503316480 | bytes 4194304 | tf_op jit(solution)/shard_map/pallas_call | solution.py:107
  42.3 0.0 collective-permute-done.1.refs_0_
  42.3 1.9 %shard_map.89 = (f32[512,640]{1,0:T(8,128)S(1)}, f32[256,640]{1,0:T(8,128)S(1)}, f32[8,256]{1,0:T(8,128)S(1)}) custom-call(f32[2]{0:T(128)S(1)} %pad_maximum_fusion.scal_ref, bf16[512,640]{1,0:T(8,128)(2,1)S(1)} %get-tuple-element.37.zib_ref, bf16[256,640]{1,0:T(8,128)(2,1)S(1)} %collective-permute-done.1.refs_0_, f32[512,640]{1,0:T(8,128)S(1)} %get-tuple-element.41.refs_1_), custom_call_target="tpu_custom_call" | custom-call | flops 503316480 | bytes 4194304 | tf_op jit(solution)/shard_map/pallas_call | solution.py:107
  44.2 2.1 %collective-permute-start.5 = (f32[512,640]{1,0:T(8,128)S(1)}, f32[512,640]{1,0:T(8,128)S(1)}, u32[]{:S(2)}, u32[]{:S(2)}) collective-permute-start(f32[512,640]{1,0:T(8,128)S(1)} %get-tuple-element.42.dzi_ref), channel_id=1, source_target_pairs={{0,1},{1,0},{2,3},{3,2},{4,5},{5,4},{6,7},{7,6},{8,9},{9,8},{10,11... | collective-permute-start | bytes 3932168 | tf_op jit(solution)/shard_map/ppermute | solution.py:261
  46.4 2.8 %collective-permute-done.5.sent_ref = f32[512,640]{1,0:T(8,128)S(1)} collective-permute-done((f32[512,640]{1,0:T(8,128)S(1)}, f32[512,640]{1,0:T(8,128)S(1)}, u32[]{:S(2)}, u32[]{:S(2)}) %collective-permute-start.5) | collective-permute-done | bytes 1310752 | tf_op jit(solution)/shard_map/ppermute | solution.py:261
  49.1 1.4 %shard_map.90 = (bf16[256,640]{1,0:T(8,128)(2,1)S(1)}, bf16[3072,128]{1,0:T(8,128)(2,1)S(1)}) custom-call(f32[512,640]{1,0:T(8,128)S(1)} %get-tuple-element.42.dzi_ref, f32[512,640]{1,0:T(8,128)S(1)} %collective-permute-done.5.sent_ref, f32[512,640]{1,0:T(8,128)S(1)} %get-tuple-element.43.zi_ref, f32[512,128]{1,0:T(8,128)S(1)} %get-tuple-element.44.inv_ref, ...), custom_call_target="tpu_custom_call" | custom-call | flops 377487360 | bytes 7340032 | tf_op jit(solution)/shard_map/pallas_call | solution.py:263
  50.6 14.5 %all_to_all.20 = bf16[4,768,128]{2,1,0:T(8,128)(2,1)S(1)} all-to-all(bf16[4,768,128]{2,1,0:T(8,128)(2,1)S(1)} %bitcast.15), channel_id=1, replica_groups=mesh['y'=8,'x'=4,'z'=8,'core'=2] {'x'}, dimensions={0} | all-to-all | bytes 1572864 | tf_op jit(solution)/shard_map/all_to_all | solution.py:279
  65.1 0.8 shard_map.91
  65.9 9.1 %all-to-all-start.1 = ((bf16[64,6,2,128]{3,2,1,0:T(2,128)(2,1)}), bf16[64,6,2,128]{3,2,1,0:T(2,128)(2,1)S(1)}, u32[]{:S(2)}, u32[]{:S(2)}) async-start(bf16[64,6,2,128]{3,2,1,0:T(2,128)(2,1)} %bitcast.4), calls=%async_computation.1 | async-start | bytes 393216 | tf_op jit(solution)/shard_map/all_to_all | solution.py:286
  75.0 7.2 %collective-permute-start.6 = (bf16[256,640]{1,0:T(8,128)(2,1)S(1)}, bf16[256,640]{1,0:T(8,128)(2,1)S(1)}, u32[]{:S(2)}, u32[]{:S(2)}) collective-permute-start(bf16[256,640]{1,0:T(8,128)(2,1)S(1)} %get-tuple-element.58), channel_id=1, source_target_pairs={{510,0},{3,1},{0,2},{5,3},{2,4},{7,5},{4,6},{9,7},{6,8},{11,9},{8,... | collective-permute-start | bytes 983048 | tf_op jit(solution)/shard_map/ppermute | solution.py:284
  82.2 3.1 %collective-permute-start.7 = (bf16[256,640]{1,0:T(8,128)(2,1)S(1)}, bf16[256,640]{1,0:T(8,128)(2,1)S(1)}, u32[]{:S(2)}, u32[]{:S(2)}) collective-permute-start(bf16[256,640]{1,0:T(8,128)(2,1)S(1)} %get-tuple-element.59), channel_id=1, source_target_pairs={{510,0},{3,1},{0,2},{5,3},{2,4},{7,5},{4,6},{9,7},{6,8},{11,9},{8,... | collective-permute-start | bytes 983048 | tf_op jit(solution)/shard_map/ppermute | solution.py:285
  85.3 1.6 %all-to-all-done.1 = bf16[64,6,2,128]{3,2,1,0:T(2,128)(2,1)S(1)} async-done(((bf16[64,6,2,128]{3,2,1,0:T(2,128)(2,1)}), bf16[64,6,2,128]{3,2,1,0:T(2,128)(2,1)S(1)}, u32[]{:S(2)}, u32[]{:S(2)}) %all-to-all-start.1) | async-done | bytes 196640 | tf_op jit(solution)/shard_map/all_to_all | solution.py:286
  86.9 0.9 shard_map.92
  87.8 4.7 %all-to-all-start.2 = ((bf16[64,6,2,128]{3,2,1,0:T(2,128)(2,1)}), bf16[64,6,2,128]{3,2,1,0:T(2,128)(2,1)S(1)}, u32[]{:S(2)}, u32[]{:S(2)}) async-start(bf16[64,6,2,128]{3,2,1,0:T(2,128)(2,1)} %bitcast.6), calls=%async_computation.2 | async-start | bytes 393216 | tf_op jit(solution)/shard_map/all_to_all | solution.py:308
  92.4 0.0 collective-permute-done.6.far_same_ref
  92.5 0.0 collective-permute-done.7.far_other_ref
  92.5 0.1 shard_map.93
  92.6 0.0 copy-start.5
  92.6 7.3 %collective-permute-start.8 = (bf16[256,640]{1,0:T(8,128)(2,1)S(1)}, bf16[256,640]{1,0:T(8,128)(2,1)S(1)}, u32[]{:S(2)}, u32[]{:S(2)}) collective-permute-start(bf16[256,640]{1,0:T(8,128)(2,1)S(1)} %get-tuple-element.62), channel_id=1, source_target_pairs={{510,0},{3,1},{0,2},{5,3},{2,4},{7,5},{4,6},{9,7},{6,8},{11,9},{8,... | collective-permute-start | bytes 983048 | tf_op jit(solution)/shard_map/ppermute | solution.py:306
  99.9 7.2 %collective-permute-start.9 = (bf16[256,640]{1,0:T(8,128)(2,1)S(1)}, bf16[256,640]{1,0:T(8,128)(2,1)S(1)}, u32[]{:S(2)}, u32[]{:S(2)}) collective-permute-start(bf16[256,640]{1,0:T(8,128)(2,1)S(1)} %get-tuple-element.63), channel_id=1, source_target_pairs={{510,1},{3,0},{0,3},{5,2},{2,5},{7,4},{4,7},{9,6},{6,9},{11,8},{8,... | collective-permute-start | bytes 983048 | tf_op jit(solution)/shard_map/ppermute | solution.py:307
  107.1 0.0 all-to-all-done.2
  107.1 1.0 broadcast_in_dim.3
  108.1 3.5 %all-to-all-start.3 = ((bf16[4,768,128]{2,1,0:T(8,128)(2,1)}), bf16[4,768,128]{2,1,0:T(8,128)(2,1)S(1)}, u32[]{:S(2)}, u32[]{:S(2)}) async-start(bf16[4,768,128]{2,1,0:T(8,128)(2,1)} %broadcast_in_dim.3), calls=%async_computation.3 | async-start | bytes 1572864 | tf_op jit(solution)/shard_map/all_to_all | solution.py:317
  111.6 0.0 collective-permute-done.8.same_ref
  111.6 0.0 copy-done.5
  111.6 0.1 shard_map.94.joined_ref
  111.7 0.0 copy-start.1
  111.7 2.0 %collective-permute-done.9.other_ref = bf16[256,640]{1,0:T(8,128)(2,1)S(1)} collective-permute-done((bf16[256,640]{1,0:T(8,128)(2,1)S(1)}, bf16[256,640]{1,0:T(8,128)(2,1)S(1)}, u32[]{:S(2)}, u32[]{:S(2)}) %collective-permute-start.9) | collective-permute-done | bytes 327712 | tf_op jit(solution)/shard_map/ppermute | solution.py:307
  113.8 1.0 shard_map.95
  114.7 0.0 copy-done.1
  114.7 1.5 %convolution_convert_fusion = bf16[256,1152]{1,0:T(8,128)(2,1)} fusion(bf16[256,640]{1,0:T(8,128)(2,1)S(1)} %get-tuple-element.64, bf16[1152,640]{1,0:T(8,128)(2,1)S(1)} %copy-done.1), kind=kOutput, calls=%fused_computation | convolution fusion | flops 377782272 | bytes 2392064 | tf_op jit(solution)/shard_map/dot_general | solution.py:316
  116.2 5.5 %all-to-all-done.3 = bf16[4,768,128]{2,1,0:T(8,128)(2,1)S(1)} async-done(((bf16[4,768,128]{2,1,0:T(8,128)(2,1)}), bf16[4,768,128]{2,1,0:T(8,128)(2,1)S(1)}, u32[]{:S(2)}, u32[]{:S(2)}) %all-to-all-start.3) | async-done | bytes 786464 | tf_op jit(solution)/shard_map/all_to_all | solution.py:317
  121.7 5.0 %collective-permute-start.10 = (bf16[3072,128]{1,0:T(8,128)(2,1)S(1)}, bf16[3072,128]{1,0:T(8,128)(2,1)S(1)}, u32[]{:S(2)}, u32[]{:S(2)}) collective-permute-start(bf16[3072,128]{1,0:T(8,128)(2,1)S(1)} %bitcast.12), channel_id=1, source_target_pairs={{0,1},{1,0},{2,3},{3,2},{4,5},{5,4},{6,7},{7,6},{8,9},{9,8},{10,11... | collective-permute-start | bytes 2359304 | tf_op jit(solution)/shard_map/ppermute | solution.py:319
  126.7 1.9 %collective-permute-done.10.other_ref = bf16[3072,128]{1,0:T(8,128)(2,1)S(1)} collective-permute-done((bf16[3072,128]{1,0:T(8,128)(2,1)S(1)}, bf16[3072,128]{1,0:T(8,128)(2,1)S(1)}, u32[]{:S(2)}, u32[]{:S(2)}) %collective-permute-start.10) | collective-permute-done | bytes 786464 | tf_op jit(solution)/shard_map/ppermute | solution.py:319
  128.6 1.4 %shard_map.96 = (bf16[1152,640]{1,0:T(8,128)(2,1)}, f32[1,1]{1,0:T(1,128)}) custom-call(s32[1]{0:T(128)} %bitcast.core_ref, bf16[3072,128]{1,0:T(8,128)(2,1)S(1)} %bitcast.13, bf16[3072,128]{1,0:T(8,128)(2,1)S(1)} %collective-permute-done.10.other_ref), custom_call_target="tpu_custom_call" | custom-call | flops 1 | bytes 3145728 | tf_op jit(solution)/shard_map/pallas_call | solution.py:321
Async XLA Ops:
  0.6 28.0 %collective-permute-start = (bf16[256,1152]{1,0:T(8,128)(2,1)}, bf16[256,1152]{1,0:T(8,128)(2,1)S(1)}, u32[]{:S(2)}, u32[]{:S(2)}) collective-permute-start(bf16[256,1152]{1,0:T(8,128)(2,1)} %own_ref.1), channel_id=1, source_target_pairs={{0,1},{1,0},{2,3},{3,2},{4,5},{5,4},{6,7},{7,6},{8,9},{9,8},{10,11... | collective-permute-start | bytes 1769480 | tf_op jit(solution)/shard_map/ppermute | solution.py:233
  9.4 25.0 %collective-permute-start.4 = (bf16[256,640]{1,0:T(8,128)(2,1)}, bf16[256,640]{1,0:T(8,128)(2,1)S(1)}, u32[]{:S(2)}, u32[]{:S(2)}) collective-permute-start(bf16[256,640]{1,0:T(8,128)(2,1)} %text_ref.1), channel_id=1, source_target_pairs={{0,508},{1,5},{2,510},{3,7},{4,0},{5,9},{6,2},{7,11},{8,4},{9,13},... | collective-permute-start | bytes 983048 | tf_op jit(solution)/shard_map/ppermute | solution.py:235
  11.4 25.0 %collective-permute-start.3 = (bf16[256,640]{1,0:T(8,128)(2,1)}, bf16[256,640]{1,0:T(8,128)(2,1)S(1)}, u32[]{:S(2)}, u32[]{:S(2)}) collective-permute-start(bf16[256,640]{1,0:T(8,128)(2,1)} %text_ref.1), channel_id=1, source_target_pairs={{0,5},{1,508},{2,7},{3,510},{4,9},{5,0},{6,11},{7,2},{8,13},{9,4},... | collective-permute-start | bytes 983048 | tf_op jit(solution)/shard_map/ppermute | solution.py:236
  22.2 18.1 %collective-permute-start.2 = (bf16[256,640]{1,0:T(8,128)(2,1)}, bf16[256,640]{1,0:T(8,128)(2,1)S(1)}, u32[]{:S(2)}, u32[]{:S(2)}) collective-permute-start(bf16[256,640]{1,0:T(8,128)(2,1)} %text_ref.1), channel_id=1, source_target_pairs={{0,510},{1,3},{2,0},{3,5},{4,2},{5,7},{6,4},{7,9},{8,6},{9,11},{10... | collective-permute-start | bytes 983048 | tf_op jit(solution)/shard_map/ppermute | solution.py:232
  25.3 17.0 %collective-permute-start.1 = (bf16[256,640]{1,0:T(8,128)(2,1)}, bf16[256,640]{1,0:T(8,128)(2,1)S(1)}, u32[]{:S(2)}, u32[]{:S(2)}) collective-permute-start(bf16[256,640]{1,0:T(8,128)(2,1)} %text_ref.1), channel_id=1, source_target_pairs={{0,3},{1,510},{2,5},{3,0},{4,7},{5,2},{6,9},{7,4},{8,11},{9,6},{10... | collective-permute-start | bytes 983048 | tf_op jit(solution)/shard_map/ppermute | solution.py:234
  28.6 1.4 %copy-start = (bf16[1152,640]{1,0:T(8,128)(2,1)S(1)}, bf16[1152,640]{1,0:T(8,128)(2,1)}, u32[]{:S(2)}) copy-start(bf16[1152,640]{1,0:T(8,128)(2,1)} %weight_ref.1) | copy-start | bytes 4423684
  30.0 1.1 copy-start.3
  31.0 1.4 %copy-start.2 = (bf16[256,640]{1,0:T(8,128)(2,1)S(1)}, bf16[256,640]{1,0:T(8,128)(2,1)}, u32[]{:S(2)}) copy-start(bf16[256,640]{1,0:T(8,128)(2,1)} %text_ref.1) | copy-start | bytes 983044
  34.4 3.5 %copy-start.4 = (f32[256,640]{1,0:T(8,128)}, f32[256,640]{1,0:T(8,128)S(1)}, u32[]{:S(2)}) copy-start(f32[256,640]{1,0:T(8,128)S(1)} %get-tuple-element.57.own_ref) | copy-start | bytes 1966084
  44.2 4.9 %collective-permute-start.5 = (f32[512,640]{1,0:T(8,128)S(1)}, f32[512,640]{1,0:T(8,128)S(1)}, u32[]{:S(2)}, u32[]{:S(2)}) collective-permute-start(f32[512,640]{1,0:T(8,128)S(1)} %get-tuple-element.42.dzi_ref), channel_id=1, source_target_pairs={{0,1},{1,0},{2,3},{3,2},{4,5},{5,4},{6,7},{7,6},{8,9},{9,8},{10,11... | collective-permute-start | bytes 3932168 | tf_op jit(solution)/shard_map/ppermute | solution.py:261
  65.9 21.0 %all-to-all-start.1 = ((bf16[64,6,2,128]{3,2,1,0:T(2,128)(2,1)}), bf16[64,6,2,128]{3,2,1,0:T(2,128)(2,1)S(1)}, u32[]{:S(2)}, u32[]{:S(2)}) async-start(bf16[64,6,2,128]{3,2,1,0:T(2,128)(2,1)} %bitcast.4), calls=%async_computation.1 | async-start | bytes 393216 | tf_op jit(solution)/shard_map/all_to_all | solution.py:286
  75.0 17.4 %collective-permute-start.6 = (bf16[256,640]{1,0:T(8,128)(2,1)S(1)}, bf16[256,640]{1,0:T(8,128)(2,1)S(1)}, u32[]{:S(2)}, u32[]{:S(2)}) collective-permute-start(bf16[256,640]{1,0:T(8,128)(2,1)S(1)} %get-tuple-element.58), channel_id=1, source_target_pairs={{510,0},{3,1},{0,2},{5,3},{2,4},{7,5},{4,6},{9,7},{6,8},{11,9},{8,... | collective-permute-start | bytes 983048 | tf_op jit(solution)/shard_map/ppermute | solution.py:284
  82.2 10.3 %collective-permute-start.7 = (bf16[256,640]{1,0:T(8,128)(2,1)S(1)}, bf16[256,640]{1,0:T(8,128)(2,1)S(1)}, u32[]{:S(2)}, u32[]{:S(2)}) collective-permute-start(bf16[256,640]{1,0:T(8,128)(2,1)S(1)} %get-tuple-element.59), channel_id=1, source_target_pairs={{510,0},{3,1},{0,2},{5,3},{2,4},{7,5},{4,6},{9,7},{6,8},{11,9},{8,... | collective-permute-start | bytes 983048 | tf_op jit(solution)/shard_map/ppermute | solution.py:285
  87.8 19.4 %all-to-all-start.2 = ((bf16[64,6,2,128]{3,2,1,0:T(2,128)(2,1)}), bf16[64,6,2,128]{3,2,1,0:T(2,128)(2,1)S(1)}, u32[]{:S(2)}, u32[]{:S(2)}) async-start(bf16[64,6,2,128]{3,2,1,0:T(2,128)(2,1)} %bitcast.6), calls=%async_computation.2 | async-start | bytes 393216 | tf_op jit(solution)/shard_map/all_to_all | solution.py:308
  92.6 19.1 %copy-start.5 = (f32[256,640]{1,0:T(8,128)S(1)}, f32[256,640]{1,0:T(8,128)}, u32[]{:S(2)}) copy-start(f32[256,640]{1,0:T(8,128)} %copy-done.4) | copy-start | bytes 1966084
  92.6 19.0 %collective-permute-start.8 = (bf16[256,640]{1,0:T(8,128)(2,1)S(1)}, bf16[256,640]{1,0:T(8,128)(2,1)S(1)}, u32[]{:S(2)}, u32[]{:S(2)}) collective-permute-start(bf16[256,640]{1,0:T(8,128)(2,1)S(1)} %get-tuple-element.62), channel_id=1, source_target_pairs={{510,0},{3,1},{0,2},{5,3},{2,4},{7,5},{4,6},{9,7},{6,8},{11,9},{8,... | collective-permute-start | bytes 983048 | tf_op jit(solution)/shard_map/ppermute | solution.py:306
  99.9 13.9 %collective-permute-start.9 = (bf16[256,640]{1,0:T(8,128)(2,1)S(1)}, bf16[256,640]{1,0:T(8,128)(2,1)S(1)}, u32[]{:S(2)}, u32[]{:S(2)}) collective-permute-start(bf16[256,640]{1,0:T(8,128)(2,1)S(1)} %get-tuple-element.63), channel_id=1, source_target_pairs={{510,1},{3,0},{0,3},{5,2},{2,5},{7,4},{4,7},{9,6},{6,9},{11,8},{8,... | collective-permute-start | bytes 983048 | tf_op jit(solution)/shard_map/ppermute | solution.py:307
  108.1 13.6 %all-to-all-start.3 = ((bf16[4,768,128]{2,1,0:T(8,128)(2,1)}), bf16[4,768,128]{2,1,0:T(8,128)(2,1)S(1)}, u32[]{:S(2)}, u32[]{:S(2)}) async-start(bf16[4,768,128]{2,1,0:T(8,128)(2,1)} %broadcast_in_dim.3), calls=%async_computation.3 | async-start | bytes 1572864 | tf_op jit(solution)/shard_map/all_to_all | solution.py:317
  111.7 3.0 %copy-start.1 = (bf16[1152,640]{1,0:T(8,128)(2,1)S(1)}, bf16[1152,640]{1,0:T(8,128)(2,1)}, u32[]{:S(2)}) copy-start(bf16[1152,640]{1,0:T(8,128)(2,1)} %weight_ref.1) | copy-start | bytes 4423684
  121.7 6.9 %collective-permute-start.10 = (bf16[3072,128]{1,0:T(8,128)(2,1)S(1)}, bf16[3072,128]{1,0:T(8,128)(2,1)S(1)}, u32[]{:S(2)}, u32[]{:S(2)}) collective-permute-start(bf16[3072,128]{1,0:T(8,128)(2,1)S(1)} %bitcast.12), channel_id=1, source_target_pairs={{0,1},{1,0},{2,3},{3,2},{4,5},{5,4},{6,7},{7,6},{8,9},{9,8},{10,11... | collective-permute-start | bytes 2359304 | tf_op jit(solution)/shard_map/ppermute | solution.py:319

commit v8 on v7

--- a/solution.py
+++ b/solution.py
@@ -254,10 +254,10 @@
     both = 2 * ROWS
     whole = (0, both, False)
     dzi, dzt0, loss0 = score([(0, both, True)], scal, zib, [text_embeds], None, F32)
+    dzi, far_other, loss2 = score([(ROWS, both, False)], scal, zib, [far_other], dzi, BF)
     dzi, far_same, loss1 = score([whole], scal, zib, [far_same], dzi, BF)
-    dzi, far_other, loss2 = score([(ROWS, both, False)], scal, zib, [far_other], dzi, BF)
+    dzi, near_other, loss4 = score([whole], scal, zib, [near_other], dzi, F32)
     dzi, near_same, loss3 = score([whole], scal, zib, [near_same], dzi, F32)
-    dzi, near_other, loss4 = score([whole], scal, zib, [near_other], dzi, F32)
     dzi_sent = lax.ppermute(dzi, axes, across)
 
     du, flat = call(

time: 133 us -> 132 us (level)
    all_to_all x1, starting transfers between devices: 9.15 us -> 5.87 us  [per_device(): lax.all_to_all(summed.reshape(ny * nz, share // 2, 2, LANES), ('y', 'z'),...]
    ppermute x1, starting transfers between devices: 1.92 us -> 4.94 us  [per_device(): near_other = lax.ppermute(text_embeds, axes, crossing(1))]
    ppermute x1, waiting for transfers between devices: 0.01 us -> 2.68 us  [per_device(): near_other = lax.ppermute(text_embeds, axes, crossing(1))]
    ppermute x1, waiting for transfers between devices: 2.42 us -> 0.01 us  [per_device(): near_same = lax.ppermute(text_embeds, axes, onward)]
  transfers between devices with their start and end apart: 14 -> 14, of which waited for: 6 -> 7; matrix products, arithmetic and copies ran while one was open for 2% -> 2% of each run, Pallas kernels for 8% -> 8%
where the time goes in v8:
time: 132 us; the launch traced here: 131 us
  starting transfers between devices  74.5 us (56%)
  waiting for transfers between devices  17.1 us (13%)
  Pallas kernels  16.3 us (12%)
  blocking collectives  14.4 us (11%)
  between operations  4.02 us (3%)
  local copies, waits for them, and re-layouts  3.44 us (3%)
  matrix products  1.49 us (1%)
    all_to_all x1, blocking collectives, per_device(): along_x = lax.all_to_all(flat.reshape(nx, part, LANES), 'x', 0, 0)  14.4 us
    ppermute x1, starting transfers between devices, per_device(): far_other = lax.ppermute(text_embeds, axes, crossing(2))  10.3 us
    pallas_call x5, Pallas kernels, score(): call(functools.partial(score_kernel, parts, dzi is not None), (jax.ShapeD...  9.27 us
    ppermute x1, starting transfers between devices, per_device(): x_other = lax.ppermute(image_feats, axes, across)  8.79 us
    ppermute x1, starting transfers between devices, per_device(): home_same = lax.ppermute(same, axes, back)  7.29 us
    ppermute x1, starting transfers between devices, per_device(): far_same = lax.ppermute(far_same, axes, back)  7.16 us
    ppermute x1, starting transfers between devices, per_device(): home_other = lax.ppermute(other, axes, [(s, d ^ 1) for s, d in back])  7.01 us
    all_to_all x1, starting transfers between devices, per_device(): lax.all_to_all(summed.reshape(ny * nz, share // 2, 2, LANES), ('y', 'z'),...  5.87 us
  transfers between devices with their start and end apart: 14, of which 7 were waited for; matrix products, arithmetic and copies ran while one was open for 2% of the time, Pallas kernels for 8%

profile of v8, /device:TPU:1, one launch (start us, length us, event | category | flops | bytes accessed | tf_op | source)
XLA Modules:
  0.0 131.3 jit_solution(14645450637195036153)
XLA Ops:
  0.6 8.8 %collective-permute-start = (bf16[256,1152]{1,0:T(8,128)(2,1)}, bf16[256,1152]{1,0:T(8,128)(2,1)S(1)}, u32[]{:S(2)}, u32[]{:S(2)}) collective-permute-start(bf16[256,1152]{1,0:T(8,128)(2,1)} %own_ref.1), channel_id=1, source_target_pairs={{0,1},{1,0},{2,3},{3,2},{4,5},{5,4},{6,7},{7,6},{8,9},{9,8},{10,11... | collective-permute-start | bytes 1769480 | tf_op jit(solution)/shard_map/ppermute | solution.py:233
  9.4 10.3 %collective-permute-start.4 = (bf16[256,640]{1,0:T(8,128)(2,1)}, bf16[256,640]{1,0:T(8,128)(2,1)S(1)}, u32[]{:S(2)}, u32[]{:S(2)}) collective-permute-start(bf16[256,640]{1,0:T(8,128)(2,1)} %text_ref.1), channel_id=1, source_target_pairs={{0,5},{1,508},{2,7},{3,510},{4,9},{5,0},{6,11},{7,2},{8,13},{9,4},... | collective-permute-start | bytes 983048 | tf_op jit(solution)/shard_map/ppermute | solution.py:236
  19.7 1.9 %collective-permute-start.3 = (bf16[256,640]{1,0:T(8,128)(2,1)}, bf16[256,640]{1,0:T(8,128)(2,1)S(1)}, u32[]{:S(2)}, u32[]{:S(2)}) collective-permute-start(bf16[256,640]{1,0:T(8,128)(2,1)} %text_ref.1), channel_id=1, source_target_pairs={{0,508},{1,5},{2,510},{3,7},{4,0},{5,9},{6,2},{7,11},{8,4},{9,13},... | collective-permute-start | bytes 983048 | tf_op jit(solution)/shard_map/ppermute | solution.py:235
  21.6 4.9 %collective-permute-start.2 = (bf16[256,640]{1,0:T(8,128)(2,1)}, bf16[256,640]{1,0:T(8,128)(2,1)S(1)}, u32[]{:S(2)}, u32[]{:S(2)}) collective-permute-start(bf16[256,640]{1,0:T(8,128)(2,1)} %text_ref.1), channel_id=1, source_target_pairs={{0,3},{1,510},{2,5},{3,0},{4,7},{5,2},{6,9},{7,4},{8,11},{9,6},{10... | collective-permute-start | bytes 983048 | tf_op jit(solution)/shard_map/ppermute | solution.py:234
  26.6 1.9 %collective-permute-start.1 = (bf16[256,640]{1,0:T(8,128)(2,1)}, bf16[256,640]{1,0:T(8,128)(2,1)S(1)}, u32[]{:S(2)}, u32[]{:S(2)}) collective-permute-start(bf16[256,640]{1,0:T(8,128)(2,1)} %text_ref.1), channel_id=1, source_target_pairs={{0,510},{1,3},{2,0},{3,5},{4,2},{5,7},{6,4},{7,9},{8,6},{9,11},{10... | collective-permute-start | bytes 983048 | tf_op jit(solution)/shard_map/ppermute | solution.py:232
  29.8 0.1 pad_maximum_fusion.scal_ref
  29.9 0.0 collective-permute-done.other_ref
  29.9 0.0 copy-start
  29.9 1.4 %copy-done = bf16[1152,640]{1,0:T(8,128)(2,1)S(1)} copy-done((bf16[1152,640]{1,0:T(8,128)(2,1)S(1)}, bf16[1152,640]{1,0:T(8,128)(2,1)}, u32[]{:S(2)}) %copy-start) | copy-done | bytes 1474584
  31.3 0.0 copy-start.3
  31.3 1.1 copy-done.3
  32.3 0.0 copy-start.2
  32.3 1.4 %shard_map.84 = (f32[512,640]{1,0:T(8,128)S(1)}, bf16[512,640]{1,0:T(8,128)(2,1)S(1)}, f32[512,128]{1,0:T(8,128)S(1)}, bf16[576,512]{1,0:T(8,128)(2,1)S(1)}) custom-call(s32[1]{0:T(128)} %bitcast.core_ref, bf16[256,1152]{1,0:T(8,128)(2,1)S(1)} %copy-done.3, bf16[256,1152]{1,0:T(8,128)(2,1)S(1)} %collective-permute-done.other_ref, bf16[1152,640]{1,0:T(8,128)(2,1)S(1)} %copy-done), custom_call_target="tpu_custom_call" | custom-call | flops 754974720 | bytes 5242880 | tf_op jit(solution)/shard_map/pallas_call | solution.py:238
  33.7 0.0 copy-done.2
  33.7 2.0 %shard_map.85 = (f32[512,640]{1,0:T(8,128)S(1)}, f32[256,640]{1,0:T(8,128)S(1)}, f32[8,256]{1,0:T(8,128)S(1)}) custom-call(f32[2]{0:T(128)S(1)} %pad_maximum_fusion.scal_ref, bf16[512,640]{1,0:T(8,128)(2,1)S(1)} %get-tuple-element.37.zib_ref, bf16[256,640]{1,0:T(8,128)(2,1)S(1)} %copy-done.2), custom_call_target="tpu_custom_call" | custom-call | flops 503316480 | bytes 4194304 | tf_op jit(solution)/shard_map/pallas_call | solution.py:107
  35.7 0.0 copy-start.4
  35.7 0.0 collective-permute-done.4.refs_0_
  35.7 1.5 %shard_map.86 = (f32[512,640]{1,0:T(8,128)S(1)}, bf16[256,640]{1,0:T(8,128)(2,1)S(1)}, f32[8,256]{1,0:T(8,128)S(1)}) custom-call(f32[2]{0:T(128)S(1)} %pad_maximum_fusion.scal_ref, bf16[512,640]{1,0:T(8,128)(2,1)S(1)} %get-tuple-element.37.zib_ref, bf16[256,640]{1,0:T(8,128)(2,1)S(1)} %collective-permute-done.4.refs_0_, f32[512,640]{1,0:T(8,128)S(1)} %get-tuple-element.38.refs_1_), custom_call_target="tpu_custom_call" | custom-call | flops 251658240 | bytes 4194304 | tf_op jit(solution)/shard_map/pallas_call | solution.py:107
  37.2 0.9 collective-permute-done.3.refs_0_
  38.1 2.0 %shard_map.87 = (f32[512,640]{1,0:T(8,128)S(1)}, bf16[256,640]{1,0:T(8,128)(2,1)S(1)}, f32[8,256]{1,0:T(8,128)S(1)}) custom-call(f32[2]{0:T(128)S(1)} %pad_maximum_fusion.scal_ref, bf16[512,640]{1,0:T(8,128)(2,1)S(1)} %get-tuple-element.37.zib_ref, bf16[256,640]{1,0:T(8,128)(2,1)S(1)} %collective-permute-done.3.refs_0_, f32[512,640]{1,0:T(8,128)S(1)} %get-tuple-element.39.refs_1_), custom_call_target="tpu_custom_call" | custom-call | flops 503316480 | bytes 4194304 | tf_op jit(solution)/shard_map/pallas_call | solution.py:107
  40.1 0.0 copy-done.4
  40.1 2.7 %collective-permute-done.2.refs_0_ = bf16[256,640]{1,0:T(8,128)(2,1)S(1)} collective-permute-done((bf16[256,640]{1,0:T(8,128)(2,1)}, bf16[256,640]{1,0:T(8,128)(2,1)S(1)}, u32[]{:S(2)}, u32[]{:S(2)}) %collective-permute-start.2) | collective-permute-done | bytes 327712 | tf_op jit(solution)/shard_map/ppermute | solution.py:234
  42.8 1.9 %shard_map.88 = (f32[512,640]{1,0:T(8,128)S(1)}, f32[256,640]{1,0:T(8,128)S(1)}, f32[8,256]{1,0:T(8,128)S(1)}) custom-call(f32[2]{0:T(128)S(1)} %pad_maximum_fusion.scal_ref, bf16[512,640]{1,0:T(8,128)(2,1)S(1)} %get-tuple-element.37.zib_ref, bf16[256,640]{1,0:T(8,128)(2,1)S(1)} %collective-permute-done.2.refs_0_, f32[512,640]{1,0:T(8,128)S(1)} %get-tuple-element.40.refs_1_), custom_call_target="tpu_custom_call" | custom-call | flops 503316480 | bytes 4194304 | tf_op jit(solution)/shard_map/pallas_call | solution.py:107
  44.7 0.0 collective-permute-done.1.refs_0_
  44.7 1.9 %shard_map.89 = (f32[512,640]{1,0:T(8,128)S(1)}, f32[256,640]{1,0:T(8,128)S(1)}, f32[8,256]{1,0:T(8,128)S(1)}) custom-call(f32[2]{0:T(128)S(1)} %pad_maximum_fusion.scal_ref, bf16[512,640]{1,0:T(8,128)(2,1)S(1)} %get-tuple-element.37.zib_ref, bf16[256,640]{1,0:T(8,128)(2,1)S(1)} %collective-permute-done.1.refs_0_, f32[512,640]{1,0:T(8,128)S(1)} %get-tuple-element.41.refs_1_), custom_call_target="tpu_custom_call" | custom-call | flops 503316480 | bytes 4194304 | tf_op jit(solution)/shard_map/pallas_call | solution.py:107
  46.7 2.9 %collective-permute-start.5 = (f32[512,640]{1,0:T(8,128)S(1)}, f32[512,640]{1,0:T(8,128)S(1)}, u32[]{:S(2)}, u32[]{:S(2)}) collective-permute-start(f32[512,640]{1,0:T(8,128)S(1)} %get-tuple-element.42.dzi_ref), channel_id=1, source_target_pairs={{0,1},{1,0},{2,3},{3,2},{4,5},{5,4},{6,7},{7,6},{8,9},{9,8},{10,11... | collective-permute-start | bytes 3932168 | tf_op jit(solution)/shard_map/ppermute | solution.py:261
  49.6 2.6 %collective-permute-done.5.sent_ref = f32[512,640]{1,0:T(8,128)S(1)} collective-permute-done((f32[512,640]{1,0:T(8,128)S(1)}, f32[512,640]{1,0:T(8,128)S(1)}, u32[]{:S(2)}, u32[]{:S(2)}) %collective-permute-start.5) | collective-permute-done | bytes 1310752 | tf_op jit(solution)/shard_map/ppermute | solution.py:261
  52.2 1.4 %shard_map.90 = (bf16[256,640]{1,0:T(8,128)(2,1)S(1)}, bf16[3072,128]{1,0:T(8,128)(2,1)S(1)}) custom-call(f32[512,640]{1,0:T(8,128)S(1)} %get-tuple-element.42.dzi_ref, f32[512,640]{1,0:T(8,128)S(1)} %collective-permute-done.5.sent_ref, f32[512,640]{1,0:T(8,128)S(1)} %get-tuple-element.43.zi_ref, f32[512,128]{1,0:T(8,128)S(1)} %get-tuple-element.44.inv_ref, ...), custom_call_target="tpu_custom_call" | custom-call | flops 377487360 | bytes 7340032 | tf_op jit(solution)/shard_map/pallas_call | solution.py:263
  53.6 14.4 %all_to_all.20 = bf16[4,768,128]{2,1,0:T(8,128)(2,1)S(1)} all-to-all(bf16[4,768,128]{2,1,0:T(8,128)(2,1)S(1)} %bitcast.15), channel_id=1, replica_groups=mesh['y'=8,'x'=4,'z'=8,'core'=2] {'x'}, dimensions={0} | all-to-all | bytes 1572864 | tf_op jit(solution)/shard_map/all_to_all | solution.py:279
  68.1 0.8 shard_map.91
  68.9 5.9 %all-to-all-start.1 = ((bf16[64,6,2,128]{3,2,1,0:T(2,128)(2,1)}), bf16[64,6,2,128]{3,2,1,0:T(2,128)(2,1)S(1)}, u32[]{:S(2)}, u32[]{:S(2)}) async-start(bf16[64,6,2,128]{3,2,1,0:T(2,128)(2,1)} %bitcast.4), calls=%async_computation.1 | async-start | bytes 393216 | tf_op jit(solution)/shard_map/all_to_all | solution.py:286
  74.7 7.2 %collective-permute-start.6 = (bf16[256,640]{1,0:T(8,128)(2,1)S(1)}, bf16[256,640]{1,0:T(8,128)(2,1)S(1)}, u32[]{:S(2)}, u32[]{:S(2)}) collective-permute-start(bf16[256,640]{1,0:T(8,128)(2,1)S(1)} %get-tuple-element.58), channel_id=1, source_target_pairs={{510,0},{3,1},{0,2},{5,3},{2,4},{7,5},{4,6},{9,7},{6,8},{11,9},{8,... | collective-permute-start | bytes 983048 | tf_op jit(solution)/shard_map/ppermute | solution.py:284
  81.9 3.1 %collective-permute-start.7 = (bf16[256,640]{1,0:T(8,128)(2,1)S(1)}, bf16[256,640]{1,0:T(8,128)(2,1)S(1)}, u32[]{:S(2)}, u32[]{:S(2)}) collective-permute-start(bf16[256,640]{1,0:T(8,128)(2,1)S(1)} %get-tuple-element.59), channel_id=1, source_target_pairs={{510,0},{3,1},{0,2},{5,3},{2,4},{7,5},{4,6},{9,7},{6,8},{11,9},{8,... | collective-permute-start | bytes 983048 | tf_op jit(solution)/shard_map/ppermute | solution.py:285
  85.0 1.6 %all-to-all-done.1 = bf16[64,6,2,128]{3,2,1,0:T(2,128)(2,1)S(1)} async-done(((bf16[64,6,2,128]{3,2,1,0:T(2,128)(2,1)}), bf16[64,6,2,128]{3,2,1,0:T(2,128)(2,1)S(1)}, u32[]{:S(2)}, u32[]{:S(2)}) %all-to-all-start.1) | async-done | bytes 196640 | tf_op jit(solution)/shard_map/all_to_all | solution.py:286
  86.6 0.9 shard_map.92
  87.5 4.7 %all-to-all-start.2 = ((bf16[64,6,2,128]{3,2,1,0:T(2,128)(2,1)}), bf16[64,6,2,128]{3,2,1,0:T(2,128)(2,1)S(1)}, u32[]{:S(2)}, u32[]{:S(2)}) async-start(bf16[64,6,2,128]{3,2,1,0:T(2,128)(2,1)} %bitcast.6), calls=%async_computation.2 | async-start | bytes 393216 | tf_op jit(solution)/shard_map/all_to_all | solution.py:308
  92.2 0.0 collective-permute-done.6.far_same_ref
  92.2 0.0 collective-permute-done.7.far_other_ref
  92.2 0.1 shard_map.93
  92.3 0.0 copy-start.5
  92.3 7.3 %collective-permute-start.8 = (bf16[256,640]{1,0:T(8,128)(2,1)S(1)}, bf16[256,640]{1,0:T(8,128)(2,1)S(1)}, u32[]{:S(2)}, u32[]{:S(2)}) collective-permute-start(bf16[256,640]{1,0:T(8,128)(2,1)S(1)} %get-tuple-element.62), channel_id=1, source_target_pairs={{510,0},{3,1},{0,2},{5,3},{2,4},{7,5},{4,6},{9,7},{6,8},{11,9},{8,... | collective-permute-start | bytes 983048 | tf_op jit(solution)/shard_map/ppermute | solution.py:306
  99.6 7.0 %collective-permute-start.9 = (bf16[256,640]{1,0:T(8,128)(2,1)S(1)}, bf16[256,640]{1,0:T(8,128)(2,1)S(1)}, u32[]{:S(2)}, u32[]{:S(2)}) collective-permute-start(bf16[256,640]{1,0:T(8,128)(2,1)S(1)} %get-tuple-element.63), channel_id=1, source_target_pairs={{510,1},{3,0},{0,3},{5,2},{2,5},{7,4},{4,7},{9,6},{6,9},{11,8},{8,... | collective-permute-start | bytes 983048 | tf_op jit(solution)/shard_map/ppermute | solution.py:307
  106.6 0.0 all-to-all-done.2
  106.6 1.0 broadcast_in_dim.3
  107.6 3.5 %all-to-all-start.3 = ((bf16[4,768,128]{2,1,0:T(8,128)(2,1)}), bf16[4,768,128]{2,1,0:T(8,128)(2,1)S(1)}, u32[]{:S(2)}, u32[]{:S(2)}) async-start(bf16[4,768,128]{2,1,0:T(8,128)(2,1)} %broadcast_in_dim.3), calls=%async_computation.3 | async-start | bytes 1572864 | tf_op jit(solution)/shard_map/all_to_all | solution.py:317
  111.1 0.0 collective-permute-done.8.same_ref
  111.1 0.0 copy-done.5
  111.2 0.1 shard_map.94.joined_ref
  111.2 0.0 copy-start.1
  111.2 2.2 %collective-permute-done.9.other_ref = bf16[256,640]{1,0:T(8,128)(2,1)S(1)} collective-permute-done((bf16[256,640]{1,0:T(8,128)(2,1)S(1)}, bf16[256,640]{1,0:T(8,128)(2,1)S(1)}, u32[]{:S(2)}, u32[]{:S(2)}) %collective-permute-start.9) | collective-permute-done | bytes 327712 | tf_op jit(solution)/shard_map/ppermute | solution.py:307
  113.4 1.0 shard_map.95
  114.4 0.0 copy-done.1
  114.4 1.5 %convolution_convert_fusion = bf16[256,1152]{1,0:T(8,128)(2,1)} fusion(bf16[256,640]{1,0:T(8,128)(2,1)S(1)} %get-tuple-element.64, bf16[1152,640]{1,0:T(8,128)(2,1)S(1)} %copy-done.1), kind=kOutput, calls=%fused_computation | convolution fusion | flops 377782272 | bytes 2392064 | tf_op jit(solution)/shard_map/dot_general | solution.py:316
  115.9 5.2 %all-to-all-done.3 = bf16[4,768,128]{2,1,0:T(8,128)(2,1)S(1)} async-done(((bf16[4,768,128]{2,1,0:T(8,128)(2,1)}), bf16[4,768,128]{2,1,0:T(8,128)(2,1)S(1)}, u32[]{:S(2)}, u32[]{:S(2)}) %all-to-all-start.3) | async-done | bytes 786464 | tf_op jit(solution)/shard_map/all_to_all | solution.py:317
  121.1 5.2 %collective-permute-start.10 = (bf16[3072,128]{1,0:T(8,128)(2,1)S(1)}, bf16[3072,128]{1,0:T(8,128)(2,1)S(1)}, u32[]{:S(2)}, u32[]{:S(2)}) collective-permute-start(bf16[3072,128]{1,0:T(8,128)(2,1)S(1)} %bitcast.12), channel_id=1, source_target_pairs={{0,1},{1,0},{2,3},{3,2},{4,5},{5,4},{6,7},{7,6},{8,9},{9,8},{10,11... | collective-permute-start | bytes 2359304 | tf_op jit(solution)/shard_map/ppermute | solution.py:319
  126.2 1.9 %collective-permute-done.10.other_ref = bf16[3072,128]{1,0:T(8,128)(2,1)S(1)} collective-permute-done((bf16[3072,128]{1,0:T(8,128)(2,1)S(1)}, bf16[3072,128]{1,0:T(8,128)(2,1)S(1)}, u32[]{:S(2)}, u32[]{:S(2)}) %collective-permute-start.10) | collective-permute-done | bytes 786464 | tf_op jit(solution)/shard_map/ppermute | solution.py:319
  128.1 1.4 %shard_map.96 = (bf16[1152,640]{1,0:T(8,128)(2,1)}, f32[1,1]{1,0:T(1,128)}) custom-call(s32[1]{0:T(128)} %bitcast.core_ref, bf16[3072,128]{1,0:T(8,128)(2,1)S(1)} %bitcast.13, bf16[3072,128]{1,0:T(8,128)(2,1)S(1)} %collective-permute-done.10.other_ref), custom_call_target="tpu_custom_call" | custom-call | flops 1 | bytes 3145728 | tf_op jit(solution)/shard_map/pallas_call | solution.py:321
Async XLA Ops:
  0.6 29.3 %collective-permute-start = (bf16[256,1152]{1,0:T(8,128)(2,1)}, bf16[256,1152]{1,0:T(8,128)(2,1)S(1)}, u32[]{:S(2)}, u32[]{:S(2)}) collective-permute-start(bf16[256,1152]{1,0:T(8,128)(2,1)} %own_ref.1), channel_id=1, source_target_pairs={{0,1},{1,0},{2,3},{3,2},{4,5},{5,4},{6,7},{7,6},{8,9},{9,8},{10,11... | collective-permute-start | bytes 1769480 | tf_op jit(solution)/shard_map/ppermute | solution.py:233
  9.4 26.3 %collective-permute-start.4 = (bf16[256,640]{1,0:T(8,128)(2,1)}, bf16[256,640]{1,0:T(8,128)(2,1)S(1)}, u32[]{:S(2)}, u32[]{:S(2)}) collective-permute-start(bf16[256,640]{1,0:T(8,128)(2,1)} %text_ref.1), channel_id=1, source_target_pairs={{0,5},{1,508},{2,7},{3,510},{4,9},{5,0},{6,11},{7,2},{8,13},{9,4},... | collective-permute-start | bytes 983048 | tf_op jit(solution)/shard_map/ppermute | solution.py:236
  19.7 18.4 %collective-permute-start.3 = (bf16[256,640]{1,0:T(8,128)(2,1)}, bf16[256,640]{1,0:T(8,128)(2,1)S(1)}, u32[]{:S(2)}, u32[]{:S(2)}) collective-permute-start(bf16[256,640]{1,0:T(8,128)(2,1)} %text_ref.1), channel_id=1, source_target_pairs={{0,508},{1,5},{2,510},{3,7},{4,0},{5,9},{6,2},{7,11},{8,4},{9,13},... | collective-permute-start | bytes 983048 | tf_op jit(solution)/shard_map/ppermute | solution.py:235
  21.6 21.1 %collective-permute-start.2 = (bf16[256,640]{1,0:T(8,128)(2,1)}, bf16[256,640]{1,0:T(8,128)(2,1)S(1)}, u32[]{:S(2)}, u32[]{:S(2)}) collective-permute-start(bf16[256,640]{1,0:T(8,128)(2,1)} %text_ref.1), channel_id=1, source_target_pairs={{0,3},{1,510},{2,5},{3,0},{4,7},{5,2},{6,9},{7,4},{8,11},{9,6},{10... | collective-permute-start | bytes 983048 | tf_op jit(solution)/shard_map/ppermute | solution.py:234
  26.6 18.1 %collective-permute-start.1 = (bf16[256,640]{1,0:T(8,128)(2,1)}, bf16[256,640]{1,0:T(8,128)(2,1)S(1)}, u32[]{:S(2)}, u32[]{:S(2)}) collective-permute-start(bf16[256,640]{1,0:T(8,128)(2,1)} %text_ref.1), channel_id=1, source_target_pairs={{0,510},{1,3},{2,0},{3,5},{4,2},{5,7},{6,4},{7,9},{8,6},{9,11},{10... | collective-permute-start | bytes 983048 | tf_op jit(solution)/shard_map/ppermute | solution.py:232
  29.9 1.4 %copy-start = (bf16[1152,640]{1,0:T(8,128)(2,1)S(1)}, bf16[1152,640]{1,0:T(8,128)(2,1)}, u32[]{:S(2)}) copy-start(bf16[1152,640]{1,0:T(8,128)(2,1)} %weight_ref.1) | copy-start | bytes 4423684
  31.3 1.1 copy-start.3
  32.3 1.4 %copy-start.2 = (bf16[256,640]{1,0:T(8,128)(2,1)S(1)}, bf16[256,640]{1,0:T(8,128)(2,1)}, u32[]{:S(2)}) copy-start(bf16[256,640]{1,0:T(8,128)(2,1)} %text_ref.1) | copy-start | bytes 983044
  35.7 4.4 %copy-start.4 = (f32[256,640]{1,0:T(8,128)}, f32[256,640]{1,0:T(8,128)S(1)}, u32[]{:S(2)}) copy-start(f32[256,640]{1,0:T(8,128)S(1)} %get-tuple-element.57.own_ref) | copy-start | bytes 1966084
  46.7 5.5 %collective-permute-start.5 = (f32[512,640]{1,0:T(8,128)S(1)}, f32[512,640]{1,0:T(8,128)S(1)}, u32[]{:S(2)}, u32[]{:S(2)}) collective-permute-start(f32[512,640]{1,0:T(8,128)S(1)} %get-tuple-element.42.dzi_ref), channel_id=1, source_target_pairs={{0,1},{1,0},{2,3},{3,2},{4,5},{5,4},{6,7},{7,6},{8,9},{9,8},{10,11... | collective-permute-start | bytes 3932168 | tf_op jit(solution)/shard_map/ppermute | solution.py:261
  68.9 17.7 %all-to-all-start.1 = ((bf16[64,6,2,128]{3,2,1,0:T(2,128)(2,1)}), bf16[64,6,2,128]{3,2,1,0:T(2,128)(2,1)S(1)}, u32[]{:S(2)}, u32[]{:S(2)}) async-start(bf16[64,6,2,128]{3,2,1,0:T(2,128)(2,1)} %bitcast.4), calls=%async_computation.1 | async-start | bytes 393216 | tf_op jit(solution)/shard_map/all_to_all | solution.py:286
  74.7 17.4 %collective-permute-start.6 = (bf16[256,640]{1,0:T(8,128)(2,1)S(1)}, bf16[256,640]{1,0:T(8,128)(2,1)S(1)}, u32[]{:S(2)}, u32[]{:S(2)}) collective-permute-start(bf16[256,640]{1,0:T(8,128)(2,1)S(1)} %get-tuple-element.58), channel_id=1, source_target_pairs={{510,0},{3,1},{0,2},{5,3},{2,4},{7,5},{4,6},{9,7},{6,8},{11,9},{8,... | collective-permute-start | bytes 983048 | tf_op jit(solution)/shard_map/ppermute | solution.py:284
  81.9 10.3 %collective-permute-start.7 = (bf16[256,640]{1,0:T(8,128)(2,1)S(1)}, bf16[256,640]{1,0:T(8,128)(2,1)S(1)}, u32[]{:S(2)}, u32[]{:S(2)}) collective-permute-start(bf16[256,640]{1,0:T(8,128)(2,1)S(1)} %get-tuple-element.59), channel_id=1, source_target_pairs={{510,0},{3,1},{0,2},{5,3},{2,4},{7,5},{4,6},{9,7},{6,8},{11,9},{8,... | collective-permute-start | bytes 983048 | tf_op jit(solution)/shard_map/ppermute | solution.py:285
  87.5 19.2 %all-to-all-start.2 = ((bf16[64,6,2,128]{3,2,1,0:T(2,128)(2,1)}), bf16[64,6,2,128]{3,2,1,0:T(2,128)(2,1)S(1)}, u32[]{:S(2)}, u32[]{:S(2)}) async-start(bf16[64,6,2,128]{3,2,1,0:T(2,128)(2,1)} %bitcast.6), calls=%async_computation.2 | async-start | bytes 393216 | tf_op jit(solution)/shard_map/all_to_all | solution.py:308
  92.3 18.8 %copy-start.5 = (f32[256,640]{1,0:T(8,128)S(1)}, f32[256,640]{1,0:T(8,128)}, u32[]{:S(2)}) copy-start(f32[256,640]{1,0:T(8,128)} %copy-done.4) | copy-start | bytes 1966084
  92.3 18.8 %collective-permute-start.8 = (bf16[256,640]{1,0:T(8,128)(2,1)S(1)}, bf16[256,640]{1,0:T(8,128)(2,1)S(1)}, u32[]{:S(2)}, u32[]{:S(2)}) collective-permute-start(bf16[256,640]{1,0:T(8,128)(2,1)S(1)} %get-tuple-element.62), channel_id=1, source_target_pairs={{510,0},{3,1},{0,2},{5,3},{2,4},{7,5},{4,6},{9,7},{6,8},{11,9},{8,... | collective-permute-start | bytes 983048 | tf_op jit(solution)/shard_map/ppermute | solution.py:306
  99.6 13.8 %collective-permute-start.9 = (bf16[256,640]{1,0:T(8,128)(2,1)S(1)}, bf16[256,640]{1,0:T(8,128)(2,1)S(1)}, u32[]{:S(2)}, u32[]{:S(2)}) collective-permute-start(bf16[256,640]{1,0:T(8,128)(2,1)S(1)} %get-tuple-element.63), channel_id=1, source_target_pairs={{510,1},{3,0},{0,3},{5,2},{2,5},{7,4},{4,7},{9,6},{6,9},{11,8},{8,... | collective-permute-start | bytes 983048 | tf_op jit(solution)/shard_map/ppermute | solution.py:307
  107.6 13.5 %all-to-all-start.3 = ((bf16[4,768,128]{2,1,0:T(8,128)(2,1)}), bf16[4,768,128]{2,1,0:T(8,128)(2,1)S(1)}, u32[]{:S(2)}, u32[]{:S(2)}) async-start(bf16[4,768,128]{2,1,0:T(8,128)(2,1)} %broadcast_in_dim.3), calls=%async_computation.3 | async-start | bytes 1572864 | tf_op jit(solution)/shard_map/all_to_all | solution.py:317
  111.2 3.2 %copy-start.1 = (bf16[1152,640]{1,0:T(8,128)(2,1)S(1)}, bf16[1152,640]{1,0:T(8,128)(2,1)}, u32[]{:S(2)}) copy-start(bf16[1152,640]{1,0:T(8,128)(2,1)} %weight_ref.1) | copy-start | bytes 4423684
  121.1 7.1 %collective-permute-start.10 = (bf16[3072,128]{1,0:T(8,128)(2,1)S(1)}, bf16[3072,128]{1,0:T(8,128)(2,1)S(1)}, u32[]{:S(2)}, u32[]{:S(2)}) collective-permute-start(bf16[3072,128]{1,0:T(8,128)(2,1)S(1)} %bitcast.12), channel_id=1, source_target_pairs={{0,1},{1,0},{2,3},{3,2},{4,5},{5,4},{6,7},{7,6},{8,9},{9,8},{10,11... | collective-permute-start | bytes 2359304 | tf_op jit(solution)/shard_map/ppermute | solution.py:319

commit v9 on v8

--- a/solution.py
+++ b/solution.py
@@ -254,9 +254,8 @@
     both = 2 * ROWS
     whole = (0, both, False)
     dzi, dzt0, loss0 = score([(0, both, True)], scal, zib, [text_embeds], None, F32)
-    dzi, far_other, loss2 = score([(ROWS, both, False)], scal, zib, [far_other], dzi, BF)
-    dzi, far_same, loss1 = score([whole], scal, zib, [far_same], dzi, BF)
-    dzi, near_other, loss4 = score([whole], scal, zib, [near_other], dzi, F32)
+    dzi, far_same, far_other, loss1 = score([whole, (ROWS, both, False)], scal, zib, [far_same, far_other], dzi, BF)
+    dzi, near_other, loss2 = score([whole], scal, zib, [near_other], dzi, F32)
     dzi, near_same, loss3 = score([whole], scal, zib, [near_same], dzi, F32)
     dzi_sent = lax.ppermute(dzi, axes, across)
 
@@ -267,12 +266,12 @@
             jax.ShapeDtypeStruct((FLAT, LANES), BF),
         ),
         0,
-        10,
+        9,
         (VMEM, VMEM),
         scratch=(pltpu.VMEM((2 * ROWS, E), BF),),
         flops=2 * 2 * ROWS * HALF * E,
         bytes_accessed=7 << 20,
-    )(dzi, dzi_sent, zi, inv_u, x_half, loss0, loss1, loss2, loss3, loss4)
+    )(dzi, dzi_sent, zi, inv_u, x_half, loss0, loss1, loss2, loss3)
 
     part = FLAT // nx
     share = FLAT // chips

time: 132 us -> 133 us (level)
    pallas_call x5 -> x4, Pallas kernels: 9.27 us -> 8.41 us  [score(): call(functools.partial(score_kernel, parts, dzi is not None), (jax.ShapeD...]
  transfers between devices with their start and end apart: 14 -> 14, of which waited for: 7 -> 7; matrix products, arithmetic and copies ran while one was open for 2% -> 2% of each run, Pallas kernels for 8% -> 7%
where the time goes in v9:
time: 133 us; the launch traced here: 132 us
  starting transfers between devices  74.9 us (56%)
  waiting for transfers between devices  17.3 us (13%)
  Pallas kernels  15.4 us (12%)
  blocking collectives  14.4 us (11%)
  local copies, waits for them, and re-layouts  4.27 us (3%)
  between operations  3.92 us (3%)
  matrix products  1.49 us (1%)
    all_to_all x1, blocking collectives, per_device(): along_x = lax.all_to_all(flat.reshape(nx, part, LANES), 'x', 0, 0)  14.4 us
    ppermute x1, starting transfers between devices, per_device(): far_other = lax.ppermute(text_embeds, axes, crossing(2))  10.3 us
    ppermute x1, starting transfers between devices, per_device(): x_other = lax.ppermute(image_feats, axes, across)  8.79 us
    pallas_call x4, Pallas kernels, score(): call(functools.partial(score_kernel, parts, dzi is not None), (jax.ShapeD...  8.41 us
    ppermute x1, starting transfers between devices, per_device(): home_same = lax.ppermute(same, axes, back)  7.28 us
    ppermute x1, starting transfers between devices, per_device(): home_other = lax.ppermute(other, axes, [(s, d ^ 1) for s, d in back])  7.24 us
    ppermute x1, starting transfers between devices, per_device(): far_same = lax.ppermute(far_same, axes, back)  7.15 us
    all_to_all x1, starting transfers between devices, per_device(): lax.all_to_all(summed.reshape(ny * nz, share // 2, 2, LANES), ('y', 'z'),...  6.31 us
  transfers between devices with their start and end apart: 14, of which 7 were waited for; matrix products, arithmetic and copies ran while one was open for 2% of the time, Pallas kernels for 7%

profile of v9, /device:TPU:1, one launch (start us, length us, event | category | flops | bytes accessed | tf_op | source)
XLA Modules:
  0.0 131.9 jit_solution(11629466716596574829)
XLA Ops:
  0.6 8.8 %collective-permute-start = (bf16[256,1152]{1,0:T(8,128)(2,1)}, bf16[256,1152]{1,0:T(8,128)(2,1)S(1)}, u32[]{:S(2)}, u32[]{:S(2)}) collective-permute-start(bf16[256,1152]{1,0:T(8,128)(2,1)} %own_ref.1), channel_id=1, source_target_pairs={{0,1},{1,0},{2,3},{3,2},{4,5},{5,4},{6,7},{7,6},{8,9},{9,8},{10,11... | collective-permute-start | bytes 1769480 | tf_op jit(solution)/shard_map/ppermute | solution.py:233
  9.4 10.3 %collective-permute-start.4 = (bf16[256,640]{1,0:T(8,128)(2,1)}, bf16[256,640]{1,0:T(8,128)(2,1)S(1)}, u32[]{:S(2)}, u32[]{:S(2)}) collective-permute-start(bf16[256,640]{1,0:T(8,128)(2,1)} %text_ref.1), channel_id=1, source_target_pairs={{0,5},{1,508},{2,7},{3,510},{4,9},{5,0},{6,11},{7,2},{8,13},{9,4},... | collective-permute-start | bytes 983048 | tf_op jit(solution)/shard_map/ppermute | solution.py:236
  19.7 1.9 %collective-permute-start.3 = (bf16[256,640]{1,0:T(8,128)(2,1)}, bf16[256,640]{1,0:T(8,128)(2,1)S(1)}, u32[]{:S(2)}, u32[]{:S(2)}) collective-permute-start(bf16[256,640]{1,0:T(8,128)(2,1)} %text_ref.1), channel_id=1, source_target_pairs={{0,508},{1,5},{2,510},{3,7},{4,0},{5,9},{6,2},{7,11},{8,4},{9,13},... | collective-permute-start | bytes 983048 | tf_op jit(solution)/shard_map/ppermute | solution.py:235
  21.6 4.9 %collective-permute-start.2 = (bf16[256,640]{1,0:T(8,128)(2,1)}, bf16[256,640]{1,0:T(8,128)(2,1)S(1)}, u32[]{:S(2)}, u32[]{:S(2)}) collective-permute-start(bf16[256,640]{1,0:T(8,128)(2,1)} %text_ref.1), channel_id=1, source_target_pairs={{0,3},{1,510},{2,5},{3,0},{4,7},{5,2},{6,9},{7,4},{8,11},{9,6},{10... | collective-permute-start | bytes 983048 | tf_op jit(solution)/shard_map/ppermute | solution.py:234
  26.6 1.9 %collective-permute-start.1 = (bf16[256,640]{1,0:T(8,128)(2,1)}, bf16[256,640]{1,0:T(8,128)(2,1)S(1)}, u32[]{:S(2)}, u32[]{:S(2)}) collective-permute-start(bf16[256,640]{1,0:T(8,128)(2,1)} %text_ref.1), channel_id=1, source_target_pairs={{0,510},{1,3},{2,0},{3,5},{4,2},{5,7},{6,4},{7,9},{8,6},{9,11},{10... | collective-permute-start | bytes 983048 | tf_op jit(solution)/shard_map/ppermute | solution.py:232
  29.8 0.1 pad_maximum_fusion.scal_ref
  29.9 0.0 collective-permute-done.other_ref
  29.9 0.0 copy-start
  29.9 1.4 %copy-done = bf16[1152,640]{1,0:T(8,128)(2,1)S(1)} copy-done((bf16[1152,640]{1,0:T(8,128)(2,1)S(1)}, bf16[1152,640]{1,0:T(8,128)(2,1)}, u32[]{:S(2)}) %copy-start) | copy-done | bytes 1474584
  31.3 0.0 copy-start.3
  31.3 1.1 copy-done.3
  32.3 0.0 copy-start.2
  32.3 1.4 %shard_map.84 = (f32[512,640]{1,0:T(8,128)S(1)}, bf16[512,640]{1,0:T(8,128)(2,1)S(1)}, f32[512,128]{1,0:T(8,128)S(1)}, bf16[576,512]{1,0:T(8,128)(2,1)S(1)}) custom-call(s32[1]{0:T(128)} %bitcast.core_ref, bf16[256,1152]{1,0:T(8,128)(2,1)S(1)} %copy-done.3, bf16[256,1152]{1,0:T(8,128)(2,1)S(1)} %collective-permute-done.other_ref, bf16[1152,640]{1,0:T(8,128)(2,1)S(1)} %copy-done), custom_call_target="tpu_custom_call" | custom-call | flops 754974720 | bytes 5242880 | tf_op jit(solution)/shard_map/pallas_call | solution.py:238
  33.7 0.0 copy-done.2
  33.7 2.0 %shard_map.85 = (f32[512,640]{1,0:T(8,128)S(1)}, f32[256,640]{1,0:T(8,128)S(1)}, f32[8,256]{1,0:T(8,128)S(1)}) custom-call(f32[2]{0:T(128)S(1)} %pad_maximum_fusion.scal_ref, bf16[512,640]{1,0:T(8,128)(2,1)S(1)} %get-tuple-element.35.zib_ref, bf16[256,640]{1,0:T(8,128)(2,1)S(1)} %copy-done.2), custom_call_target="tpu_custom_call" | custom-call | flops 503316480 | bytes 4194304 | tf_op jit(solution)/shard_map/pallas_call | solution.py:107
  35.7 0.0 copy-start.4
  35.7 0.8 copy-done.4
  36.6 0.0 collective-permute-done.4.refs_1_
  36.6 1.5 %collective-permute-done.3.refs_0_ = bf16[256,640]{1,0:T(8,128)(2,1)S(1)} collective-permute-done((bf16[256,640]{1,0:T(8,128)(2,1)}, bf16[256,640]{1,0:T(8,128)(2,1)S(1)}, u32[]{:S(2)}, u32[]{:S(2)}) %collective-permute-start.3) | collective-permute-done | bytes 327712 | tf_op jit(solution)/shard_map/ppermute | solution.py:235
  38.1 2.6 %shard_map.86 = (f32[512,640]{1,0:T(8,128)S(1)}, bf16[256,640]{1,0:T(8,128)(2,1)S(1)}, bf16[256,640]{1,0:T(8,128)(2,1)S(1)}, f32[8,256]{1,0:T(8,128)S(1)}) custom-call(f32[2]{0:T(128)S(1)} %pad_maximum_fusion.scal_ref, bf16[512,640]{1,0:T(8,128)(2,1)S(1)} %get-tuple-element.35.zib_ref, bf16[256,640]{1,0:T(8,128)(2,1)S(1)} %collective-permute-done.3.refs_0_, ...), custom_call_target="tpu_custom_call" | custom-call | flops 754974720 | bytes 4194304 | tf_op jit(solution)/shard_map/pallas_call | solution.py:107
  40.7 2.1 %collective-permute-done.2.refs_0_ = bf16[256,640]{1,0:T(8,128)(2,1)S(1)} collective-permute-done((bf16[256,640]{1,0:T(8,128)(2,1)}, bf16[256,640]{1,0:T(8,128)(2,1)S(1)}, u32[]{:S(2)}, u32[]{:S(2)}) %collective-permute-start.2) | collective-permute-done | bytes 327712 | tf_op jit(solution)/shard_map/ppermute | solution.py:234
  42.8 1.9 %shard_map.87 = (f32[512,640]{1,0:T(8,128)S(1)}, f32[256,640]{1,0:T(8,128)S(1)}, f32[8,256]{1,0:T(8,128)S(1)}) custom-call(f32[2]{0:T(128)S(1)} %pad_maximum_fusion.scal_ref, bf16[512,640]{1,0:T(8,128)(2,1)S(1)} %get-tuple-element.35.zib_ref, bf16[256,640]{1,0:T(8,128)(2,1)S(1)} %collective-permute-done.2.refs_0_, f32[512,640]{1,0:T(8,128)S(1)} %get-tuple-element.37.refs_1_), custom_call_target="tpu_custom_call" | custom-call | flops 503316480 | bytes 4194304 | tf_op jit(solution)/shard_map/pallas_call | solution.py:107
  44.7 0.0 collective-permute-done.1.refs_0_
  44.7 1.9 %shard_map.88 = (f32[512,640]{1,0:T(8,128)S(1)}, f32[256,640]{1,0:T(8,128)S(1)}, f32[8,256]{1,0:T(8,128)S(1)}) custom-call(f32[2]{0:T(128)S(1)} %pad_maximum_fusion.scal_ref, bf16[512,640]{1,0:T(8,128)(2,1)S(1)} %get-tuple-element.35.zib_ref, bf16[256,640]{1,0:T(8,128)(2,1)S(1)} %collective-permute-done.1.refs_0_, f32[512,640]{1,0:T(8,128)S(1)} %get-tuple-element.38.refs_1_), custom_call_target="tpu_custom_call" | custom-call | flops 503316480 | bytes 4194304 | tf_op jit(solution)/shard_map/pallas_call | solution.py:107
  46.7 2.8 %collective-permute-start.5 = (f32[512,640]{1,0:T(8,128)S(1)}, f32[512,640]{1,0:T(8,128)S(1)}, u32[]{:S(2)}, u32[]{:S(2)}) collective-permute-start(f32[512,640]{1,0:T(8,128)S(1)} %get-tuple-element.39.dzi_ref), channel_id=1, source_target_pairs={{0,1},{1,0},{2,3},{3,2},{4,5},{5,4},{6,7},{7,6},{8,9},{9,8},{10,11... | collective-permute-start | bytes 3932168 | tf_op jit(solution)/shard_map/ppermute | solution.py:260
  49.5 2.6 %collective-permute-done.5.sent_ref = f32[512,640]{1,0:T(8,128)S(1)} collective-permute-done((f32[512,640]{1,0:T(8,128)S(1)}, f32[512,640]{1,0:T(8,128)S(1)}, u32[]{:S(2)}, u32[]{:S(2)}) %collective-permute-start.5) | collective-permute-done | bytes 1310752 | tf_op jit(solution)/shard_map/ppermute | solution.py:260
  52.1 1.4 %shard_map.89 = (bf16[256,640]{1,0:T(8,128)(2,1)S(1)}, bf16[3072,128]{1,0:T(8,128)(2,1)S(1)}) custom-call(f32[512,640]{1,0:T(8,128)S(1)} %get-tuple-element.39.dzi_ref, f32[512,640]{1,0:T(8,128)S(1)} %collective-permute-done.5.sent_ref, f32[512,640]{1,0:T(8,128)S(1)} %get-tuple-element.40.zi_ref, f32[512,128]{1,0:T(8,128)S(1)} %get-tuple-element.41.inv_ref, ...), custom_call_target="tpu_custom_call" | custom-call | flops 377487360 | bytes 7340032 | tf_op jit(solution)/shard_map/pallas_call | solution.py:262
  53.6 14.4 %all_to_all.20 = bf16[4,768,128]{2,1,0:T(8,128)(2,1)S(1)} all-to-all(bf16[4,768,128]{2,1,0:T(8,128)(2,1)S(1)} %bitcast.15), channel_id=1, replica_groups=mesh['y'=8,'x'=4,'z'=8,'core'=2] {'x'}, dimensions={0} | all-to-all | bytes 1572864 | tf_op jit(solution)/shard_map/all_to_all | solution.py:278
  68.0 0.8 shard_map.90
  68.8 6.3 %all-to-all-start.1 = ((bf16[64,6,2,128]{3,2,1,0:T(2,128)(2,1)}), bf16[64,6,2,128]{3,2,1,0:T(2,128)(2,1)S(1)}, u32[]{:S(2)}, u32[]{:S(2)}) async-start(bf16[64,6,2,128]{3,2,1,0:T(2,128)(2,1)} %bitcast.4), calls=%async_computation.1 | async-start | bytes 393216 | tf_op jit(solution)/shard_map/all_to_all | solution.py:285
  75.1 7.2 %collective-permute-start.6 = (bf16[256,640]{1,0:T(8,128)(2,1)S(1)}, bf16[256,640]{1,0:T(8,128)(2,1)S(1)}, u32[]{:S(2)}, u32[]{:S(2)}) collective-permute-start(bf16[256,640]{1,0:T(8,128)(2,1)S(1)} %get-tuple-element.54), channel_id=1, source_target_pairs={{510,0},{3,1},{0,2},{5,3},{2,4},{7,5},{4,6},{9,7},{6,8},{11,9},{8,... | collective-permute-start | bytes 983048 | tf_op jit(solution)/shard_map/ppermute | solution.py:283
  82.3 3.1 %collective-permute-start.7 = (bf16[256,640]{1,0:T(8,128)(2,1)S(1)}, bf16[256,640]{1,0:T(8,128)(2,1)S(1)}, u32[]{:S(2)}, u32[]{:S(2)}) collective-permute-start(bf16[256,640]{1,0:T(8,128)(2,1)S(1)} %get-tuple-element.55), channel_id=1, source_target_pairs={{510,0},{3,1},{0,2},{5,3},{2,4},{7,5},{4,6},{9,7},{6,8},{11,9},{8,... | collective-permute-start | bytes 983048 | tf_op jit(solution)/shard_map/ppermute | solution.py:284
  85.4 1.6 %all-to-all-done.1 = bf16[64,6,2,128]{3,2,1,0:T(2,128)(2,1)S(1)} async-done(((bf16[64,6,2,128]{3,2,1,0:T(2,128)(2,1)}), bf16[64,6,2,128]{3,2,1,0:T(2,128)(2,1)S(1)}, u32[]{:S(2)}, u32[]{:S(2)}) %all-to-all-start.1) | async-done | bytes 196640 | tf_op jit(solution)/shard_map/all_to_all | solution.py:285
  87.0 0.9 shard_map.91
  87.9 4.7 %all-to-all-start.2 = ((bf16[64,6,2,128]{3,2,1,0:T(2,128)(2,1)}), bf16[64,6,2,128]{3,2,1,0:T(2,128)(2,1)S(1)}, u32[]{:S(2)}, u32[]{:S(2)}) async-start(bf16[64,6,2,128]{3,2,1,0:T(2,128)(2,1)} %bitcast.6), calls=%async_computation.2 | async-start | bytes 393216 | tf_op jit(solution)/shard_map/all_to_all | solution.py:307
  92.5 0.0 collective-permute-done.6.far_same_ref
  92.6 0.0 collective-permute-done.7.far_other_ref
  92.6 0.1 shard_map.92
  92.7 0.0 copy-start.5
  92.7 7.3 %collective-permute-start.8 = (bf16[256,640]{1,0:T(8,128)(2,1)S(1)}, bf16[256,640]{1,0:T(8,128)(2,1)S(1)}, u32[]{:S(2)}, u32[]{:S(2)}) collective-permute-start(bf16[256,640]{1,0:T(8,128)(2,1)S(1)} %get-tuple-element.58), channel_id=1, source_target_pairs={{510,0},{3,1},{0,2},{5,3},{2,4},{7,5},{4,6},{9,7},{6,8},{11,9},{8,... | collective-permute-start | bytes 983048 | tf_op jit(solution)/shard_map/ppermute | solution.py:305
  100.0 7.2 %collective-permute-start.9 = (bf16[256,640]{1,0:T(8,128)(2,1)S(1)}, bf16[256,640]{1,0:T(8,128)(2,1)S(1)}, u32[]{:S(2)}, u32[]{:S(2)}) collective-permute-start(bf16[256,640]{1,0:T(8,128)(2,1)S(1)} %get-tuple-element.59), channel_id=1, source_target_pairs={{510,1},{3,0},{0,3},{5,2},{2,5},{7,4},{4,7},{9,6},{6,9},{11,8},{8,... | collective-permute-start | bytes 983048 | tf_op jit(solution)/shard_map/ppermute | solution.py:306
  107.2 0.0 all-to-all-done.2
  107.2 1.0 broadcast_in_dim.3
  108.2 3.5 %all-to-all-start.3 = ((bf16[4,768,128]{2,1,0:T(8,128)(2,1)}), bf16[4,768,128]{2,1,0:T(8,128)(2,1)S(1)}, u32[]{:S(2)}, u32[]{:S(2)}) async-start(bf16[4,768,128]{2,1,0:T(8,128)(2,1)} %broadcast_in_dim.3), calls=%async_computation.3 | async-start | bytes 1572864 | tf_op jit(solution)/shard_map/all_to_all | solution.py:316
  111.7 0.0 collective-permute-done.8.same_ref
  111.7 0.0 copy-done.5
  111.7 0.1 shard_map.93.joined_ref
  111.8 0.0 copy-start.1
  111.8 2.0 %collective-permute-done.9.other_ref = bf16[256,640]{1,0:T(8,128)(2,1)S(1)} collective-permute-done((bf16[256,640]{1,0:T(8,128)(2,1)S(1)}, bf16[256,640]{1,0:T(8,128)(2,1)S(1)}, u32[]{:S(2)}, u32[]{:S(2)}) %collective-permute-start.9) | collective-permute-done | bytes 327712 | tf_op jit(solution)/shard_map/ppermute | solution.py:306
  113.9 1.0 shard_map.94
  114.8 0.0 copy-done.1
  114.8 1.5 %convolution_convert_fusion = bf16[256,1152]{1,0:T(8,128)(2,1)} fusion(bf16[256,640]{1,0:T(8,128)(2,1)S(1)} %get-tuple-element.60, bf16[1152,640]{1,0:T(8,128)(2,1)S(1)} %copy-done.1), kind=kOutput, calls=%fused_computation | convolution fusion | flops 377782272 | bytes 2392064 | tf_op jit(solution)/shard_map/dot_general | solution.py:315
  116.3 5.5 %all-to-all-done.3 = bf16[4,768,128]{2,1,0:T(8,128)(2,1)S(1)} async-done(((bf16[4,768,128]{2,1,0:T(8,128)(2,1)}), bf16[4,768,128]{2,1,0:T(8,128)(2,1)S(1)}, u32[]{:S(2)}, u32[]{:S(2)}) %all-to-all-start.3) | async-done | bytes 786464 | tf_op jit(solution)/shard_map/all_to_all | solution.py:316
  121.8 5.0 %collective-permute-start.10 = (bf16[3072,128]{1,0:T(8,128)(2,1)S(1)}, bf16[3072,128]{1,0:T(8,128)(2,1)S(1)}, u32[]{:S(2)}, u32[]{:S(2)}) collective-permute-start(bf16[3072,128]{1,0:T(8,128)(2,1)S(1)} %bitcast.12), channel_id=1, source_target_pairs={{0,1},{1,0},{2,3},{3,2},{4,5},{5,4},{6,7},{7,6},{8,9},{9,8},{10,11... | collective-permute-start | bytes 2359304 | tf_op jit(solution)/shard_map/ppermute | solution.py:318
  126.8 1.9 %collective-permute-done.10.other_ref = bf16[3072,128]{1,0:T(8,128)(2,1)S(1)} collective-permute-done((bf16[3072,128]{1,0:T(8,128)(2,1)S(1)}, bf16[3072,128]{1,0:T(8,128)(2,1)S(1)}, u32[]{:S(2)}, u32[]{:S(2)}) %collective-permute-start.10) | collective-permute-done | bytes 786464 | tf_op jit(solution)/shard_map/ppermute | solution.py:318
  128.7 1.4 %shard_map.95 = (bf16[1152,640]{1,0:T(8,128)(2,1)}, f32[1,1]{1,0:T(1,128)}) custom-call(s32[1]{0:T(128)} %bitcast.core_ref, bf16[3072,128]{1,0:T(8,128)(2,1)S(1)} %bitcast.13, bf16[3072,128]{1,0:T(8,128)(2,1)S(1)} %collective-permute-done.10.other_ref), custom_call_target="tpu_custom_call" | custom-call | flops 1 | bytes 3145728 | tf_op jit(solution)/shard_map/pallas_call | solution.py:320
Async XLA Ops:
  0.6 29.3 %collective-permute-start = (bf16[256,1152]{1,0:T(8,128)(2,1)}, bf16[256,1152]{1,0:T(8,128)(2,1)S(1)}, u32[]{:S(2)}, u32[]{:S(2)}) collective-permute-start(bf16[256,1152]{1,0:T(8,128)(2,1)} %own_ref.1), channel_id=1, source_target_pairs={{0,1},{1,0},{2,3},{3,2},{4,5},{5,4},{6,7},{7,6},{8,9},{9,8},{10,11... | collective-permute-start | bytes 1769480 | tf_op jit(solution)/shard_map/ppermute | solution.py:233
  9.4 27.1 %collective-permute-start.4 = (bf16[256,640]{1,0:T(8,128)(2,1)}, bf16[256,640]{1,0:T(8,128)(2,1)S(1)}, u32[]{:S(2)}, u32[]{:S(2)}) collective-permute-start(bf16[256,640]{1,0:T(8,128)(2,1)} %text_ref.1), channel_id=1, source_target_pairs={{0,5},{1,508},{2,7},{3,510},{4,9},{5,0},{6,11},{7,2},{8,13},{9,4},... | collective-permute-start | bytes 983048 | tf_op jit(solution)/shard_map/ppermute | solution.py:236
  19.7 18.4 %collective-permute-start.3 = (bf16[256,640]{1,0:T(8,128)(2,1)}, bf16[256,640]{1,0:T(8,128)(2,1)S(1)}, u32[]{:S(2)}, u32[]{:S(2)}) collective-permute-start(bf16[256,640]{1,0:T(8,128)(2,1)} %text_ref.1), channel_id=1, source_target_pairs={{0,508},{1,5},{2,510},{3,7},{4,0},{5,9},{6,2},{7,11},{8,4},{9,13},... | collective-permute-start | bytes 983048 | tf_op jit(solution)/shard_map/ppermute | solution.py:235
  21.6 21.1 %collective-permute-start.2 = (bf16[256,640]{1,0:T(8,128)(2,1)}, bf16[256,640]{1,0:T(8,128)(2,1)S(1)}, u32[]{:S(2)}, u32[]{:S(2)}) collective-permute-start(bf16[256,640]{1,0:T(8,128)(2,1)} %text_ref.1), channel_id=1, source_target_pairs={{0,3},{1,510},{2,5},{3,0},{4,7},{5,2},{6,9},{7,4},{8,11},{9,6},{10... | collective-permute-start | bytes 983048 | tf_op jit(solution)/shard_map/ppermute | solution.py:234
  26.6 18.1 %collective-permute-start.1 = (bf16[256,640]{1,0:T(8,128)(2,1)}, bf16[256,640]{1,0:T(8,128)(2,1)S(1)}, u32[]{:S(2)}, u32[]{:S(2)}) collective-permute-start(bf16[256,640]{1,0:T(8,128)(2,1)} %text_ref.1), channel_id=1, source_target_pairs={{0,510},{1,3},{2,0},{3,5},{4,2},{5,7},{6,4},{7,9},{8,6},{9,11},{10... | collective-permute-start | bytes 983048 | tf_op jit(solution)/shard_map/ppermute | solution.py:232
  29.9 1.4 %copy-start = (bf16[1152,640]{1,0:T(8,128)(2,1)S(1)}, bf16[1152,640]{1,0:T(8,128)(2,1)}, u32[]{:S(2)}) copy-start(bf16[1152,640]{1,0:T(8,128)(2,1)} %weight_ref.1) | copy-start | bytes 4423684
  31.3 1.1 copy-start.3
  32.3 1.4 %copy-start.2 = (bf16[256,640]{1,0:T(8,128)(2,1)S(1)}, bf16[256,640]{1,0:T(8,128)(2,1)}, u32[]{:S(2)}) copy-start(bf16[256,640]{1,0:T(8,128)(2,1)} %text_ref.1) | copy-start | bytes 983044
  35.7 0.8 copy-start.4
  46.7 5.5 %collective-permute-start.5 = (f32[512,640]{1,0:T(8,128)S(1)}, f32[512,640]{1,0:T(8,128)S(1)}, u32[]{:S(2)}, u32[]{:S(2)}) collective-permute-start(f32[512,640]{1,0:T(8,128)S(1)} %get-tuple-element.39.dzi_ref), channel_id=1, source_target_pairs={{0,1},{1,0},{2,3},{3,2},{4,5},{5,4},{6,7},{7,6},{8,9},{9,8},{10,11... | collective-permute-start | bytes 3932168 | tf_op jit(solution)/shard_map/ppermute | solution.py:260
  68.8 18.2 %all-to-all-start.1 = ((bf16[64,6,2,128]{3,2,1,0:T(2,128)(2,1)}), bf16[64,6,2,128]{3,2,1,0:T(2,128)(2,1)S(1)}, u32[]{:S(2)}, u32[]{:S(2)}) async-start(bf16[64,6,2,128]{3,2,1,0:T(2,128)(2,1)} %bitcast.4), calls=%async_computation.1 | async-start | bytes 393216 | tf_op jit(solution)/shard_map/all_to_all | solution.py:285
  75.1 17.4 %collective-permute-start.6 = (bf16[256,640]{1,0:T(8,128)(2,1)S(1)}, bf16[256,640]{1,0:T(8,128)(2,1)S(1)}, u32[]{:S(2)}, u32[]{:S(2)}) collective-permute-start(bf16[256,640]{1,0:T(8,128)(2,1)S(1)} %get-tuple-element.54), channel_id=1, source_target_pairs={{510,0},{3,1},{0,2},{5,3},{2,4},{7,5},{4,6},{9,7},{6,8},{11,9},{8,... | collective-permute-start | bytes 983048 | tf_op jit(solution)/shard_map/ppermute | solution.py:283
  82.3 10.3 %collective-permute-start.7 = (bf16[256,640]{1,0:T(8,128)(2,1)S(1)}, bf16[256,640]{1,0:T(8,128)(2,1)S(1)}, u32[]{:S(2)}, u32[]{:S(2)}) collective-permute-start(bf16[256,640]{1,0:T(8,128)(2,1)S(1)} %get-tuple-element.55), channel_id=1, source_target_pairs={{510,0},{3,1},{0,2},{5,3},{2,4},{7,5},{4,6},{9,7},{6,8},{11,9},{8,... | collective-permute-start | bytes 983048 | tf_op jit(solution)/shard_map/ppermute | solution.py:284
  87.9 19.4 %all-to-all-start.2 = ((bf16[64,6,2,128]{3,2,1,0:T(2,128)(2,1)}), bf16[64,6,2,128]{3,2,1,0:T(2,128)(2,1)S(1)}, u32[]{:S(2)}, u32[]{:S(2)}) async-start(bf16[64,6,2,128]{3,2,1,0:T(2,128)(2,1)} %bitcast.6), calls=%async_computation.2 | async-start | bytes 393216 | tf_op jit(solution)/shard_map/all_to_all | solution.py:307
  92.7 19.1 %copy-start.5 = (f32[256,640]{1,0:T(8,128)S(1)}, f32[256,640]{1,0:T(8,128)}, u32[]{:S(2)}) copy-start(f32[256,640]{1,0:T(8,128)} %copy-done.4) | copy-start | bytes 1966084
  92.7 19.0 %collective-permute-start.8 = (bf16[256,640]{1,0:T(8,128)(2,1)S(1)}, bf16[256,640]{1,0:T(8,128)(2,1)S(1)}, u32[]{:S(2)}, u32[]{:S(2)}) collective-permute-start(bf16[256,640]{1,0:T(8,128)(2,1)S(1)} %get-tuple-element.58), channel_id=1, source_target_pairs={{510,0},{3,1},{0,2},{5,3},{2,4},{7,5},{4,6},{9,7},{6,8},{11,9},{8,... | collective-permute-start | bytes 983048 | tf_op jit(solution)/shard_map/ppermute | solution.py:305
  100.0 13.9 %collective-permute-start.9 = (bf16[256,640]{1,0:T(8,128)(2,1)S(1)}, bf16[256,640]{1,0:T(8,128)(2,1)S(1)}, u32[]{:S(2)}, u32[]{:S(2)}) collective-permute-start(bf16[256,640]{1,0:T(8,128)(2,1)S(1)} %get-tuple-element.59), channel_id=1, source_target_pairs={{510,1},{3,0},{0,3},{5,2},{2,5},{7,4},{4,7},{9,6},{6,9},{11,8},{8,... | collective-permute-start | bytes 983048 | tf_op jit(solution)/shard_map/ppermute | solution.py:306
  108.2 13.6 %all-to-all-start.3 = ((bf16[4,768,128]{2,1,0:T(8,128)(2,1)}), bf16[4,768,128]{2,1,0:T(8,128)(2,1)S(1)}, u32[]{:S(2)}, u32[]{:S(2)}) async-start(bf16[4,768,128]{2,1,0:T(8,128)(2,1)} %broadcast_in_dim.3), calls=%async_computation.3 | async-start | bytes 1572864 | tf_op jit(solution)/shard_map/all_to_all | solution.py:316
  111.8 3.0 %copy-start.1 = (bf16[1152,640]{1,0:T(8,128)(2,1)S(1)}, bf16[1152,640]{1,0:T(8,128)(2,1)}, u32[]{:S(2)}) copy-start(bf16[1152,640]{1,0:T(8,128)(2,1)} %weight_ref.1) | copy-start | bytes 4423684
  121.8 6.9 %collective-permute-start.10 = (bf16[3072,128]{1,0:T(8,128)(2,1)S(1)}, bf16[3072,128]{1,0:T(8,128)(2,1)S(1)}, u32[]{:S(2)}, u32[]{:S(2)}) collective-permute-start(bf16[3072,128]{1,0:T(8,128)(2,1)S(1)} %bitcast.12), channel_id=1, source_target_pairs={{0,1},{1,0},{2,3},{3,2},{4,5},{5,4},{6,7},{7,6},{8,9},{9,8},{10,11... | collective-permute-start | bytes 2359304 | tf_op jit(solution)/shard_map/ppermute | solution.py:318

commit v10 on v8

--- a/solution.py
+++ b/solution.py
@@ -51,11 +51,13 @@
     xt_ref[...] = all_ref[pl.ds(pl.multiple_of(core_ref[0] * HALF, HALF), HALF), :]
 
 
-def score_kernel(parts, has_dzi, scal_ref, zib_ref, *refs):
+def score_kernel(parts, has_dzi, last, scal_ref, zib_ref, *refs):
     text_refs, refs = refs[: len(parts)], refs[len(parts) :]
     dzi_in = None
     if has_dzi:
         dzi_in, *refs = refs
+    if last:
+        sent_ref, *refs = refs
     dzi_ref, dzt_refs, (loss_ref, s_ref, c_ref) = refs[0], refs[1:-3], refs[-3:]
     scale = scal_ref[0]
     bias = scal_ref[1]
@@ -100,20 +102,23 @@
         dzt = scale * lax.dot_general(coef, zib, (((0,), (0,)), ((), ())), preferred_element_type=F32)
         dzt_refs[q][...] = dzt.astype(dzt_refs[q].dtype)
     loss_ref[...] = loss
-
-
-def score(parts, scal, zib, texts, dzi, dzt_dtype):
+    if last:
+        sent_ref[...] = dzi_ref[...].astype(BF)
+
+
+def score(parts, scal, zib, texts, dzi, dzt_dtype, last=False):
     args = (scal, zib, *texts) + (() if dzi is None else (dzi,))
     return call(
-        functools.partial(score_kernel, parts, dzi is not None),
+        functools.partial(score_kernel, parts, dzi is not None, last),
         (
+            *([jax.ShapeDtypeStruct((2 * ROWS, E), BF)] if last else []),
             jax.ShapeDtypeStruct((2 * ROWS, E), F32),
             *(jax.ShapeDtypeStruct((ROWS, E), dzt_dtype) for _ in parts),
             jax.ShapeDtypeStruct((8, ROWS), F32),
         ),
         1,
         len(args) - 1,
-        (VMEM,) * (len(parts) + 2),
+        (VMEM,) * (len(parts) + 2 + last),
         scratch=(pltpu.VMEM((2 * ROWS, ROWS), F32), pltpu.VMEM((2 * ROWS, ROWS), BF)),
         flops=sum(6 * (hi - lo) * ROWS * E for lo, hi, _ in parts),
         bytes_accessed=4 << 20,
@@ -125,7 +130,7 @@
     for part in range(2):
         rows = pl.ds(part * ROWS, ROWS)
         swapped = pl.ds((1 - part) * ROWS, ROWS)
-        dzi = dzi_ref[rows, :] + sent_ref[swapped, :]
+        dzi = dzi_ref[rows, :] + sent_ref[swapped, :].astype(F32)
         zi = zi_ref[rows, :]
         along = jnp.sum(zi * dzi, axis=1, keepdims=True)
         du = ((dzi - zi * along) * inv_ref[rows, 0:1]).astype(BF)
@@ -257,8 +262,8 @@
     dzi, far_other, loss2 = score([(ROWS, both, False)], scal, zib, [far_other], dzi, BF)
     dzi, far_same, loss1 = score([whole], scal, zib, [far_same], dzi, BF)
     dzi, near_other, loss4 = score([whole], scal, zib, [near_other], dzi, F32)
-    dzi, near_same, loss3 = score([whole], scal, zib, [near_same], dzi, F32)
-    dzi_sent = lax.ppermute(dzi, axes, across)
+    rounded, dzi, near_same, loss3 = score([whole], scal, zib, [near_same], dzi, F32, last=True)
+    dzi_sent = lax.ppermute(rounded, axes, across)
 
     du, flat = call(
         head_kernel,

time: 132 us -> 131 us (level)
  no operation moved by 1% of the time
where the time goes in v10:
time: 131 us; the launch traced here: 130 us
  starting transfers between devices  74.5 us (57%)
  Pallas kernels  16.3 us (12%)
  waiting for transfers between devices  16.2 us (12%)
  blocking collectives  14.4 us (11%)
  between operations  4.02 us (3%)
  local copies, waits for them, and re-layouts  3.44 us (3%)
  matrix products  1.49 us (1%)
    all_to_all x1, blocking collectives, per_device(): along_x = lax.all_to_all(flat.reshape(nx, part, LANES), 'x', 0, 0)  14.4 us
    ppermute x1, starting transfers between devices, per_device(): far_other = lax.ppermute(text_embeds, axes, crossing(2))  10.3 us
    pallas_call x5, Pallas kernels, score(): call(functools.partial(score_kernel, parts, dzi is not None, last), (*([j...  9.28 us
    ppermute x1, starting transfers between devices, per_device(): x_other = lax.ppermute(image_feats, axes, across)  8.79 us
    ppermute x1, starting transfers between devices, per_device(): home_same = lax.ppermute(same, axes, back)  7.29 us
    ppermute x1, starting transfers between devices, per_device(): far_same = lax.ppermute(far_same, axes, back)  7.16 us
    ppermute x1, starting transfers between devices, per_device(): home_other = lax.ppermute(other, axes, [(s, d ^ 1) for s, d in back])  7.01 us
    all_to_all x1, starting transfers between devices, per_device(): lax.all_to_all(summed.reshape(ny * nz, share // 2, 2, LANES), ('y', 'z'),...  5.87 us
  transfers between devices with their start and end apart: 14, of which 7 were waited for; matrix products, arithmetic and copies ran while one was open for 2% of the time, Pallas kernels for 8%

profile of v10, /device:TPU:1, one launch (start us, length us, event | category | flops | bytes accessed | tf_op | source)
XLA Modules:
  0.0 130.4 jit_solution(9209659119061343201)
XLA Ops:
  0.6 8.8 %collective-permute-start = (bf16[256,1152]{1,0:T(8,128)(2,1)}, bf16[256,1152]{1,0:T(8,128)(2,1)S(1)}, u32[]{:S(2)}, u32[]{:S(2)}) collective-permute-start(bf16[256,1152]{1,0:T(8,128)(2,1)} %own_ref.1), channel_id=1, source_target_pairs={{0,1},{1,0},{2,3},{3,2},{4,5},{5,4},{6,7},{7,6},{8,9},{9,8},{10,11... | collective-permute-start | bytes 1769480 | tf_op jit(solution)/shard_map/ppermute | solution.py:238
  9.4 10.3 %collective-permute-start.4 = (bf16[256,640]{1,0:T(8,128)(2,1)}, bf16[256,640]{1,0:T(8,128)(2,1)S(1)}, u32[]{:S(2)}, u32[]{:S(2)}) collective-permute-start(bf16[256,640]{1,0:T(8,128)(2,1)} %text_ref.1), channel_id=1, source_target_pairs={{0,5},{1,508},{2,7},{3,510},{4,9},{5,0},{6,11},{7,2},{8,13},{9,4},... | collective-permute-start | bytes 983048 | tf_op jit(solution)/shard_map/ppermute | solution.py:241
  19.7 1.9 %collective-permute-start.3 = (bf16[256,640]{1,0:T(8,128)(2,1)}, bf16[256,640]{1,0:T(8,128)(2,1)S(1)}, u32[]{:S(2)}, u32[]{:S(2)}) collective-permute-start(bf16[256,640]{1,0:T(8,128)(2,1)} %text_ref.1), channel_id=1, source_target_pairs={{0,508},{1,5},{2,510},{3,7},{4,0},{5,9},{6,2},{7,11},{8,4},{9,13},... | collective-permute-start | bytes 983048 | tf_op jit(solution)/shard_map/ppermute | solution.py:240
  21.6 4.9 %collective-permute-start.2 = (bf16[256,640]{1,0:T(8,128)(2,1)}, bf16[256,640]{1,0:T(8,128)(2,1)S(1)}, u32[]{:S(2)}, u32[]{:S(2)}) collective-permute-start(bf16[256,640]{1,0:T(8,128)(2,1)} %text_ref.1), channel_id=1, source_target_pairs={{0,3},{1,510},{2,5},{3,0},{4,7},{5,2},{6,9},{7,4},{8,11},{9,6},{10... | collective-permute-start | bytes 983048 | tf_op jit(solution)/shard_map/ppermute | solution.py:239
  26.6 1.9 %collective-permute-start.1 = (bf16[256,640]{1,0:T(8,128)(2,1)}, bf16[256,640]{1,0:T(8,128)(2,1)S(1)}, u32[]{:S(2)}, u32[]{:S(2)}) collective-permute-start(bf16[256,640]{1,0:T(8,128)(2,1)} %text_ref.1), channel_id=1, source_target_pairs={{0,510},{1,3},{2,0},{3,5},{4,2},{5,7},{6,4},{7,9},{8,6},{9,11},{10... | collective-permute-start | bytes 983048 | tf_op jit(solution)/shard_map/ppermute | solution.py:237
  29.8 0.1 pad_maximum_fusion.scal_ref
  29.9 0.0 collective-permute-done.other_ref
  29.9 0.0 copy-start
  29.9 1.4 %copy-done = bf16[1152,640]{1,0:T(8,128)(2,1)S(1)} copy-done((bf16[1152,640]{1,0:T(8,128)(2,1)S(1)}, bf16[1152,640]{1,0:T(8,128)(2,1)}, u32[]{:S(2)}) %copy-start) | copy-done | bytes 1474584
  31.3 0.0 copy-start.3
  31.3 1.1 copy-done.3
  32.3 0.0 copy-start.2
  32.3 1.4 %shard_map.84 = (f32[512,640]{1,0:T(8,128)S(1)}, bf16[512,640]{1,0:T(8,128)(2,1)S(1)}, f32[512,128]{1,0:T(8,128)S(1)}, bf16[576,512]{1,0:T(8,128)(2,1)S(1)}) custom-call(s32[1]{0:T(128)} %bitcast.core_ref, bf16[256,1152]{1,0:T(8,128)(2,1)S(1)} %copy-done.3, bf16[256,1152]{1,0:T(8,128)(2,1)S(1)} %collective-permute-done.other_ref, bf16[1152,640]{1,0:T(8,128)(2,1)S(1)} %copy-done), custom_call_target="tpu_custom_call" | custom-call | flops 754974720 | bytes 5242880 | tf_op jit(solution)/shard_map/pallas_call | solution.py:243
  33.7 0.0 copy-done.2
  33.7 2.0 %shard_map.85 = (f32[512,640]{1,0:T(8,128)S(1)}, f32[256,640]{1,0:T(8,128)S(1)}, f32[8,256]{1,0:T(8,128)S(1)}) custom-call(f32[2]{0:T(128)S(1)} %pad_maximum_fusion.scal_ref, bf16[512,640]{1,0:T(8,128)(2,1)S(1)} %get-tuple-element.38.zib_ref, bf16[256,640]{1,0:T(8,128)(2,1)S(1)} %copy-done.2), custom_call_target="tpu_custom_call" | custom-call | flops 503316480 | bytes 4194304 | tf_op jit(solution)/shard_map/pallas_call | solution.py:111
  35.7 0.0 copy-start.4
  35.7 0.0 collective-permute-done.4.refs_0_
  35.7 1.5 %shard_map.86 = (f32[512,640]{1,0:T(8,128)S(1)}, bf16[256,640]{1,0:T(8,128)(2,1)S(1)}, f32[8,256]{1,0:T(8,128)S(1)}) custom-call(f32[2]{0:T(128)S(1)} %pad_maximum_fusion.scal_ref, bf16[512,640]{1,0:T(8,128)(2,1)S(1)} %get-tuple-element.38.zib_ref, bf16[256,640]{1,0:T(8,128)(2,1)S(1)} %collective-permute-done.4.refs_0_, f32[512,640]{1,0:T(8,128)S(1)} %get-tuple-element.39.refs_1_), custom_call_target="tpu_custom_call" | custom-call | flops 251658240 | bytes 4194304 | tf_op jit(solution)/shard_map/pallas_call | solution.py:111
  37.2 0.9 collective-permute-done.3.refs_0_
  38.1 2.0 %shard_map.87 = (f32[512,640]{1,0:T(8,128)S(1)}, bf16[256,640]{1,0:T(8,128)(2,1)S(1)}, f32[8,256]{1,0:T(8,128)S(1)}) custom-call(f32[2]{0:T(128)S(1)} %pad_maximum_fusion.scal_ref, bf16[512,640]{1,0:T(8,128)(2,1)S(1)} %get-tuple-element.38.zib_ref, bf16[256,640]{1,0:T(8,128)(2,1)S(1)} %collective-permute-done.3.refs_0_, f32[512,640]{1,0:T(8,128)S(1)} %get-tuple-element.40.refs_1_), custom_call_target="tpu_custom_call" | custom-call | flops 503316480 | bytes 4194304 | tf_op jit(solution)/shard_map/pallas_call | solution.py:111
  40.1 0.0 copy-done.4
  40.1 2.7 %collective-permute-done.2.refs_0_ = bf16[256,640]{1,0:T(8,128)(2,1)S(1)} collective-permute-done((bf16[256,640]{1,0:T(8,128)(2,1)}, bf16[256,640]{1,0:T(8,128)(2,1)S(1)}, u32[]{:S(2)}, u32[]{:S(2)}) %collective-permute-start.2) | collective-permute-done | bytes 327712 | tf_op jit(solution)/shard_map/ppermute | solution.py:239
  42.8 1.9 %shard_map.88 = (f32[512,640]{1,0:T(8,128)S(1)}, f32[256,640]{1,0:T(8,128)S(1)}, f32[8,256]{1,0:T(8,128)S(1)}) custom-call(f32[2]{0:T(128)S(1)} %pad_maximum_fusion.scal_ref, bf16[512,640]{1,0:T(8,128)(2,1)S(1)} %get-tuple-element.38.zib_ref, bf16[256,640]{1,0:T(8,128)(2,1)S(1)} %collective-permute-done.2.refs_0_, f32[512,640]{1,0:T(8,128)S(1)} %get-tuple-element.41.refs_1_), custom_call_target="tpu_custom_call" | custom-call | flops 503316480 | bytes 4194304 | tf_op jit(solution)/shard_map/pallas_call | solution.py:111
  44.7 0.0 collective-permute-done.1.refs_0_
  44.7 2.0 %shard_map.89 = (bf16[512,640]{1,0:T(8,128)(2,1)S(1)}, f32[512,640]{1,0:T(8,128)S(1)}, f32[256,640]{1,0:T(8,128)S(1)}, f32[8,256]{1,0:T(8,128)S(1)}) custom-call(f32[2]{0:T(128)S(1)} %pad_maximum_fusion.scal_ref, bf16[512,640]{1,0:T(8,128)(2,1)S(1)} %get-tuple-element.38.zib_ref, bf16[256,640]{1,0:T(8,128)(2,1)S(1)} %collective-permute-done.1.refs_0_, ...), custom_call_target="tpu_custom_call" | custom-call | flops 503316480 | bytes 4194304 | tf_op jit(solution)/shard_map/pallas_call | solution.py:111
  46.7 2.9 %collective-permute-start.5 = (bf16[512,640]{1,0:T(8,128)(2,1)S(1)}, bf16[512,640]{1,0:T(8,128)(2,1)S(1)}, u32[]{:S(2)}, u32[]{:S(2)}) collective-permute-start(bf16[512,640]{1,0:T(8,128)(2,1)S(1)} %get-tuple-element.44), channel_id=1, source_target_pairs={{0,1},{1,0},{2,3},{3,2},{4,5},{5,4},{6,7},{7,6},{8,9},{9,8},{10,11... | collective-permute-start | bytes 1966088 | tf_op jit(solution)/shard_map/ppermute | solution.py:266
  49.6 1.7 %collective-permute-done.5.sent_ref = bf16[512,640]{1,0:T(8,128)(2,1)S(1)} collective-permute-done((bf16[512,640]{1,0:T(8,128)(2,1)S(1)}, bf16[512,640]{1,0:T(8,128)(2,1)S(1)}, u32[]{:S(2)}, u32[]{:S(2)}) %collective-permute-start.5) | collective-permute-done | bytes 655392 | tf_op jit(solution)/shard_map/ppermute | solution.py:266
  51.3 1.4 %shard_map.90 = (bf16[256,640]{1,0:T(8,128)(2,1)S(1)}, bf16[3072,128]{1,0:T(8,128)(2,1)S(1)}) custom-call(f32[512,640]{1,0:T(8,128)S(1)} %get-tuple-element.43.dzi_ref, bf16[512,640]{1,0:T(8,128)(2,1)S(1)} %collective-permute-done.5.sent_ref, f32[512,640]{1,0:T(8,128)S(1)} %get-tuple-element.45.zi_ref, f32[512,128]{1,0:T(8,128)S(1)} %get-tuple-element.46.inv_ref, ...), custom_call_target="tpu_custom_call" | custom-call | flops 377487360 | bytes 7340032 | tf_op jit(solution)/shard_map/pallas_call | solution.py:268
  52.7 14.4 %all_to_all.20 = bf16[4,768,128]{2,1,0:T(8,128)(2,1)S(1)} all-to-all(bf16[4,768,128]{2,1,0:T(8,128)(2,1)S(1)} %bitcast.15), channel_id=1, replica_groups=mesh['y'=8,'x'=4,'z'=8,'core'=2] {'x'}, dimensions={0} | all-to-all | bytes 1572864 | tf_op jit(solution)/shard_map/all_to_all | solution.py:284
  67.2 0.8 shard_map.91
  67.9 5.9 %all-to-all-start.1 = ((bf16[64,6,2,128]{3,2,1,0:T(2,128)(2,1)}), bf16[64,6,2,128]{3,2,1,0:T(2,128)(2,1)S(1)}, u32[]{:S(2)}, u32[]{:S(2)}) async-start(bf16[64,6,2,128]{3,2,1,0:T(2,128)(2,1)} %bitcast.4), calls=%async_computation.1 | async-start | bytes 393216 | tf_op jit(solution)/shard_map/all_to_all | solution.py:291
  73.8 7.2 %collective-permute-start.6 = (bf16[256,640]{1,0:T(8,128)(2,1)S(1)}, bf16[256,640]{1,0:T(8,128)(2,1)S(1)}, u32[]{:S(2)}, u32[]{:S(2)}) collective-permute-start(bf16[256,640]{1,0:T(8,128)(2,1)S(1)} %get-tuple-element.60), channel_id=1, source_target_pairs={{510,0},{3,1},{0,2},{5,3},{2,4},{7,5},{4,6},{9,7},{6,8},{11,9},{8,... | collective-permute-start | bytes 983048 | tf_op jit(solution)/shard_map/ppermute | solution.py:289
  81.0 3.1 %collective-permute-start.7 = (bf16[256,640]{1,0:T(8,128)(2,1)S(1)}, bf16[256,640]{1,0:T(8,128)(2,1)S(1)}, u32[]{:S(2)}, u32[]{:S(2)}) collective-permute-start(bf16[256,640]{1,0:T(8,128)(2,1)S(1)} %get-tuple-element.61), channel_id=1, source_target_pairs={{510,0},{3,1},{0,2},{5,3},{2,4},{7,5},{4,6},{9,7},{6,8},{11,9},{8,... | collective-permute-start | bytes 983048 | tf_op jit(solution)/shard_map/ppermute | solution.py:290
  84.1 1.6 %all-to-all-done.1 = bf16[64,6,2,128]{3,2,1,0:T(2,128)(2,1)S(1)} async-done(((bf16[64,6,2,128]{3,2,1,0:T(2,128)(2,1)}), bf16[64,6,2,128]{3,2,1,0:T(2,128)(2,1)S(1)}, u32[]{:S(2)}, u32[]{:S(2)}) %all-to-all-start.1) | async-done | bytes 196640 | tf_op jit(solution)/shard_map/all_to_all | solution.py:291
  85.7 0.9 shard_map.92
  86.5 4.7 %all-to-all-start.2 = ((bf16[64,6,2,128]{3,2,1,0:T(2,128)(2,1)}), bf16[64,6,2,128]{3,2,1,0:T(2,128)(2,1)S(1)}, u32[]{:S(2)}, u32[]{:S(2)}) async-start(bf16[64,6,2,128]{3,2,1,0:T(2,128)(2,1)} %bitcast.6), calls=%async_computation.2 | async-start | bytes 393216 | tf_op jit(solution)/shard_map/all_to_all | solution.py:313
  91.2 0.0 collective-permute-done.6.far_same_ref
  91.3 0.0 collective-permute-done.7.far_other_ref
  91.3 0.1 shard_map.93
  91.4 0.0 copy-start.5
  91.4 7.3 %collective-permute-start.8 = (bf16[256,640]{1,0:T(8,128)(2,1)S(1)}, bf16[256,640]{1,0:T(8,128)(2,1)S(1)}, u32[]{:S(2)}, u32[]{:S(2)}) collective-permute-start(bf16[256,640]{1,0:T(8,128)(2,1)S(1)} %get-tuple-element.64), channel_id=1, source_target_pairs={{510,0},{3,1},{0,2},{5,3},{2,4},{7,5},{4,6},{9,7},{6,8},{11,9},{8,... | collective-permute-start | bytes 983048 | tf_op jit(solution)/shard_map/ppermute | solution.py:311
  98.7 7.0 %collective-permute-start.9 = (bf16[256,640]{1,0:T(8,128)(2,1)S(1)}, bf16[256,640]{1,0:T(8,128)(2,1)S(1)}, u32[]{:S(2)}, u32[]{:S(2)}) collective-permute-start(bf16[256,640]{1,0:T(8,128)(2,1)S(1)} %get-tuple-element.65), channel_id=1, source_target_pairs={{510,1},{3,0},{0,3},{5,2},{2,5},{7,4},{4,7},{9,6},{6,9},{11,8},{8,... | collective-permute-start | bytes 983048 | tf_op jit(solution)/shard_map/ppermute | solution.py:312
  105.7 0.0 all-to-all-done.2
  105.7 1.0 broadcast_in_dim.3
  106.7 3.5 %all-to-all-start.3 = ((bf16[4,768,128]{2,1,0:T(8,128)(2,1)}), bf16[4,768,128]{2,1,0:T(8,128)(2,1)S(1)}, u32[]{:S(2)}, u32[]{:S(2)}) async-start(bf16[4,768,128]{2,1,0:T(8,128)(2,1)} %broadcast_in_dim.3), calls=%async_computation.3 | async-start | bytes 1572864 | tf_op jit(solution)/shard_map/all_to_all | solution.py:322
  110.2 0.0 collective-permute-done.8.same_ref
  110.2 0.0 copy-done.5
  110.2 0.1 shard_map.94.joined_ref
  110.3 0.0 copy-start.1
  110.3 2.2 %collective-permute-done.9.other_ref = bf16[256,640]{1,0:T(8,128)(2,1)S(1)} collective-permute-done((bf16[256,640]{1,0:T(8,128)(2,1)S(1)}, bf16[256,640]{1,0:T(8,128)(2,1)S(1)}, u32[]{:S(2)}, u32[]{:S(2)}) %collective-permute-start.9) | collective-permute-done | bytes 327712 | tf_op jit(solution)/shard_map/ppermute | solution.py:312
  112.5 1.0 shard_map.95
  113.5 0.0 copy-done.1
  113.5 1.5 %convolution_convert_fusion = bf16[256,1152]{1,0:T(8,128)(2,1)} fusion(bf16[256,640]{1,0:T(8,128)(2,1)S(1)} %get-tuple-element.66, bf16[1152,640]{1,0:T(8,128)(2,1)S(1)} %copy-done.1), kind=kOutput, calls=%fused_computation | convolution fusion | flops 377782272 | bytes 2392064 | tf_op jit(solution)/shard_map/dot_general | solution.py:321
  115.0 5.2 %all-to-all-done.3 = bf16[4,768,128]{2,1,0:T(8,128)(2,1)S(1)} async-done(((bf16[4,768,128]{2,1,0:T(8,128)(2,1)}), bf16[4,768,128]{2,1,0:T(8,128)(2,1)S(1)}, u32[]{:S(2)}, u32[]{:S(2)}) %all-to-all-start.3) | async-done | bytes 786464 | tf_op jit(solution)/shard_map/all_to_all | solution.py:322
  120.2 5.2 %collective-permute-start.10 = (bf16[3072,128]{1,0:T(8,128)(2,1)S(1)}, bf16[3072,128]{1,0:T(8,128)(2,1)S(1)}, u32[]{:S(2)}, u32[]{:S(2)}) collective-permute-start(bf16[3072,128]{1,0:T(8,128)(2,1)S(1)} %bitcast.12), channel_id=1, source_target_pairs={{0,1},{1,0},{2,3},{3,2},{4,5},{5,4},{6,7},{7,6},{8,9},{9,8},{10,11... | collective-permute-start | bytes 2359304 | tf_op jit(solution)/shard_map/ppermute | solution.py:324
  125.3 1.9 %collective-permute-done.10.other_ref = bf16[3072,128]{1,0:T(8,128)(2,1)S(1)} collective-permute-done((bf16[3072,128]{1,0:T(8,128)(2,1)S(1)}, bf16[3072,128]{1,0:T(8,128)(2,1)S(1)}, u32[]{:S(2)}, u32[]{:S(2)}) %collective-permute-start.10) | collective-permute-done | bytes 786464 | tf_op jit(solution)/shard_map/ppermute | solution.py:324
  127.2 1.4 %shard_map.96 = (bf16[1152,640]{1,0:T(8,128)(2,1)}, f32[1,1]{1,0:T(1,128)}) custom-call(s32[1]{0:T(128)} %bitcast.core_ref, bf16[3072,128]{1,0:T(8,128)(2,1)S(1)} %bitcast.13, bf16[3072,128]{1,0:T(8,128)(2,1)S(1)} %collective-permute-done.10.other_ref), custom_call_target="tpu_custom_call" | custom-call | flops 1 | bytes 3145728 | tf_op jit(solution)/shard_map/pallas_call | solution.py:326
Async XLA Ops:
  0.6 29.3 %collective-permute-start = (bf16[256,1152]{1,0:T(8,128)(2,1)}, bf16[256,1152]{1,0:T(8,128)(2,1)S(1)}, u32[]{:S(2)}, u32[]{:S(2)}) collective-permute-start(bf16[256,1152]{1,0:T(8,128)(2,1)} %own_ref.1), channel_id=1, source_target_pairs={{0,1},{1,0},{2,3},{3,2},{4,5},{5,4},{6,7},{7,6},{8,9},{9,8},{10,11... | collective-permute-start | bytes 1769480 | tf_op jit(solution)/shard_map/ppermute | solution.py:238
  9.4 26.3 %collective-permute-start.4 = (bf16[256,640]{1,0:T(8,128)(2,1)}, bf16[256,640]{1,0:T(8,128)(2,1)S(1)}, u32[]{:S(2)}, u32[]{:S(2)}) collective-permute-start(bf16[256,640]{1,0:T(8,128)(2,1)} %text_ref.1), channel_id=1, source_target_pairs={{0,5},{1,508},{2,7},{3,510},{4,9},{5,0},{6,11},{7,2},{8,13},{9,4},... | collective-permute-start | bytes 983048 | tf_op jit(solution)/shard_map/ppermute | solution.py:241
  19.7 18.4 %collective-permute-start.3 = (bf16[256,640]{1,0:T(8,128)(2,1)}, bf16[256,640]{1,0:T(8,128)(2,1)S(1)}, u32[]{:S(2)}, u32[]{:S(2)}) collective-permute-start(bf16[256,640]{1,0:T(8,128)(2,1)} %text_ref.1), channel_id=1, source_target_pairs={{0,508},{1,5},{2,510},{3,7},{4,0},{5,9},{6,2},{7,11},{8,4},{9,13},... | collective-permute-start | bytes 983048 | tf_op jit(solution)/shard_map/ppermute | solution.py:240
  21.6 21.1 %collective-permute-start.2 = (bf16[256,640]{1,0:T(8,128)(2,1)}, bf16[256,640]{1,0:T(8,128)(2,1)S(1)}, u32[]{:S(2)}, u32[]{:S(2)}) collective-permute-start(bf16[256,640]{1,0:T(8,128)(2,1)} %text_ref.1), channel_id=1, source_target_pairs={{0,3},{1,510},{2,5},{3,0},{4,7},{5,2},{6,9},{7,4},{8,11},{9,6},{10... | collective-permute-start | bytes 983048 | tf_op jit(solution)/shard_map/ppermute | solution.py:239
  26.6 18.1 %collective-permute-start.1 = (bf16[256,640]{1,0:T(8,128)(2,1)}, bf16[256,640]{1,0:T(8,128)(2,1)S(1)}, u32[]{:S(2)}, u32[]{:S(2)}) collective-permute-start(bf16[256,640]{1,0:T(8,128)(2,1)} %text_ref.1), channel_id=1, source_target_pairs={{0,510},{1,3},{2,0},{3,5},{4,2},{5,7},{6,4},{7,9},{8,6},{9,11},{10... | collective-permute-start | bytes 983048 | tf_op jit(solution)/shard_map/ppermute | solution.py:237
  29.9 1.4 %copy-start = (bf16[1152,640]{1,0:T(8,128)(2,1)S(1)}, bf16[1152,640]{1,0:T(8,128)(2,1)}, u32[]{:S(2)}) copy-start(bf16[1152,640]{1,0:T(8,128)(2,1)} %weight_ref.1) | copy-start | bytes 4423684
  31.3 1.1 copy-start.3
  32.3 1.4 %copy-start.2 = (bf16[256,640]{1,0:T(8,128)(2,1)S(1)}, bf16[256,640]{1,0:T(8,128)(2,1)}, u32[]{:S(2)}) copy-start(bf16[256,640]{1,0:T(8,128)(2,1)} %text_ref.1) | copy-start | bytes 983044
  35.7 4.4 %copy-start.4 = (f32[256,640]{1,0:T(8,128)}, f32[256,640]{1,0:T(8,128)S(1)}, u32[]{:S(2)}) copy-start(f32[256,640]{1,0:T(8,128)S(1)} %get-tuple-element.59.own_ref) | copy-start | bytes 1966084
  46.7 4.6 %collective-permute-start.5 = (bf16[512,640]{1,0:T(8,128)(2,1)S(1)}, bf16[512,640]{1,0:T(8,128)(2,1)S(1)}, u32[]{:S(2)}, u32[]{:S(2)}) collective-permute-start(bf16[512,640]{1,0:T(8,128)(2,1)S(1)} %get-tuple-element.44), channel_id=1, source_target_pairs={{0,1},{1,0},{2,3},{3,2},{4,5},{5,4},{6,7},{7,6},{8,9},{9,8},{10,11... | collective-permute-start | bytes 1966088 | tf_op jit(solution)/shard_map/ppermute | solution.py:266
  67.9 17.7 %all-to-all-start.1 = ((bf16[64,6,2,128]{3,2,1,0:T(2,128)(2,1)}), bf16[64,6,2,128]{3,2,1,0:T(2,128)(2,1)S(1)}, u32[]{:S(2)}, u32[]{:S(2)}) async-start(bf16[64,6,2,128]{3,2,1,0:T(2,128)(2,1)} %bitcast.4), calls=%async_computation.1 | async-start | bytes 393216 | tf_op jit(solution)/shard_map/all_to_all | solution.py:291
  73.8 17.4 %collective-permute-start.6 = (bf16[256,640]{1,0:T(8,128)(2,1)S(1)}, bf16[256,640]{1,0:T(8,128)(2,1)S(1)}, u32[]{:S(2)}, u32[]{:S(2)}) collective-permute-start(bf16[256,640]{1,0:T(8,128)(2,1)S(1)} %get-tuple-element.60), channel_id=1, source_target_pairs={{510,0},{3,1},{0,2},{5,3},{2,4},{7,5},{4,6},{9,7},{6,8},{11,9},{8,... | collective-permute-start | bytes 983048 | tf_op jit(solution)/shard_map/ppermute | solution.py:289
  81.0 10.3 %collective-permute-start.7 = (bf16[256,640]{1,0:T(8,128)(2,1)S(1)}, bf16[256,640]{1,0:T(8,128)(2,1)S(1)}, u32[]{:S(2)}, u32[]{:S(2)}) collective-permute-start(bf16[256,640]{1,0:T(8,128)(2,1)S(1)} %get-tuple-element.61), channel_id=1, source_target_pairs={{510,0},{3,1},{0,2},{5,3},{2,4},{7,5},{4,6},{9,7},{6,8},{11,9},{8,... | collective-permute-start | bytes 983048 | tf_op jit(solution)/shard_map/ppermute | solution.py:290
  86.5 19.2 %all-to-all-start.2 = ((bf16[64,6,2,128]{3,2,1,0:T(2,128)(2,1)}), bf16[64,6,2,128]{3,2,1,0:T(2,128)(2,1)S(1)}, u32[]{:S(2)}, u32[]{:S(2)}) async-start(bf16[64,6,2,128]{3,2,1,0:T(2,128)(2,1)} %bitcast.6), calls=%async_computation.2 | async-start | bytes 393216 | tf_op jit(solution)/shard_map/all_to_all | solution.py:313
  91.4 18.8 %copy-start.5 = (f32[256,640]{1,0:T(8,128)S(1)}, f32[256,640]{1,0:T(8,128)}, u32[]{:S(2)}) copy-start(f32[256,640]{1,0:T(8,128)} %copy-done.4) | copy-start | bytes 1966084
  91.4 18.8 %collective-permute-start.8 = (bf16[256,640]{1,0:T(8,128)(2,1)S(1)}, bf16[256,640]{1,0:T(8,128)(2,1)S(1)}, u32[]{:S(2)}, u32[]{:S(2)}) collective-permute-start(bf16[256,640]{1,0:T(8,128)(2,1)S(1)} %get-tuple-element.64), channel_id=1, source_target_pairs={{510,0},{3,1},{0,2},{5,3},{2,4},{7,5},{4,6},{9,7},{6,8},{11,9},{8,... | collective-permute-start | bytes 983048 | tf_op jit(solution)/shard_map/ppermute | solution.py:311
  98.7 13.8 %collective-permute-start.9 = (bf16[256,640]{1,0:T(8,128)(2,1)S(1)}, bf16[256,640]{1,0:T(8,128)(2,1)S(1)}, u32[]{:S(2)}, u32[]{:S(2)}) collective-permute-start(bf16[256,640]{1,0:T(8,128)(2,1)S(1)} %get-tuple-element.65), channel_id=1, source_target_pairs={{510,1},{3,0},{0,3},{5,2},{2,5},{7,4},{4,7},{9,6},{6,9},{11,8},{8,... | collective-permute-start | bytes 983048 | tf_op jit(solution)/shard_map/ppermute | solution.py:312
  106.7 13.5 %all-to-all-start.3 = ((bf16[4,768,128]{2,1,0:T(8,128)(2,1)}), bf16[4,768,128]{2,1,0:T(8,128)(2,1)S(1)}, u32[]{:S(2)}, u32[]{:S(2)}) async-start(bf16[4,768,128]{2,1,0:T(8,128)(2,1)} %broadcast_in_dim.3), calls=%async_computation.3 | async-start | bytes 1572864 | tf_op jit(solution)/shard_map/all_to_all | solution.py:322
  110.3 3.2 %copy-start.1 = (bf16[1152,640]{1,0:T(8,128)(2,1)S(1)}, bf16[1152,640]{1,0:T(8,128)(2,1)}, u32[]{:S(2)}) copy-start(bf16[1152,640]{1,0:T(8,128)(2,1)} %weight_ref.1) | copy-start | bytes 4423684
  120.2 7.1 %collective-permute-start.10 = (bf16[3072,128]{1,0:T(8,128)(2,1)S(1)}, bf16[3072,128]{1,0:T(8,128)(2,1)S(1)}, u32[]{:S(2)}, u32[]{:S(2)}) collective-permute-start(bf16[3072,128]{1,0:T(8,128)(2,1)S(1)} %bitcast.12), channel_id=1, source_target_pairs={{0,1},{1,0},{2,3},{3,2},{4,5},{5,4},{6,7},{7,6},{8,9},{9,8},{10,11... | collective-permute-start | bytes 2359304 | tf_op jit(solution)/shard_map/ppermute | solution.py:324
